TPU v7x, 32 devices: a whole 2x2x4 slice. The times are simulated.
32 devices in a mesh: seq: 8 (over y, x, core), head: 4 (over z).
Axes of the slice: x: 2, y: 2, z: 4, core: 2. Of those that a mesh axis runs over, the one named last changes fastest.
Arguments:
- spatial_qkv: bfloat16 [3, 16, 1024, 1152], P(None, 'seq', None, 'head'), may hold values from -300 to 300
- stream: bfloat16 [16, 1024, 1152], P('seq', None, 'head'), may hold values from -6 to 6
- out_spatial: bfloat16 [1152, 1152], P('head'), may hold values from -0.1875 to 0.1875
- qkv_temporal: bfloat16 [3, 1152, 1152], P(None, None, 'head'), may hold values from -16 to 16
- out_temporal: bfloat16 [1152, 1152], P('head'), may hold values from -0.1875 to 0.1875
- modulation: float32 [2, 4, 1152], replicated, may hold values from -2 to 2
- tok_count: int32 [2], replicated, may hold values from 128 to 1024, as said below
- frame_count: int32 [2], replicated, may hold values from 2 to 8, as said below
Outputs:
- result: bfloat16 [16, 1024, 1152], P(None, 'seq', 'head')
Inputs may be any that keep to these rules, and one draw needn't show every extreme that they name: `tok_count`: the same count holds for every frame of a clip; some clip has exactly 1024. `frame_count`: some clip has exactly 8.
All inputs are finite; a program needn't handle non-finite values.
Results may differ from a plain program's by a relative error of at most 0.024.
Values may be sent and summed in bfloat16 or wider, within the bound.
No kernel may reach another device: no remote copies, remote signals or barrier semaphores. Data moves between devices by JAX's collectives and lax.ppermute only.
A program may use at most 128 MiB of HBM per device.

v0:
```python
import functools
import math

import jax
import jax.numpy as jnp
from jax import lax
from jax.experimental import pallas as pl
from jax.experimental.pallas import tpu as pltpu
from jax.sharding import Mesh
from jax.sharding import PartitionSpec as P

HEAD_DIM = 72
FRAMES = 8
PAIR = 2 * HEAD_DIM
KINDS = 3
SLICES = 8
EPS = 1e-6
F32 = jnp.float32
BF16 = jnp.bfloat16
MIB = 1024 * 1024


def flip(array):
    return jnp.swapaxes(array, 0, 1)


def tn(lhs, rhs):
    return lax.dot_general(lhs, rhs, (((0,), (0,)), ((), ())), preferred_element_type=F32)


def runs_of(chunk, rank, sizes):
    groups, ranks, heads, block, span, run = sizes
    starts = []
    for piece in range(span // run):
        place = chunk * span + piece * run
        starts.append((place // block * ranks + rank) * block + place % block)
    return starts


def spatial_kernel(sizes, info_ref, qkv_ref, stream_ref, out_ref, query_ref, key_ref, value_ref, part_ref):
    groups, ranks, heads, block, span, run = sizes
    chunk = pl.program_id(0)
    _, frames, width, tokens = qkv_ref.shape
    pairs = width // PAIR
    per_frame = tokens // heads
    scale = math.log2(math.e) / math.sqrt(HEAD_DIM)
    count = info_ref[0]

    @pl.when(chunk == 0)
    def arrange():
        for each in range(heads):
            for frame in range(frames):
                pieces = [
                    qkv_ref[0, frame, :, start:start + run]
                    for rank in range(ranks) for start in runs_of(each, rank, sizes)
                ]
                query_ref[each, frame] = jnp.concatenate(pieces, axis=1)
            pieces = [
                stream_ref[frame, :, start:start + run]
                for rank in range(ranks) for frame in range(frames) for start in runs_of(each, rank, sizes)
            ]
            out_ref[each, width:, :] = jnp.concatenate(pieces, axis=1)
        for frame in range(frames):
            key_ref[frame] = flip(qkv_ref[1, frame].astype(F32)).astype(BF16)
            for pair in range(pairs):
                value_ref[frame, pair, :PAIR, :] = qkv_ref[2, frame, pair * PAIR:(pair + 1) * PAIR, :]
                value_ref[frame, pair, PAIR:, :] = jnp.ones((value_ref.shape[2] - PAIR, tokens), BF16)

    def attend(keys, masked):
        for frame in range(frames):
            for head in range(2 * pairs):
                pair = head // 2
                low = (pair * PAIR) // 128 * 128
                high = min(-(-((pair + 1) * PAIR) // 128) * 128, width)
                row = lax.broadcasted_iota(jnp.int32, (high - low, per_frame), 0) + low
                mine = (row >= head * HEAD_DIM) & (row < (head + 1) * HEAD_DIM)
                query = jnp.where(mine, query_ref[chunk, frame, low:high, :], jnp.zeros((), BF16))
                scores = jnp.dot(key_ref[frame, :keys, low:high], query, preferred_element_type=F32)
                if masked:
                    token = lax.broadcasted_iota(jnp.int32, (keys, per_frame), 0)
                    scores = jnp.where(token < count, scores, -jnp.inf)
                highest = jnp.max(scores, axis=0, keepdims=True)
                raised = jnp.exp2(scores * scale - highest * scale).astype(BF16)
                summed = jnp.dot(value_ref[frame, pair, :, :keys], raised, preferred_element_type=F32)
                inside = head % 2 * HEAD_DIM
                result = summed[inside:inside + HEAD_DIM] / summed[PAIR:PAIR + 1]
                for rank in range(ranks):
                    lane = (rank * frames + frame) * span
                    part_ref[head * HEAD_DIM:(head + 1) * HEAD_DIM, lane:lane + span] = (
                        result[:, rank * span:(rank + 1) * span]
                    )

    half = tokens // 2

    @pl.when(count >= tokens)
    def whole():
        attend(tokens, False)

    @pl.when((count < tokens) & (count > half))
    def some():
        attend(tokens, True)

    @pl.when(count <= half)
    def few():
        attend(half, True)

    out_ref[chunk, :width, :] = part_ref[...].astype(BF16)


def spatial_attention(info, qkv, stream, sizes):
    groups, ranks, heads, block, span, run = sizes
    _, frames, width, tokens = qkv.shape
    rows = frames * tokens // heads
    pairs = width // PAIR
    vmem = pl.BlockSpec(memory_space=pltpu.VMEM)
    return pl.pallas_call(
        functools.partial(spatial_kernel, sizes),
        grid_spec=pltpu.PrefetchScalarGridSpec(
            num_scalar_prefetch=1,
            grid=(heads,),
            in_specs=[vmem, vmem],
            out_specs=vmem,
            scratch_shapes=[
                pltpu.VMEM((heads, frames, width, tokens // heads), BF16),
                pltpu.VMEM((frames, tokens, width), BF16),
                pltpu.VMEM((frames, pairs, PAIR + 16, tokens), BF16),
                pltpu.VMEM((width, rows), F32),
            ],
        ),
        out_shape=jax.ShapeDtypeStruct((heads, 2 * width, rows), BF16),
        compiler_params=pltpu.CompilerParams(vmem_limit_bytes=24 * MIB),
        cost_estimate=pl.CostEstimate(flops=28 * 10**9, bytes_accessed=5 * 10**6, transcendentals=8 * 10**6),
        name="spatial_attention",
    )(info, qkv, stream)


def mix_kernel(heads, ranks, info_ref, plane_ref, core_ref, gate_ref, rows_ref, *refs):
    out_refs, weight_ref, mixed_ref = refs[:-2], refs[-2], refs[-1]
    rank, me, core, member = info_ref[3], info_ref[4], info_ref[5], info_ref[6]
    members, _, strip, _ = plane_ref.shape
    width = rows_ref.shape[1] // 2
    half = weight_ref.shape[0] // (2 * heads)
    last = half // strip - 1
    for far, ref in enumerate((plane_ref, core_ref)):
        for other in range(members):
            whose = jnp.minimum(member ^ other, last)
            for step in range(heads):
                source = lax.rem(me - step + heads, heads)
                start = source * width + (core ^ far) * half + whose * strip
                weight_ref[pl.ds(pl.multiple_of(start, 16), strip), :] = ref[other, step]
    summed = None
    for source in range(heads):
        term = tn(weight_ref[source * width:(source + 1) * width, :], rows_ref[source, :width, :])
        summed = term if summed is None else summed + term
    for source in range(heads):
        here = slice(source * width, (source + 1) * width)
        mixed = rows_ref[source, width:, :].astype(F32) + gate_ref[here, 0:1] * summed[here]
        mixed_ref[here, :] = mixed.astype(BF16)
    lanes = mixed_ref.shape[1] // ranks
    for step in range(ranks):
        to = lax.rem(rank + step, ranks)
        out_refs[step][...] = mixed_ref[:, pl.ds(pl.multiple_of(to * lanes, lanes), lanes)]


def mix(info, by_plane, by_core, arrived, columns, ranks):
    heads, width, rows = arrived.shape
    width = width // 2
    features = by_plane.shape[3]
    vmem = pl.BlockSpec(memory_space=pltpu.VMEM)
    return pl.pallas_call(
        functools.partial(mix_kernel, heads, ranks),
        in_specs=[pl.BlockSpec(memory_space=pltpu.SMEM)] + [vmem] * 4,
        out_specs=[vmem] * ranks,
        out_shape=[jax.ShapeDtypeStruct((features, rows // ranks), BF16)] * ranks,
        scratch_shapes=[pltpu.VMEM((heads * width, features), BF16), pltpu.VMEM((features, rows), BF16)],
        compiler_params=pltpu.CompilerParams(vmem_limit_bytes=28 * MIB),
        cost_estimate=pl.CostEstimate(flops=5 * 10**9, bytes_accessed=4 * 10**6, transcendentals=0),
        name="mix",
    )(info, by_plane, by_core, columns, arrived)


def frame_at(place, rank, sizes):
    ranks = sizes[1]
    frames = FRAMES // ranks
    return lax.rem(rank - place // frames + ranks, ranks) * frames + place % frames


def temporal_kernel(sizes, info_ref, cols_ref, *refs):
    groups, ranks, heads, block, span, run = sizes
    kinds = KINDS + 1
    mixed_refs, refs = refs[:ranks], refs[ranks:]
    piece_refs, out_refs = refs[:kinds], refs[kinds:-5]
    normed_ref, attended_ref, result_ref, weight_ref, last_ref = refs[-5:]
    step = pl.program_id(0)
    features, lanes = mixed_refs[0].shape
    rows = ranks * lanes
    scale = 1.0 / math.sqrt(HEAD_DIM)
    frame_count = info_ref[1]
    rank_here = info_ref[3]

    @pl.when(step == 0)
    def norm():
        for rank in range(ranks):
            full = mixed_refs[rank][...].astype(F32)
            center = full - jnp.mean(full, axis=0, keepdims=True)
            variance = jnp.mean(center * center, axis=0, keepdims=True)
            normed = center * lax.rsqrt(variance + EPS)
            normed = normed * (1.0 + cols_ref[:, 2:3]) + cols_ref[:, 1:2]
            normed_ref[:, rank * lanes:(rank + 1) * lanes] = normed.astype(BF16)

    for kind in range(KINDS):
        weight_ref[kind * PAIR:(kind + 1) * PAIR, :] = piece_refs[kind][0, 0]
    here = pl.ds(pl.multiple_of(step * PAIR, PAIR), PAIR)
    last_ref[here, :] = piece_refs[KINDS][0, 0]
    projected = jnp.dot(weight_ref[...], normed_ref[...], preferred_element_type=F32)
    frame = lax.broadcasted_iota(jnp.int32, (FRAMES, rows), 1) // span
    delta = lax.broadcasted_iota(jnp.int32, (FRAMES, rows), 0)
    key_frame = frame_at(lax.rem(frame - delta + FRAMES, FRAMES), rank_here, sizes)
    live = key_frame < frame_count

    def turned(array):
        return [array if d == 0 else pltpu.roll(array, d * span, 1) for d in range(FRAMES)]

    attended = []
    for head in range(2):
        query = projected[head * HEAD_DIM:(head + 1) * HEAD_DIM]
        key = projected[PAIR + head * HEAD_DIM:PAIR + (head + 1) * HEAD_DIM]
        value = projected[2 * PAIR + head * HEAD_DIM:2 * PAIR + (head + 1) * HEAD_DIM]
        scores = [jnp.sum(query * each, axis=0, keepdims=True) for each in turned(key)]
        scores = jnp.concatenate(scores, axis=0) * scale
        scores = jnp.where(live, scores, -jnp.inf)
        raised = jnp.exp(scores - jnp.max(scores, axis=0, keepdims=True))
        shares = raised / jnp.sum(raised, axis=0, keepdims=True)
        summed = None
        for d, each in enumerate(turned(value)):
            term = shares[d:d + 1] * each
            summed = term if summed is None else summed + term
        attended.append(summed)
    attended_ref[here, :] = jnp.concatenate(attended, axis=0).astype(BF16)

    @pl.when(step == pl.num_programs(0) - 1)
    def finish():
        width = features // heads
        clip, me, count = info_ref[2], info_ref[4], info_ref[0]
        total = tn(last_ref[...], attended_ref[...])
        for rank in range(ranks):
            lane = slice(rank * lanes, (rank + 1) * lanes)
            full = mixed_refs[rank][...].astype(F32) + cols_ref[:, 3:4] * total[:, lane]
            place = lax.broadcasted_iota(jnp.int32, (1, lanes), 1) + rank * lanes
            among = me * span + place % span
            token = (among // block * ranks + rank_here) * block + among % block
            valid = (frame_at(place // span, rank_here, sizes) < frame_count) & (token < count)
            result_ref[:, lane] = jnp.where(valid, full, 0.0).astype(BF16)
        parts = span // run
        share = max(heads // groups, 1)
        for part in range(parts):
            slot = lax.rem(part + parts - lax.rem(clip, parts), parts)
            turn = clip * share if parts == 1 else clip // parts
            for step_to in range(heads):
                to = lax.rem(me * (parts == 1) + step_to + turn, heads)
                rows_to = pl.ds(pl.multiple_of(to * width, width), width)

                def pick():
                    if parts == 1:
                        return result_ref[rows_to, :]
                    found = result_ref[rows_to, :]
                    return jnp.concatenate(
                        [found[:, f * span + part * run:f * span + (part + 1) * run] for f in range(FRAMES)], axis=1
                    )

                for each in range(parts):
                    @pl.when(slot == each)
                    def store():
                        out_refs[each * heads + step_to][...] = pick()


def temporal(info, mixed, columns, pieces, sizes):
    groups, ranks, heads, block, span, run = sizes
    features, lanes = mixed[0].shape
    rows = ranks * lanes
    kinds = KINDS + 1
    count = heads * (span // run)
    shape = (features // heads, FRAMES * run)

    def piece(kind):
        return pl.BlockSpec((1, 1, PAIR, features), lambda s, info: (2 * kind + s % 2, s // 2, 0, 0))

    return pl.pallas_call(
        functools.partial(temporal_kernel, sizes),
        grid_spec=pltpu.PrefetchScalarGridSpec(
            num_scalar_prefetch=1,
            grid=(2 * heads,),
            in_specs=[
                pl.BlockSpec(columns.shape, lambda s, info: (0, 0)),
            ] + [pl.BlockSpec(memory_space=pltpu.VMEM)] * ranks + [piece(kind) for kind in range(kinds)],
            out_specs=[pl.BlockSpec(shape, lambda s, info: (0, 0))] * count,
            scratch_shapes=[
                pltpu.VMEM((features, rows), BF16),
                pltpu.VMEM((features, rows), BF16),
                pltpu.VMEM((features, rows), BF16),
                pltpu.VMEM((KINDS * PAIR, features), BF16),
                pltpu.VMEM((features, features), BF16),
            ],
        ),
        out_shape=[jax.ShapeDtypeStruct(shape, BF16)] * count,
        compiler_params=pltpu.CompilerParams(vmem_limit_bytes=56 * MIB),
        cost_estimate=pl.CostEstimate(flops=20 * 10**9, bytes_accessed=12 * 10**6, transcendentals=0),
        name="temporal",
    )(info, columns, *mixed, *[pieces] * kinds)


def place_kernel(sizes, info_ref, *refs):
    groups, ranks, heads, block, span, run = sizes
    parts = span // run
    share = block // run
    piece_refs, out_ref, held_ref = refs[:-2], refs[-2], refs[-1]
    clip, rank, me = info_ref[2], info_ref[3], info_ref[4]
    for part in range(parts):
        for step in range(heads):
            if parts == 1:
                source = lax.rem(me - step + heads + groups * heads - clip * share, heads)
            else:
                source = lax.rem(me - step + heads, heads) * parts + lax.rem(clip - part + parts, parts)
            held_ref[source] = piece_refs[part * heads + step][...]
    for group in range(groups):
        for at in range(FRAMES):
            pieces = [held_ref[group * share + e, :, at * run:(at + 1) * run] for e in range(share)]
            out_ref[group * FRAMES + frame_at(at, rank, sizes)] = jnp.concatenate(pieces, axis=1) if share > 1 else pieces[0]


def place(info, pieces, sizes):
    groups, ranks, heads, block, span, run = sizes
    width, lanes = pieces[0].shape
    vmem = pl.BlockSpec(memory_space=pltpu.VMEM)
    return pl.pallas_call(
        functools.partial(place_kernel, sizes),
        in_specs=[pl.BlockSpec(memory_space=pltpu.SMEM)] + [vmem] * len(pieces),
        out_specs=vmem,
        out_shape=jax.ShapeDtypeStruct((groups * FRAMES, width, block), BF16),
        scratch_shapes=[pltpu.VMEM((len(pieces), width, lanes), BF16)],
        compiler_params=pltpu.CompilerParams(vmem_limit_bytes=12 * MIB),
        name="place",
    )(info, *pieces)


def routes(step, part, sizes):
    groups, ranks, heads, block, span, run = sizes
    parts = span // run
    share = block // run
    pairs = []
    for clip in range(groups):
        for head in range(heads):
            if parts == 1:
                to = (head // share, (head + step + clip * share) % heads)
            else:
                to = (head * parts + (part + clip) % parts, (step + clip // parts) % heads)
            pairs.append((clip * heads + head, to[0] * heads + to[1]))
    return pairs


def on_device(
    shape, spatial_qkv, stream, out_spatial, qkv_temporal, out_temporal, modulation, tok_count, frame_count
):
    outer, clips_inner, rank_hi, cores, heads = shape
    groups = outer * clips_inner
    ranks = rank_hi * cores
    assert cores == 2 and clips_inner * rank_hi == KINDS + 1
    clip = lax.axis_index(("outer", "clip"))
    rank = lax.axis_index(("rank", "core"))
    core = lax.axis_index("core")
    head = lax.axis_index("head")
    member = lax.axis_index(("clip", "rank"))
    width = spatial_qkv.shape[3]
    features = out_spatial.shape[1]
    frames, tokens = stream.shape[:2]
    block = tokens // (groups * ranks)
    span = tokens // (ranks * heads)
    run = min(block, span)
    sizes = (groups, ranks, heads, block, span, run)

    def send(array, axis, size, step):
        return lax.ppermute(array, axis, [(i, (i + step) % size) for i in range(size)])

    def around(arrays, axis, size):
        return [arrays[0]] + [send(arrays[k], axis, size, k) for k in range(1, size)]

    def swap(array, axis, size, bit):
        return lax.ppermute(array, axis, [(i, i ^ bit) for i in range(size)])

    info = jnp.stack([tok_count[clip], frame_count[clip], clip, rank, head, core, member]).astype(jnp.int32)
    here = lax.dynamic_index_in_dim(modulation, clip, 0, keepdims=False)
    columns = here.T

    plane = clips_inner * rank_hi
    turned = jnp.swapaxes(qkv_temporal, 1, 2)
    weight = lax.dynamic_slice(turned, (jnp.minimum(member, KINDS - 1), core * PAIR, 0), (1, PAIR, features))[0]
    other = lax.dynamic_slice(out_temporal, (core * PAIR, 0), (PAIR, features))
    weight = jnp.where(member < KINDS, weight, other)
    half = width // cores
    strip = half // KINDS
    spatial = lax.dynamic_slice(
        out_spatial, (core * half + jnp.minimum(member, KINDS - 1) * strip, 0), (strip, features)
    )
    mine = jnp.concatenate([weight, spatial], axis=0)
    mine, info = lax.optimization_barrier((mine, info))
    mine = around([mine] * heads, "head", heads)
    attended = spatial_attention(info, jnp.swapaxes(spatial_qkv, 2, 3), jnp.swapaxes(stream, 1, 2), sizes)
    mine, attended = lax.optimization_barrier((mine, attended))

    pieces = lax.all_gather(jnp.stack([each[:PAIR] for each in mine]), ("clip", "rank", "core"))
    same = jnp.stack([each[PAIR:] for each in mine])
    by_plane = [same] + [swap(same, ("clip", "rank"), plane, bit) for bit in range(1, plane)]
    arrived = lax.all_to_all(attended, "head", 0, 0)
    by_plane = jnp.stack(by_plane)
    by_core = swap(by_plane, "core", cores, 1)
    mixed = mix(info, by_plane, by_core, arrived, columns, ranks)
    mixed = around(mixed, ("rank", "core"), ranks)
    result = temporal(info, mixed, columns, pieces, sizes)
    arrived = [
        lax.ppermute(result[part * heads + step], ("outer", "clip", "head"), routes(step, part, sizes))
        for part in range(span // run) for step in range(heads)
    ]
    return jnp.swapaxes(place(info, arrived, sizes), 1, 2)


def solution(mesh):
    seq, heads = mesh.shape["seq"], mesh.shape["head"]

    def whole(spatial_qkv, stream, *rest):
        frames = spatial_qkv.shape[1] // seq
        ranks = FRAMES // frames
        clips_inner = SLICES // ranks
        shape = (seq // SLICES, clips_inner, ranks // 2, 2, heads)
        fine = Mesh(mesh.devices.reshape(shape), ("outer", "clip", "rank", "core", "head"))
        split = ("outer", "clip", "rank", "core")
        in_specs = (
            P(None, split, None, "head"),
            P(split, None, "head"),
            P("head", None),
            P(None, None, "head"),
            P("head", None),
            P(),
            P(),
            P(),
        )
        return jax.shard_map(
            functools.partial(on_device, shape), mesh=fine, in_specs=in_specs, out_specs=P(None, split, "head"),
            check_vma=False,
        )(spatial_qkv, stream, *rest)

    return whole
```

profile of v0, /device:TPU:13, one launch (start us, length us, event | category | flops | bytes accessed | tf_op | source)
XLA Modules:
  0.0 208.0 jit_solution(17193783269367498866)
XLA Ops:
  6.5 1.4 dynamic_slice.22
  7.9 1.2 dynamic_slice.23
  10.4 1.3 stack.68.info_ref
  11.6 1.3 collective-permute-start
  14.0 1.4 collective-permute-start.2
  15.4 2.0 copy-done.4
  17.4 29.3 %spatial_attention.1 = bf16[4,576,512]{2,1,0:T(8,128)(2,1)} custom-call(s32[7]{0:T(128)S(1)} %stack.68.info_ref, bf16[3,2,288,1024]{3,2,1,0:T(8,128)(2,1)S(1)} %bitcast.39, bf16[2,288,1024]{2,1,0:T(8,128)(2,1)S(1)} %bitcast.40), custom_call_target="tpu_custom_call" | custom-call | flops 28000000000 | bytes 5000000 | tf_op jit(solution)/shard_map/spatial_attention/pallas_call | solution.py:116
  46.7 3.5 %collective-permute-done.1 = bf16[192,1152]{1,0:T(8,128)(2,1)S(1)} collective-permute-done((bf16[192,1152]{1,0:T(8,128)(2,1)S(1)}, bf16[192,1152]{1,0:T(8,128)(2,1)S(1)}, u32[]{:S(2)}, u32[]{:S(2)}) %collective-permute-start.1) | collective-permute-done | bytes 442400 | tf_op jit(solution)/shard_map/ppermute | solution.py:382
  50.2 3.0 %collective-permute-done.2 = bf16[192,1152]{1,0:T(8,128)(2,1)} collective-permute-done((bf16[192,1152]{1,0:T(8,128)(2,1)S(1)}, bf16[192,1152]{1,0:T(8,128)(2,1)}, u32[]{:S(2)}, u32[]{:S(2)}) %collective-permute-start.2) | collective-permute-done | bytes 442400 | tf_op jit(solution)/shard_map/ppermute | solution.py:382
  54.3 1.3 pad_maximum_fusion.1
  55.6 3.6 %all-to-all-start = ((bf16[4,576,512]{2,1,0:T(8,128)(2,1)}), bf16[4,576,512]{2,1,0:T(8,128)(2,1)S(1)}, u32[]{:S(2)}, u32[]{:S(2)}) async-start(bf16[4,576,512]{2,1,0:T(8,128)(2,1)} %spatial_attention.1), calls=%async_computation | async-start | bytes 4718592 | tf_op jit(solution)/shard_map/all_to_all | solution.py:413
  62.5 1.2 collective-permute-start.4
  64.0 14.5 %collective-permute-done.5 = bf16[4,48,1152]{2,1,0:T(8,128)(2,1)S(1)} collective-permute-done((bf16[4,48,1152]{2,1,0:T(8,128)(2,1)S(1)}, bf16[4,48,1152]{2,1,0:T(8,128)(2,1)S(1)}, u32[]{:S(2)}, u32[]{:S(2)}) %collective-permute-start.5) | collective-permute-done | bytes 442400 | tf_op jit(solution)/shard_map/ppermute | solution.py:388
  78.5 14.7 %collective-permute-done.4 = bf16[4,48,1152]{2,1,0:T(8,128)(2,1)S(1)} collective-permute-done((bf16[4,48,1152]{2,1,0:T(8,128)(2,1)S(1)}, bf16[4,48,1152]{2,1,0:T(8,128)(2,1)S(1)}, u32[]{:S(2)}, u32[]{:S(2)}) %collective-permute-start.4) | collective-permute-done | bytes 442400 | tf_op jit(solution)/shard_map/ppermute | solution.py:388
  93.2 2.3 %collective-permute-done.3 = bf16[4,48,1152]{2,1,0:T(8,128)(2,1)S(1)} collective-permute-done((bf16[4,48,1152]{2,1,0:T(8,128)(2,1)S(1)}, bf16[4,48,1152]{2,1,0:T(8,128)(2,1)S(1)}, u32[]{:S(2)}, u32[]{:S(2)}) %collective-permute-start.3) | collective-permute-done | bytes 442400 | tf_op jit(solution)/shard_map/ppermute | solution.py:388
  95.5 1.5 pad_maximum_fusion.plane_ref
  97.0 2.1 collective-permute-start.6
  100.1 2.6 %collective-permute-done.6.core_ref = bf16[4,4,48,1152]{3,2,1,0:T(8,128)(2,1)} collective-permute-done((bf16[4,4,48,1152]{3,2,1,0:T(8,128)(2,1)}, bf16[4,4,48,1152]{3,2,1,0:T(8,128)(2,1)}, u32[]{:S(2)}, u32[]{:S(2)}) %collective-permute-start.6) | collective-permute-done | bytes 1769504 | tf_op jit(solution)/shard_map/ppermute | solution.py:388
  102.7 6.4 %all-to-all-done.rows_ref = bf16[4,576,512]{2,1,0:T(8,128)(2,1)S(1)} async-done(((bf16[4,576,512]{2,1,0:T(8,128)(2,1)}), bf16[4,576,512]{2,1,0:T(8,128)(2,1)S(1)}, u32[]{:S(2)}, u32[]{:S(2)}) %all-to-all-start) | async-done | bytes 2359328 | tf_op jit(solution)/shard_map/all_to_all | solution.py:413
  110.2 5.6 %mix.1 = (bf16[1152,128]{1,0:T(8,128)(2,1)S(1)}, bf16[1152,128]{1,0:T(8,128)(2,1)S(1)}, bf16[1152,128]{1,0:T(8,128)(2,1)S(1)}, bf16[1152,128]{1,0:T(8,128)(2,1)S(1)}) custom-call(s32[7]{0:T(128)S(1)} %stack.68.info_ref, bf16[4,4,48,1152]{3,2,1,0:T(8,128)(2,1)} %pad_maximum_fusion.plane_ref, bf16[4,4,48,1152]{3,2,1,0:T(8,128)(2,1)} %collective-permute-done.6.core_ref, ...), custom_call_target="tpu_custom_call" | custom-call | flops 5000000000 | bytes 4000000 | tf_op jit(solution)/shard_map/mix/pallas_call | solution.py:170
  116.4 3.2 %collective-permute-start.7 = (bf16[1152,128]{1,0:T(8,128)(2,1)S(1)}, bf16[1152,128]{1,0:T(8,128)(2,1)S(1)}, u32[]{:S(2)}, u32[]{:S(2)}) collective-permute-start(bf16[1152,128]{1,0:T(8,128)(2,1)S(1)} %get-tuple-element.28), channel_id=1, source_target_pairs={{0,4},{4,8},{8,12},{12,0},{1,5},{5,9},{9,13},{13,1},{2,6},{6,10},{... | collective-permute-start | bytes 884744 | tf_op jit(solution)/shard_map/ppermute | solution.py:382
  120.0 12.5 %collective-permute-done.7.refs_1_ = bf16[1152,128]{1,0:T(8,128)(2,1)S(1)} collective-permute-done((bf16[1152,128]{1,0:T(8,128)(2,1)S(1)}, bf16[1152,128]{1,0:T(8,128)(2,1)S(1)}, u32[]{:S(2)}, u32[]{:S(2)}) %collective-permute-start.7) | collective-permute-done | bytes 294944 | tf_op jit(solution)/shard_map/ppermute | solution.py:382
  132.5 13.5 %collective-permute-done.8.refs_2_ = bf16[1152,128]{1,0:T(8,128)(2,1)S(1)} collective-permute-done((bf16[1152,128]{1,0:T(8,128)(2,1)S(1)}, bf16[1152,128]{1,0:T(8,128)(2,1)S(1)}, u32[]{:S(2)}, u32[]{:S(2)}) %collective-permute-start.8) | collective-permute-done | bytes 294944 | tf_op jit(solution)/shard_map/ppermute | solution.py:382
  146.2 1.6 all-gather.3.cloned.1.call-done
  147.8 17.1 %temporal.1 = (bf16[288,512]{1,0:T(8,128)(2,1)}, bf16[288,512]{1,0:T(8,128)(2,1)}, bf16[288,512]{1,0:T(8,128)(2,1)}, bf16[288,512]{1,0:T(8,128)(2,1)}) custom-call(s32[7]{0:T(128)} %copy-done.2, f32[1152,4]{1,0:T(8,128)} %bitcast.37, bf16[1152,128]{1,0:T(8,128)(2,1)} %copy-done.6, bf16[1152,128]{1,0:T(8,128)(2,1)} %copy-done.10, ...), custom_call_target="tpu_custom_call" | custom-call | flops 20000000000 | bytes 12000000 | tf_op jit(solution)/shard_map/temporal/pallas_call | solution.py:288
  165.0 3.2 %collective-permute-start.10 = (bf16[288,512]{1,0:T(8,128)(2,1)}, bf16[288,512]{1,0:T(8,128)(2,1)S(1)}, u32[]{:S(2)}, u32[]{:S(2)}) collective-permute-start(bf16[288,512]{1,0:T(8,128)(2,1)} %get-tuple-element.31), channel_id=1, source_target_pairs={{0,0},{1,1},{2,18},{3,19},{16,2},{17,3},{18,16},{19,17},{4,4},{5,5... | collective-permute-start | bytes 884744 | tf_op jit(solution)/shard_map/ppermute | solution.py:420
  168.2 3.5 %collective-permute-start.12 = (bf16[288,512]{1,0:T(8,128)(2,1)}, bf16[288,512]{1,0:T(8,128)(2,1)S(1)}, u32[]{:S(2)}, u32[]{:S(2)}) collective-permute-start(bf16[288,512]{1,0:T(8,128)(2,1)} %get-tuple-element.33), channel_id=1, source_target_pairs={{0,2},{1,3},{2,16},{3,17},{16,0},{17,1},{18,18},{19,19},{4,6},{5,7... | collective-permute-start | bytes 884744 | tf_op jit(solution)/shard_map/ppermute | solution.py:420
  171.7 3.0 %collective-permute-start.13 = (bf16[288,512]{1,0:T(8,128)(2,1)}, bf16[288,512]{1,0:T(8,128)(2,1)S(1)}, u32[]{:S(2)}, u32[]{:S(2)}) collective-permute-start(bf16[288,512]{1,0:T(8,128)(2,1)} %get-tuple-element.34), channel_id=1, source_target_pairs={{0,3},{1,0},{2,17},{3,18},{16,1},{17,2},{18,19},{19,16},{4,7},{5,4... | collective-permute-start | bytes 884744 | tf_op jit(solution)/shard_map/ppermute | solution.py:420
  174.7 12.6 %collective-permute-done.10.refs_0_ = bf16[288,512]{1,0:T(8,128)(2,1)S(1)} collective-permute-done((bf16[288,512]{1,0:T(8,128)(2,1)}, bf16[288,512]{1,0:T(8,128)(2,1)S(1)}, u32[]{:S(2)}, u32[]{:S(2)}) %collective-permute-start.10) | collective-permute-done | bytes 294944 | tf_op jit(solution)/shard_map/ppermute | solution.py:420
  187.2 7.3 %collective-permute-done.11.refs_1_ = bf16[288,512]{1,0:T(8,128)(2,1)S(1)} collective-permute-done((bf16[288,512]{1,0:T(8,128)(2,1)}, bf16[288,512]{1,0:T(8,128)(2,1)S(1)}, u32[]{:S(2)}, u32[]{:S(2)}) %collective-permute-start.11) | collective-permute-done | bytes 294944 | tf_op jit(solution)/shard_map/ppermute | solution.py:420
  194.6 4.5 %collective-permute-done.13.refs_3_ = bf16[288,512]{1,0:T(8,128)(2,1)S(1)} collective-permute-done((bf16[288,512]{1,0:T(8,128)(2,1)}, bf16[288,512]{1,0:T(8,128)(2,1)S(1)}, u32[]{:S(2)}, u32[]{:S(2)}) %collective-permute-start.13) | collective-permute-done | bytes 294944 | tf_op jit(solution)/shard_map/ppermute | solution.py:420
  199.1 2.0 place.1
  (46 shorter events, 10.4 us)
Async XLA Ops:
  6.5 2.6 %copy-start = (bf16[288,1152]{1,0:T(8,128)(2,1)S(1)}, bf16[288,1152]{1,0:T(8,128)(2,1)}, u32[]{:S(2)}) copy-start(bf16[288,1152]{1,0:T(8,128)(2,1)} %param.10) | copy-start | bytes 1990660
  6.5 8.9 %copy-start.5 = (bf16[2,1024,288]{1,2,0:T(8,128)(2,1)S(1)}, bf16[2,1024,288]{1,2,0:T(8,128)(2,1)}, u32[]{:S(2)}) copy-start(bf16[2,1024,288]{1,2,0:T(8,128)(2,1)} %param.9) | copy-start | bytes 3538948
  6.5 141.3 %all-gather.3.cloned.1.call-start = ((), (), s32[]{:S(2)}) async-start(), calls=%async_computation.1 | async-start | bytes 11943936 | tf_op jit(solution)/shard_map/all_gather | solution.py:410
  11.6 97.5 %copy-start.2 = (s32[7]{0:T(128)}, s32[7]{0:T(128)S(1)}, u32[]{:S(2)}) copy-start(s32[7]{0:T(128)S(1)} %stack.68.info_ref) | copy-start | bytes 88
  11.6 35.1 %collective-permute-start = (bf16[192,1152]{1,0:T(8,128)(2,1)S(1)}, bf16[192,1152]{1,0:T(8,128)(2,1)S(1)}, u32[]{:S(2)}, u32[]{:S(2)}) collective-permute-start(bf16[192,1152]{1,0:T(8,128)(2,1)S(1)} %pad_maximum_fusion.2), channel_id=1, source_target_pairs={{0,1},{1,2},{2,3},{3,0},{4,5},{5,6},{6,7},{7,4},{8,9},{9,10},{10,1... | collective-permute-start | bytes 1327112 | tf_op jit(solution)/shard_map/ppermute | solution.py:382
  13.0 37.3 %collective-permute-start.1 = (bf16[192,1152]{1,0:T(8,128)(2,1)S(1)}, bf16[192,1152]{1,0:T(8,128)(2,1)S(1)}, u32[]{:S(2)}, u32[]{:S(2)}) collective-permute-start(bf16[192,1152]{1,0:T(8,128)(2,1)S(1)} %pad_maximum_fusion.2), channel_id=1, source_target_pairs={{0,2},{1,3},{2,0},{3,1},{4,6},{5,7},{6,4},{7,5},{8,10},{9,11},{10,... | collective-permute-start | bytes 1327112 | tf_op jit(solution)/shard_map/ppermute | solution.py:382
  14.0 39.1 %collective-permute-start.2 = (bf16[192,1152]{1,0:T(8,128)(2,1)S(1)}, bf16[192,1152]{1,0:T(8,128)(2,1)}, u32[]{:S(2)}, u32[]{:S(2)}) collective-permute-start(bf16[192,1152]{1,0:T(8,128)(2,1)S(1)} %pad_maximum_fusion.2), channel_id=1, source_target_pairs={{0,3},{1,0},{2,1},{3,2},{4,7},{5,4},{6,5},{7,6},{8,11},{9,8},{10,9... | collective-permute-start | bytes 1327112 | tf_op jit(solution)/shard_map/ppermute | solution.py:382
  15.4 2.0 copy-start.4
  46.7 8.9 %copy-start.7 = (bf16[192,1152]{1,0:T(8,128)(2,1)}, bf16[192,1152]{1,0:T(8,128)(2,1)S(1)}, u32[]{:S(2)}) copy-start(bf16[192,1152]{1,0:T(8,128)(2,1)S(1)} %collective-permute-done) | copy-start | bytes 1327108
  50.2 5.4 %copy-start.8 = (bf16[192,1152]{1,0:T(8,128)(2,1)}, bf16[192,1152]{1,0:T(8,128)(2,1)S(1)}, u32[]{:S(2)}) copy-start(bf16[192,1152]{1,0:T(8,128)(2,1)S(1)} %collective-permute-done.1) | copy-start | bytes 1327108
  55.6 53.5 %all-to-all-start = ((bf16[4,576,512]{2,1,0:T(8,128)(2,1)}), bf16[4,576,512]{2,1,0:T(8,128)(2,1)S(1)}, u32[]{:S(2)}, u32[]{:S(2)}) async-start(bf16[4,576,512]{2,1,0:T(8,128)(2,1)} %spatial_attention.1), calls=%async_computation | async-start | bytes 4718592 | tf_op jit(solution)/shard_map/all_to_all | solution.py:413
  61.2 17.2 %collective-permute-start.5 = (bf16[4,48,1152]{2,1,0:T(8,128)(2,1)S(1)}, bf16[4,48,1152]{2,1,0:T(8,128)(2,1)S(1)}, u32[]{:S(2)}, u32[]{:S(2)}) collective-permute-start(bf16[4,48,1152]{2,1,0:T(8,128)(2,1)S(1)} %get-tuple-element.36), channel_id=1, source_target_pairs={{0,24},{8,16},{16,8},{24,0},{1,25},{9,17},{17,9},{25,1},{2,26},{10... | collective-permute-start | bytes 1327112 | tf_op jit(solution)/shard_map/ppermute | solution.py:388
  62.5 30.7 %collective-permute-start.4 = (bf16[4,48,1152]{2,1,0:T(8,128)(2,1)S(1)}, bf16[4,48,1152]{2,1,0:T(8,128)(2,1)S(1)}, u32[]{:S(2)}, u32[]{:S(2)}) collective-permute-start(bf16[4,48,1152]{2,1,0:T(8,128)(2,1)S(1)} %get-tuple-element.36), channel_id=1, source_target_pairs={{0,16},{8,24},{16,0},{24,8},{1,17},{9,25},{17,1},{25,9},{2,18},{10... | collective-permute-start | bytes 1327112 | tf_op jit(solution)/shard_map/ppermute | solution.py:388
  63.7 31.8 %collective-permute-start.3 = (bf16[4,48,1152]{2,1,0:T(8,128)(2,1)S(1)}, bf16[4,48,1152]{2,1,0:T(8,128)(2,1)S(1)}, u32[]{:S(2)}, u32[]{:S(2)}) collective-permute-start(bf16[4,48,1152]{2,1,0:T(8,128)(2,1)S(1)} %get-tuple-element.36), channel_id=1, source_target_pairs={{0,8},{8,0},{16,24},{24,16},{1,9},{9,1},{17,25},{25,17},{2,10},{10... | collective-permute-start | bytes 1327112 | tf_op jit(solution)/shard_map/ppermute | solution.py:388
  95.5 3.5 %copy-start.9 = (f32[2,4,1152]{2,1,0:T(4,128)S(1)}, f32[2,4,1152]{2,1,0:T(4,128)}, u32[]{:S(2)}) copy-start(f32[2,4,1152]{2,1,0:T(4,128)} %param.13) | copy-start | bytes 110596
  97.0 5.7 %collective-permute-start.6 = (bf16[4,4,48,1152]{3,2,1,0:T(8,128)(2,1)}, bf16[4,4,48,1152]{3,2,1,0:T(8,128)(2,1)}, u32[]{:S(2)}, u32[]{:S(2)}) collective-permute-start(bf16[4,4,48,1152]{3,2,1,0:T(8,128)(2,1)} %pad_maximum_fusion.plane_ref), channel_id=1, source_target_pairs={{0,4},{4,0},{1,5},{5,1},{2,6},{6,2},{3,7},{7,3},{8,12},{12,8},{9,1... | collective-permute-start | bytes 5308424 | tf_op jit(solution)/shard_map/ppermute | solution.py:388
  109.1 1.1 copy-start.1
  115.7 0.7 copy-start.6
  116.4 16.1 %collective-permute-start.7 = (bf16[1152,128]{1,0:T(8,128)(2,1)S(1)}, bf16[1152,128]{1,0:T(8,128)(2,1)S(1)}, u32[]{:S(2)}, u32[]{:S(2)}) collective-permute-start(bf16[1152,128]{1,0:T(8,128)(2,1)S(1)} %get-tuple-element.28), channel_id=1, source_target_pairs={{0,4},{4,8},{8,12},{12,0},{1,5},{5,9},{9,13},{13,1},{2,6},{6,10},{... | collective-permute-start | bytes 884744 | tf_op jit(solution)/shard_map/ppermute | solution.py:382
  119.6 26.4 %collective-permute-start.8 = (bf16[1152,128]{1,0:T(8,128)(2,1)S(1)}, bf16[1152,128]{1,0:T(8,128)(2,1)S(1)}, u32[]{:S(2)}, u32[]{:S(2)}) collective-permute-start(bf16[1152,128]{1,0:T(8,128)(2,1)S(1)} %get-tuple-element.29), channel_id=1, source_target_pairs={{0,8},{4,12},{8,0},{12,4},{1,9},{5,13},{9,1},{13,5},{2,10},{6,14},... | collective-permute-start | bytes 884744 | tf_op jit(solution)/shard_map/ppermute | solution.py:382
  119.8 26.3 %collective-permute-start.9 = (bf16[1152,128]{1,0:T(8,128)(2,1)S(1)}, bf16[1152,128]{1,0:T(8,128)(2,1)S(1)}, u32[]{:S(2)}, u32[]{:S(2)}) collective-permute-start(bf16[1152,128]{1,0:T(8,128)(2,1)S(1)} %get-tuple-element.30), channel_id=1, source_target_pairs={{0,12},{4,0},{8,4},{12,8},{1,13},{5,1},{9,5},{13,9},{2,14},{6,2},{... | collective-permute-start | bytes 884744 | tf_op jit(solution)/shard_map/ppermute | solution.py:382
  132.5 15.3 %copy-start.10 = (bf16[1152,128]{1,0:T(8,128)(2,1)}, bf16[1152,128]{1,0:T(8,128)(2,1)S(1)}, u32[]{:S(2)}) copy-start(bf16[1152,128]{1,0:T(8,128)(2,1)S(1)} %collective-permute-done.7.refs_1_) | copy-start | bytes 884740
  146.0 1.8 copy-start.11
  146.2 1.6 copy-start.12
  147.8 51.3 %copy-start.3 = (s32[7]{0:T(128)S(1)}, s32[7]{0:T(128)}, u32[]{:S(2)}) copy-start(s32[7]{0:T(128)} %copy-done.2) | copy-start | bytes 88
  165.0 22.3 %collective-permute-start.10 = (bf16[288,512]{1,0:T(8,128)(2,1)}, bf16[288,512]{1,0:T(8,128)(2,1)S(1)}, u32[]{:S(2)}, u32[]{:S(2)}) collective-permute-start(bf16[288,512]{1,0:T(8,128)(2,1)} %get-tuple-element.31), channel_id=1, source_target_pairs={{0,0},{1,1},{2,18},{3,19},{16,2},{17,3},{18,16},{19,17},{4,4},{5,5... | collective-permute-start | bytes 884744 | tf_op jit(solution)/shard_map/ppermute | solution.py:420
  168.1 26.5 %collective-permute-start.11 = (bf16[288,512]{1,0:T(8,128)(2,1)}, bf16[288,512]{1,0:T(8,128)(2,1)S(1)}, u32[]{:S(2)}, u32[]{:S(2)}) collective-permute-start(bf16[288,512]{1,0:T(8,128)(2,1)} %get-tuple-element.32), channel_id=1, source_target_pairs={{0,1},{1,2},{2,19},{3,16},{16,3},{17,0},{18,17},{19,18},{4,5},{5,6... | collective-permute-start | bytes 884744 | tf_op jit(solution)/shard_map/ppermute | solution.py:420
  168.2 26.4 %collective-permute-start.12 = (bf16[288,512]{1,0:T(8,128)(2,1)}, bf16[288,512]{1,0:T(8,128)(2,1)S(1)}, u32[]{:S(2)}, u32[]{:S(2)}) collective-permute-start(bf16[288,512]{1,0:T(8,128)(2,1)} %get-tuple-element.33), channel_id=1, source_target_pairs={{0,2},{1,3},{2,16},{3,17},{16,0},{17,1},{18,18},{19,19},{4,6},{5,7... | collective-permute-start | bytes 884744 | tf_op jit(solution)/shard_map/ppermute | solution.py:420
  171.7 27.5 %collective-permute-start.13 = (bf16[288,512]{1,0:T(8,128)(2,1)}, bf16[288,512]{1,0:T(8,128)(2,1)S(1)}, u32[]{:S(2)}, u32[]{:S(2)}) collective-permute-start(bf16[288,512]{1,0:T(8,128)(2,1)} %get-tuple-element.34), channel_id=1, source_target_pairs={{0,3},{1,0},{2,17},{3,18},{16,1},{17,2},{18,19},{19,16},{4,7},{5,4... | collective-permute-start | bytes 884744 | tf_op jit(solution)/shard_map/ppermute | solution.py:420
Sparse Core Ops, SparseCore 0:
  55.7 92.0 all-gather.2
where the time goes:
time: 209 us; the launch traced here: 208 us
  waiting for transfers between devices  99.2 us (47%)
  Pallas kernels  54 us (26%)
  starting transfers between devices  25.5 us (12%)
  between operations  13.5 us (6%)
  local copies, waits for them, and re-layouts  11.8 us (6%)
  other arithmetic  4.03 us (2%)
    ppermute x4, waiting for transfers between devices, swap(): return lax.ppermute(array, axis, [(i, i ^ bit) for i in range(size)])  34.1 us
    ppermute x6, waiting for transfers between devices, send(): lax.ppermute(array, axis, [(i, (i + step) % size) for i in range(size)])  32.6 us
    pallas_call x1, Pallas kernels, spatial_attention(): pl.pallas_call(functools.partial(spatial_kernel, sizes), grid_spec=pltpu....  29.3 us
    ppermute x4, waiting for transfers between devices, on_device(): lax.ppermute(result[part * heads + step], ('outer', 'clip', 'head'), rout...  24.5 us
    pallas_call x1, Pallas kernels, temporal(): pl.pallas_call(functools.partial(temporal_kernel, sizes), grid_spec=pltpu...  17.1 us
    ppermute x4, starting transfers between devices, on_device(): lax.ppermute(result[part * heads + step], ('outer', 'clip', 'head'), rout...  9.68 us
    ppermute x6, starting transfers between devices, send(): lax.ppermute(array, axis, [(i, (i + step) % size) for i in range(size)])  7.37 us
    all_to_all x1, waiting for transfers between devices, on_device(): arrived = lax.all_to_all(attended, 'head', 0, 0)  6.42 us
  transfers between devices with their start and end apart: 16, of which 14 were waited for; matrix products, arithmetic and copies ran while one was open for 2% of the time, Pallas kernels for 17%

commit v1 on v0

--- a/solution.py
+++ b/solution.py
@@ -189,7 +189,7 @@
     groups, ranks, heads, block, span, run = sizes
     kinds = KINDS + 1
     mixed_refs, refs = refs[:ranks], refs[ranks:]
-    piece_refs, out_refs = refs[:kinds], refs[kinds:-5]
+    piece_refs, out_refs = refs[:2 * heads], refs[2 * heads:-5]
     normed_ref, attended_ref, result_ref, weight_ref, last_ref = refs[-5:]
     step = pl.program_id(0)
     features, lanes = mixed_refs[0].shape
@@ -208,11 +208,19 @@
             normed = normed * (1.0 + cols_ref[:, 2:3]) + cols_ref[:, 1:2]
             normed_ref[:, rank * lanes:(rank + 1) * lanes] = normed.astype(BF16)
 
-    for kind in range(KINDS):
-        weight_ref[kind * PAIR:(kind + 1) * PAIR, :] = piece_refs[kind][0, 0]
+    member = info_ref[6]
     here = pl.ds(pl.multiple_of(step * PAIR, PAIR), PAIR)
-    last_ref[here, :] = piece_refs[KINDS][0, 0]
-    projected = jnp.dot(weight_ref[...], normed_ref[...], preferred_element_type=F32)
+    for group in range(len(piece_refs) // 2):
+        @pl.when(step // 2 == group)
+        def take():
+            for other in range(kinds):
+                kind = member ^ other
+                rows_to = pl.ds(pl.multiple_of(kind * PAIR, PAIR), PAIR)
+                at = (other // 2, other % 2) if group % 2 == 0 else (other % 2, other // 2)
+                weight_ref[rows_to, :] = piece_refs[2 * group + at[0]][at[1], step % 2]
+
+    last_ref[here, :] = weight_ref[KINDS * PAIR:, :]
+    projected = jnp.dot(weight_ref[:KINDS * PAIR, :], normed_ref[...], preferred_element_type=F32)
     frame = lax.broadcasted_iota(jnp.int32, (FRAMES, rows), 1) // span
     delta = lax.broadcasted_iota(jnp.int32, (FRAMES, rows), 0)
     key_frame = frame_at(lax.rem(frame - delta + FRAMES, FRAMES), rank_here, sizes)
@@ -282,9 +290,6 @@
     count = heads * (span // run)
     shape = (features // heads, FRAMES * run)
 
-    def piece(kind):
-        return pl.BlockSpec((1, 1, PAIR, features), lambda s, info: (2 * kind + s % 2, s // 2, 0, 0))
-
     return pl.pallas_call(
         functools.partial(temporal_kernel, sizes),
         grid_spec=pltpu.PrefetchScalarGridSpec(
@@ -292,21 +297,21 @@
             grid=(2 * heads,),
             in_specs=[
                 pl.BlockSpec(columns.shape, lambda s, info: (0, 0)),
-            ] + [pl.BlockSpec(memory_space=pltpu.VMEM)] * ranks + [piece(kind) for kind in range(kinds)],
+            ] + [pl.BlockSpec(memory_space=pltpu.VMEM)] * (ranks + len(pieces)),
             out_specs=[pl.BlockSpec(shape, lambda s, info: (0, 0))] * count,
             scratch_shapes=[
                 pltpu.VMEM((features, rows), BF16),
                 pltpu.VMEM((features, rows), BF16),
                 pltpu.VMEM((features, rows), BF16),
-                pltpu.VMEM((KINDS * PAIR, features), BF16),
+                pltpu.VMEM((kinds * PAIR, features), BF16),
                 pltpu.VMEM((features, features), BF16),
             ],
         ),
         out_shape=[jax.ShapeDtypeStruct(shape, BF16)] * count,
-        compiler_params=pltpu.CompilerParams(vmem_limit_bytes=56 * MIB),
+        compiler_params=pltpu.CompilerParams(vmem_limit_bytes=24 * MIB),
         cost_estimate=pl.CostEstimate(flops=20 * 10**9, bytes_accessed=12 * 10**6, transcendentals=0),
         name="temporal",
-    )(info, columns, *mixed, *[pieces] * kinds)
+    )(info, columns, *mixed, *pieces)
 
 
 def place_kernel(sizes, info_ref, *refs):
@@ -407,14 +412,22 @@
     attended = spatial_attention(info, jnp.swapaxes(spatial_qkv, 2, 3), jnp.swapaxes(stream, 1, 2), sizes)
     mine, attended = lax.optimization_barrier((mine, attended))
 
-    pieces = lax.all_gather(jnp.stack([each[:PAIR] for each in mine]), ("clip", "rank", "core"))
+    arrived = lax.all_to_all(attended, "head", 0, 0)
     same = jnp.stack([each[PAIR:] for each in mine])
     by_plane = [same] + [swap(same, ("clip", "rank"), plane, bit) for bit in range(1, plane)]
-    arrived = lax.all_to_all(attended, "head", 0, 0)
     by_plane = jnp.stack(by_plane)
     by_core = swap(by_plane, "core", cores, 1)
+    pieces = []
+    for first, second, pair in ((1, 2, mine[:2]), (2, 1, mine[2:])):
+        half = jnp.stack([each[:PAIR] for each in pair])
+        half = jnp.stack([half, swap(half, ("clip", "rank"), plane, first)])
+        pieces.append((half, swap(half, ("clip", "rank"), plane, second)))
+    pieces = [each for group in pieces for each in group]
+    crossed = [swap(each, "core", cores, 1) for each in pieces[::2]]
     mixed = mix(info, by_plane, by_core, arrived, columns, ranks)
+    pieces, mixed = lax.optimization_barrier((pieces, mixed))
     mixed = around(mixed, ("rank", "core"), ranks)
+    pieces += [crossed[0], swap(pieces[1], "core", cores, 1), crossed[1], swap(pieces[3], "core", cores, 1)]
     result = temporal(info, mixed, columns, pieces, sizes)
     arrived = [
         lax.ppermute(result[part * heads + step], ("outer", "clip", "head"), routes(step, part, sizes))

time: 209 us -> 187 us (0.89)
  between operations: 13.5 us -> 0.14 us
  Pallas kernels: 54 us -> 44.4 us
  waiting for transfers between devices: 99.2 us -> 92.8 us
  starting transfers between devices: 25.5 us -> 31.2 us
  other arithmetic: 4.03 us -> 7.54 us
    pallas_call x1, Pallas kernels: 29.3 us -> 19 us  [spatial_attention(): pl.pallas_call(functools.partial(spatial_kernel, sizes), grid_spec=pltpu....]
    ppermute x4 -> x12, starting transfers between devices: 4.78 us -> 13.6 us  [swap(): return lax.ppermute(array, axis, [(i, i ^ bit) for i in range(size)])]
    ppermute x4 -> x12, waiting for transfers between devices: 34.1 us -> 25.8 us  [swap(): return lax.ppermute(array, axis, [(i, i ^ bit) for i in range(size)])]
    all_to_all x1, waiting for transfers between devices: 6.42 us -> 13.1 us  [on_device(): arrived = lax.all_to_all(attended, 'head', 0, 0)]
    ppermute x6, waiting for transfers between devices: 32.6 us -> 30 us  [send(): lax.ppermute(array, axis, [(i, (i + step) % size) for i in range(size)])]
    another operation x2, other arithmetic: 1.56 us -> 3.76 us  [on_device(): by_plane = jnp.stack(by_plane)]
  transfers between devices with their start and end apart: 16 -> 23, of which waited for: 14 -> 15; matrix products, arithmetic and copies ran while one was open for 2% -> 4% of each run, Pallas kernels for 17% -> 13%
where the time goes in v1:
time: 187 us; the launch traced here: 186 us
  waiting for transfers between devices  92.8 us (50%)
  Pallas kernels  44.4 us (24%)
  starting transfers between devices  31.2 us (17%)
  local copies, waits for them, and re-layouts  10.2 us (5%)
  other arithmetic  7.54 us (4%)
    ppermute x6, waiting for transfers between devices, send(): lax.ppermute(array, axis, [(i, (i + step) % size) for i in range(size)])  30 us
    ppermute x12, waiting for transfers between devices, swap(): return lax.ppermute(array, axis, [(i, i ^ bit) for i in range(size)])  25.8 us
    ppermute x4, waiting for transfers between devices, on_device(): lax.ppermute(result[part * heads + step], ('outer', 'clip', 'head'), rout...  23.9 us
    pallas_call x1, Pallas kernels, spatial_attention(): pl.pallas_call(functools.partial(spatial_kernel, sizes), grid_spec=pltpu....  19 us
    pallas_call x1, Pallas kernels, temporal(): pl.pallas_call(functools.partial(temporal_kernel, sizes), grid_spec=pltpu...  17.7 us
    ppermute x12, starting transfers between devices, swap(): return lax.ppermute(array, axis, [(i, i ^ bit) for i in range(size)])  13.6 us
    all_to_all x1, waiting for transfers between devices, on_device(): arrived = lax.all_to_all(attended, 'head', 0, 0)  13.1 us
    ppermute x4, starting transfers between devices, on_device(): lax.ppermute(result[part * heads + step], ('outer', 'clip', 'head'), rout...  8.12 us
  transfers between devices with their start and end apart: 23, of which 15 were waited for; matrix products, arithmetic and copies ran while one was open for 4% of the time, Pallas kernels for 13%

profile of v1, /device:TPU:13, one launch (start us, length us, event | category | flops | bytes accessed | tf_op | source)
XLA Modules:
  0.0 186.2 jit_solution(13409595099605020512)
XLA Ops:
  0.0 1.4 dynamic_slice.22
  3.9 1.3 stack.89.info_ref
  5.2 1.3 collective-permute-start
  7.6 1.4 collective-permute-start.2
  9.0 2.0 %copy-done.3 = bf16[3,2,1024,288]{2,3,1,0:T(8,128)(2,1)S(1)} copy-done((bf16[3,2,1024,288]{2,3,1,0:T(8,128)(2,1)S(1)}, bf16[3,2,1024,288]{2,3,1,0:T(8,128)(2,1)}, u32[]{:S(2)}) %copy-start.3) | copy-done | bytes 3538968
  11.0 19.0 %spatial_attention.1 = bf16[4,576,512]{2,1,0:T(8,128)(2,1)} custom-call(s32[7]{0:T(128)S(1)} %stack.89.info_ref, bf16[3,2,288,1024]{3,2,1,0:T(8,128)(2,1)S(1)} %bitcast.44, bf16[2,288,1024]{2,1,0:T(8,128)(2,1)S(1)} %bitcast.45), custom_call_target="tpu_custom_call" | custom-call | flops 28000000000 | bytes 5000000 | tf_op jit(solution)/shard_map/spatial_attention/pallas_call | solution.py:116
  30.0 13.7 %collective-permute-done.1 = bf16[192,1152]{1,0:T(8,128)(2,1)S(1)} collective-permute-done((bf16[192,1152]{1,0:T(8,128)(2,1)S(1)}, bf16[192,1152]{1,0:T(8,128)(2,1)S(1)}, u32[]{:S(2)}, u32[]{:S(2)}) %collective-permute-start.1) | collective-permute-done | bytes 442400 | tf_op jit(solution)/shard_map/ppermute | solution.py:387
  43.8 2.8 %collective-permute-done.2 = bf16[192,1152]{1,0:T(8,128)(2,1)S(1)} collective-permute-done((bf16[192,1152]{1,0:T(8,128)(2,1)S(1)}, bf16[192,1152]{1,0:T(8,128)(2,1)S(1)}, u32[]{:S(2)}, u32[]{:S(2)}) %collective-permute-start.2) | collective-permute-done | bytes 442400 | tf_op jit(solution)/shard_map/ppermute | solution.py:387
  51.1 3.6 %all-to-all-start = ((bf16[4,576,512]{2,1,0:T(8,128)(2,1)}), bf16[4,576,512]{2,1,0:T(8,128)(2,1)S(1)}, u32[]{:S(2)}, u32[]{:S(2)}) async-start(bf16[4,576,512]{2,1,0:T(8,128)(2,1)} %spatial_attention.1), calls=%async_computation | async-start | bytes 4718592 | tf_op jit(solution)/shard_map/all_to_all | solution.py:415
  56.5 1.3 collective-permute-start.3
  57.8 2.2 %collective-permute-done.7 = bf16[4,48,1152]{2,1,0:T(8,128)(2,1)} collective-permute-done((bf16[4,48,1152]{2,1,0:T(8,128)(2,1)}, bf16[4,48,1152]{2,1,0:T(8,128)(2,1)}, u32[]{:S(2)}, u32[]{:S(2)}) %collective-permute-start.7) | collective-permute-done | bytes 442400 | tf_op jit(solution)/shard_map/ppermute | solution.py:393
  60.0 1.8 collective-permute-done.8
  61.8 7.6 %collective-permute-done.9 = bf16[4,48,1152]{2,1,0:T(8,128)(2,1)} collective-permute-done((bf16[4,48,1152]{2,1,0:T(8,128)(2,1)}, bf16[4,48,1152]{2,1,0:T(8,128)(2,1)}, u32[]{:S(2)}, u32[]{:S(2)}) %collective-permute-start.9) | collective-permute-done | bytes 442400 | tf_op jit(solution)/shard_map/ppermute | solution.py:393
  69.5 2.8 %pad_maximum_fusion.plane_ref = bf16[4,4,48,1152]{3,2,1,0:T(8,128)(2,1)} fusion(bf16[1,4,48,1152]{3,2,1,0:T(8,128)(2,1)} %bitcast.26, bf16[1,4,48,1152]{3,2,1,0:T(8,128)(2,1)} %bitcast.25, bf16[1,4,48,1152]{3,2,1,0:T(8,128)(2,1)} %bitcast.24, bf16[1,4,48,1152]{3,2,1,0:T(8,128)(2,1)S(1)} %copy-done.5), kind=kLoop, calls=%fused_computation | loop fusion | flops 2654208 | bytes 3538944 | tf_op jit(solution)/shard_map/stack | solution.py:418
  72.2 3.8 %collective-permute-start.10 = (bf16[4,4,48,1152]{3,2,1,0:T(8,128)(2,1)}, bf16[4,4,48,1152]{3,2,1,0:T(8,128)(2,1)}, u32[]{:S(2)}, u32[]{:S(2)}) collective-permute-start(bf16[4,4,48,1152]{3,2,1,0:T(8,128)(2,1)} %pad_maximum_fusion.plane_ref), channel_id=1, source_target_pairs={{0,4},{4,0},{1,5},{5,1},{2,6},{6,2},{3,7},{7,3},{8,12},{12,8},{9,1... | collective-permute-start | bytes 5308424 | tf_op jit(solution)/shard_map/ppermute | solution.py:393
  76.1 8.4 %collective-permute-done.5 = bf16[2,144,1152]{2,1,0:T(8,128)(2,1)S(1)} collective-permute-done((bf16[2,144,1152]{2,1,0:T(8,128)(2,1)S(1)}, bf16[2,144,1152]{2,1,0:T(8,128)(2,1)S(1)}, u32[]{:S(2)}, u32[]{:S(2)}) %collective-permute-start.5) | collective-permute-done | bytes 663584 | tf_op jit(solution)/shard_map/ppermute | solution.py:393
  88.4 2.2 %collective-permute-start.16 = (bf16[2,2,144,1152]{3,2,1,0:T(8,128)(2,1)}, bf16[2,2,144,1152]{3,2,1,0:T(8,128)(2,1)}, u32[]{:S(2)}, u32[]{:S(2)}) collective-permute-start(bf16[2,2,144,1152]{3,2,1,0:T(8,128)(2,1)} %pad_maximum_fusion.2.refs_6_), channel_id=1, source_target_pairs={{0,4},{4,0},{1,5},{5,1},{2,6},{6,2},{3,7},{7,3},{8,12},{12,8},{9,1... | collective-permute-start | bytes 3981320 | tf_op jit(solution)/shard_map/ppermute | solution.py:393
  90.7 13.1 %all-to-all-done.rows_ref = bf16[4,576,512]{2,1,0:T(8,128)(2,1)S(1)} async-done(((bf16[4,576,512]{2,1,0:T(8,128)(2,1)}), bf16[4,576,512]{2,1,0:T(8,128)(2,1)S(1)}, u32[]{:S(2)}, u32[]{:S(2)}) %all-to-all-start) | async-done | bytes 2359328 | tf_op jit(solution)/shard_map/all_to_all | solution.py:415
  104.8 5.6 %mix.1 = (bf16[1152,128]{1,0:T(8,128)(2,1)S(1)}, bf16[1152,128]{1,0:T(8,128)(2,1)S(1)}, bf16[1152,128]{1,0:T(8,128)(2,1)S(1)}, bf16[1152,128]{1,0:T(8,128)(2,1)S(1)}) custom-call(s32[7]{0:T(128)S(1)} %stack.89.info_ref, bf16[4,4,48,1152]{3,2,1,0:T(8,128)(2,1)} %pad_maximum_fusion.plane_ref, bf16[4,4,48,1152]{3,2,1,0:T(8,128)(2,1)} %collective-permute-done.10.core_ref, ...), custom_call_target="tpu_custom_call" | custom-call | flops 5000000000 | bytes 4000000 | tf_op jit(solution)/shard_map/mix/pallas_call | solution.py:170
  110.5 4.5 %collective-permute-done.6.refs_7_ = bf16[2,2,144,1152]{3,2,1,0:T(8,128)(2,1)} collective-permute-done((bf16[2,2,144,1152]{3,2,1,0:T(8,128)(2,1)}, bf16[2,2,144,1152]{3,2,1,0:T(8,128)(2,1)}, u32[]{:S(2)}, u32[]{:S(2)}) %collective-permute-start.6) | collective-permute-done | bytes 1327136 | tf_op jit(solution)/shard_map/ppermute | solution.py:393
  116.1 2.9 %collective-permute-start.15 = (bf16[2,2,144,1152]{3,2,1,0:T(8,128)(2,1)}, bf16[2,2,144,1152]{3,2,1,0:T(8,128)(2,1)S(1)}, u32[]{:S(2)}, u32[]{:S(2)}) collective-permute-start(bf16[2,2,144,1152]{3,2,1,0:T(8,128)(2,1)} %collective-permute-done.4.refs_5_), channel_id=1, source_target_pairs={{0,4},{4,0},{1,5},{5,1},{2,6},{6,2},{3,7},{7,3},{8,12},{12,8},{9,1... | collective-permute-start | bytes 3981320 | tf_op jit(solution)/shard_map/ppermute | solution.py:393
  119.0 1.6 collective-permute-start.11
  121.0 5.8 %collective-permute-done.11.refs_1_ = bf16[1152,128]{1,0:T(8,128)(2,1)S(1)} collective-permute-done((bf16[1152,128]{1,0:T(8,128)(2,1)S(1)}, bf16[1152,128]{1,0:T(8,128)(2,1)S(1)}, u32[]{:S(2)}, u32[]{:S(2)}) %collective-permute-start.11) | collective-permute-done | bytes 294944 | tf_op jit(solution)/shard_map/ppermute | solution.py:387
  126.9 7.0 %collective-permute-done.12.refs_2_ = bf16[1152,128]{1,0:T(8,128)(2,1)S(1)} collective-permute-done((bf16[1152,128]{1,0:T(8,128)(2,1)S(1)}, bf16[1152,128]{1,0:T(8,128)(2,1)S(1)}, u32[]{:S(2)}, u32[]{:S(2)}) %collective-permute-start.12) | collective-permute-done | bytes 294944 | tf_op jit(solution)/shard_map/ppermute | solution.py:387
  134.4 17.7 %temporal.1 = (bf16[288,512]{1,0:T(8,128)(2,1)S(1)}, bf16[288,512]{1,0:T(8,128)(2,1)S(1)}, bf16[288,512]{1,0:T(8,128)(2,1)S(1)}, bf16[288,512]{1,0:T(8,128)(2,1)S(1)}) custom-call(s32[7]{0:T(128)S(1)} %stack.89.info_ref, f32[1152,4]{1,0:T(8,128)S(1)} %bitcast.43, bf16[1152,128]{1,0:T(8,128)(2,1)S(1)} %get-tuple-element.39.refs_0_, ...), custom_call_target="tpu_custom_call" | custom-call | flops 20000000000 | bytes 12000000 | tf_op jit(solution)/shard_map/temporal/pallas_call | solution.py:293
  152.1 2.1 %collective-permute-start.18 = (bf16[288,512]{1,0:T(8,128)(2,1)S(1)}, bf16[288,512]{1,0:T(8,128)(2,1)S(1)}, u32[]{:S(2)}, u32[]{:S(2)}) collective-permute-start(bf16[288,512]{1,0:T(8,128)(2,1)S(1)} %get-tuple-element.47), channel_id=1, source_target_pairs={{0,0},{1,1},{2,18},{3,19},{16,2},{17,3},{18,16},{19,17},{4,4},{5,5... | collective-permute-start | bytes 884744 | tf_op jit(solution)/shard_map/ppermute | solution.py:433
  154.3 2.5 %collective-permute-start.20 = (bf16[288,512]{1,0:T(8,128)(2,1)S(1)}, bf16[288,512]{1,0:T(8,128)(2,1)S(1)}, u32[]{:S(2)}, u32[]{:S(2)}) collective-permute-start(bf16[288,512]{1,0:T(8,128)(2,1)S(1)} %get-tuple-element.49), channel_id=1, source_target_pairs={{0,2},{1,3},{2,16},{3,17},{16,0},{17,1},{18,18},{19,19},{4,6},{5,7... | collective-permute-start | bytes 884744 | tf_op jit(solution)/shard_map/ppermute | solution.py:433
  156.9 3.4 %collective-permute-start.21 = (bf16[288,512]{1,0:T(8,128)(2,1)S(1)}, bf16[288,512]{1,0:T(8,128)(2,1)S(1)}, u32[]{:S(2)}, u32[]{:S(2)}) collective-permute-start(bf16[288,512]{1,0:T(8,128)(2,1)S(1)} %get-tuple-element.50), channel_id=1, source_target_pairs={{0,3},{1,0},{2,17},{3,18},{16,1},{17,2},{18,19},{19,16},{4,7},{5,4... | collective-permute-start | bytes 884744 | tf_op jit(solution)/shard_map/ppermute | solution.py:433
  160.3 13.5 %collective-permute-done.18.refs_0_ = bf16[288,512]{1,0:T(8,128)(2,1)S(1)} collective-permute-done((bf16[288,512]{1,0:T(8,128)(2,1)S(1)}, bf16[288,512]{1,0:T(8,128)(2,1)S(1)}, u32[]{:S(2)}, u32[]{:S(2)}) %collective-permute-start.18) | collective-permute-done | bytes 294944 | tf_op jit(solution)/shard_map/ppermute | solution.py:433
  173.8 6.0 %collective-permute-done.19.refs_1_ = bf16[288,512]{1,0:T(8,128)(2,1)S(1)} collective-permute-done((bf16[288,512]{1,0:T(8,128)(2,1)S(1)}, bf16[288,512]{1,0:T(8,128)(2,1)S(1)}, u32[]{:S(2)}, u32[]{:S(2)}) %collective-permute-start.19) | collective-permute-done | bytes 294944 | tf_op jit(solution)/shard_map/ppermute | solution.py:433
  179.8 4.4 %collective-permute-done.21.refs_3_ = bf16[288,512]{1,0:T(8,128)(2,1)S(1)} collective-permute-done((bf16[288,512]{1,0:T(8,128)(2,1)S(1)}, bf16[288,512]{1,0:T(8,128)(2,1)S(1)}, u32[]{:S(2)}, u32[]{:S(2)}) %collective-permute-start.21) | collective-permute-done | bytes 294944 | tf_op jit(solution)/shard_map/ppermute | solution.py:433
  184.2 2.0 %place.1 = bf16[16,288,128]{2,1,0:T(8,128)(2,1)} custom-call(s32[7]{0:T(128)S(1)} %stack.89.info_ref, bf16[288,512]{1,0:T(8,128)(2,1)S(1)} %collective-permute-done.18.refs_0_, bf16[288,512]{1,0:T(8,128)(2,1)S(1)} %collective-permute-done.19.refs_1_, bf16[288,512]{1,0:T(8,128)(2,1)S(1)} %collective-permute-done.20.refs_2_, ...), custom_call_target="tpu_custom_call" | custom-call | tf_op jit(solution)/shard_map/place/pallas_call | solution.py:340
  (58 shorter events, 17.0 us)
Async XLA Ops:
  0.0 2.7 %copy-start = (bf16[288,1152]{1,0:T(8,128)(2,1)S(1)}, bf16[288,1152]{1,0:T(8,128)(2,1)}, u32[]{:S(2)}) copy-start(bf16[288,1152]{1,0:T(8,128)(2,1)} %param.10) | copy-start | bytes 1990660
  0.0 9.0 %copy-start.4 = (bf16[2,1024,288]{1,2,0:T(8,128)(2,1)S(1)}, bf16[2,1024,288]{1,2,0:T(8,128)(2,1)}, u32[]{:S(2)}) copy-start(bf16[2,1024,288]{1,2,0:T(8,128)(2,1)} %param.9) | copy-start | bytes 3538948
  5.2 24.8 %collective-permute-start = (bf16[192,1152]{1,0:T(8,128)(2,1)S(1)}, bf16[192,1152]{1,0:T(8,128)(2,1)S(1)}, u32[]{:S(2)}, u32[]{:S(2)}) collective-permute-start(bf16[192,1152]{1,0:T(8,128)(2,1)S(1)} %pad_maximum_fusion.5), channel_id=1, source_target_pairs={{0,1},{1,2},{2,3},{3,0},{4,5},{5,6},{6,7},{7,4},{8,9},{9,10},{10,1... | collective-permute-start | bytes 1327112 | tf_op jit(solution)/shard_map/ppermute | solution.py:387
  6.5 37.3 %collective-permute-start.1 = (bf16[192,1152]{1,0:T(8,128)(2,1)S(1)}, bf16[192,1152]{1,0:T(8,128)(2,1)S(1)}, u32[]{:S(2)}, u32[]{:S(2)}) collective-permute-start(bf16[192,1152]{1,0:T(8,128)(2,1)S(1)} %pad_maximum_fusion.5), channel_id=1, source_target_pairs={{0,2},{1,3},{2,0},{3,1},{4,6},{5,7},{6,4},{7,5},{8,10},{9,11},{10,... | collective-permute-start | bytes 1327112 | tf_op jit(solution)/shard_map/ppermute | solution.py:387
  7.6 39.0 %collective-permute-start.2 = (bf16[192,1152]{1,0:T(8,128)(2,1)S(1)}, bf16[192,1152]{1,0:T(8,128)(2,1)S(1)}, u32[]{:S(2)}, u32[]{:S(2)}) collective-permute-start(bf16[192,1152]{1,0:T(8,128)(2,1)S(1)} %pad_maximum_fusion.5), channel_id=1, source_target_pairs={{0,3},{1,0},{2,1},{3,2},{4,7},{5,4},{6,5},{7,6},{8,11},{9,8},{10,9... | collective-permute-start | bytes 1327112 | tf_op jit(solution)/shard_map/ppermute | solution.py:387
  9.0 2.0 %copy-start.3 = (bf16[3,2,1024,288]{2,3,1,0:T(8,128)(2,1)S(1)}, bf16[3,2,1024,288]{2,3,1,0:T(8,128)(2,1)}, u32[]{:S(2)}) copy-start(bf16[3,2,1024,288]{2,3,1,0:T(8,128)(2,1)} %param.8) | copy-start | bytes 10616836
  30.0 21.1 %copy-start.6 = (bf16[192,1152]{1,0:T(8,128)(2,1)}, bf16[192,1152]{1,0:T(8,128)(2,1)S(1)}, u32[]{:S(2)}) copy-start(bf16[192,1152]{1,0:T(8,128)(2,1)S(1)} %collective-permute-done) | copy-start | bytes 1327108
  43.8 7.3 %copy-start.8 = (bf16[192,1152]{1,0:T(8,128)(2,1)}, bf16[192,1152]{1,0:T(8,128)(2,1)S(1)}, u32[]{:S(2)}) copy-start(bf16[192,1152]{1,0:T(8,128)(2,1)S(1)} %collective-permute-done.1) | copy-start | bytes 1327108
  48.4 11.6 %collective-permute-start.7 = (bf16[4,48,1152]{2,1,0:T(8,128)(2,1)}, bf16[4,48,1152]{2,1,0:T(8,128)(2,1)}, u32[]{:S(2)}, u32[]{:S(2)}) collective-permute-start(bf16[4,48,1152]{2,1,0:T(8,128)(2,1)} %get-tuple-element.56), channel_id=1, source_target_pairs={{0,8},{8,0},{16,24},{24,16},{1,9},{9,1},{17,25},{25,17},{2,10},{10... | collective-permute-start | bytes 1327112 | tf_op jit(solution)/shard_map/ppermute | solution.py:393
  49.7 12.2 %collective-permute-start.8 = (bf16[4,48,1152]{2,1,0:T(8,128)(2,1)}, bf16[4,48,1152]{2,1,0:T(8,128)(2,1)}, u32[]{:S(2)}, u32[]{:S(2)}) collective-permute-start(bf16[4,48,1152]{2,1,0:T(8,128)(2,1)} %get-tuple-element.56), channel_id=1, source_target_pairs={{0,16},{8,24},{16,0},{24,8},{1,17},{9,25},{17,1},{25,9},{2,18},{10... | collective-permute-start | bytes 1327112 | tf_op jit(solution)/shard_map/ppermute | solution.py:393
  49.9 19.6 %collective-permute-start.9 = (bf16[4,48,1152]{2,1,0:T(8,128)(2,1)}, bf16[4,48,1152]{2,1,0:T(8,128)(2,1)}, u32[]{:S(2)}, u32[]{:S(2)}) collective-permute-start(bf16[4,48,1152]{2,1,0:T(8,128)(2,1)} %get-tuple-element.56), channel_id=1, source_target_pairs={{0,24},{8,16},{16,8},{24,0},{1,25},{9,17},{17,9},{25,1},{2,26},{10... | collective-permute-start | bytes 1327112 | tf_op jit(solution)/shard_map/ppermute | solution.py:393
  51.1 52.7 %all-to-all-start = ((bf16[4,576,512]{2,1,0:T(8,128)(2,1)}), bf16[4,576,512]{2,1,0:T(8,128)(2,1)S(1)}, u32[]{:S(2)}, u32[]{:S(2)}) async-start(bf16[4,576,512]{2,1,0:T(8,128)(2,1)} %spatial_attention.1), calls=%async_computation | async-start | bytes 4718592 | tf_op jit(solution)/shard_map/all_to_all | solution.py:415
  54.7 1.2 copy-start.7
  56.1 13.4 %copy-start.5 = (bf16[1,4,48,1152]{3,2,1,0:T(8,128)(2,1)S(1)}, bf16[1,4,48,1152]{3,2,1,0:T(8,128)(2,1)}, u32[]{:S(2)}) copy-start(bf16[1,4,48,1152]{3,2,1,0:T(8,128)(2,1)} %get-tuple-element.55) | copy-start | bytes 1327108
  56.1 28.4 %collective-permute-start.5 = (bf16[2,144,1152]{2,1,0:T(8,128)(2,1)S(1)}, bf16[2,144,1152]{2,1,0:T(8,128)(2,1)S(1)}, u32[]{:S(2)}, u32[]{:S(2)}) collective-permute-start(bf16[2,144,1152]{2,1,0:T(8,128)(2,1)S(1)} %get-tuple-element.52), channel_id=1, source_target_pairs={{0,16},{8,24},{16,0},{24,8},{1,17},{9,25},{17,1},{25,9},{2,18},{10... | collective-permute-start | bytes 1990664 | tf_op jit(solution)/shard_map/ppermute | solution.py:393
  56.5 29.4 %collective-permute-start.3 = (bf16[2,144,1152]{2,1,0:T(8,128)(2,1)S(1)}, bf16[2,144,1152]{2,1,0:T(8,128)(2,1)S(1)}, u32[]{:S(2)}, u32[]{:S(2)}) collective-permute-start(bf16[2,144,1152]{2,1,0:T(8,128)(2,1)S(1)} %get-tuple-element.54), channel_id=1, source_target_pairs={{0,8},{8,0},{16,24},{24,16},{1,9},{9,1},{17,25},{25,17},{2,10},{10... | collective-permute-start | bytes 1990664 | tf_op jit(solution)/shard_map/ppermute | solution.py:393
  72.2 18.4 %collective-permute-start.10 = (bf16[4,4,48,1152]{3,2,1,0:T(8,128)(2,1)}, bf16[4,4,48,1152]{3,2,1,0:T(8,128)(2,1)}, u32[]{:S(2)}, u32[]{:S(2)}) collective-permute-start(bf16[4,4,48,1152]{3,2,1,0:T(8,128)(2,1)} %pad_maximum_fusion.plane_ref), channel_id=1, source_target_pairs={{0,4},{4,0},{1,5},{5,1},{2,6},{6,2},{3,7},{7,3},{8,12},{12,8},{9,1... | collective-permute-start | bytes 5308424 | tf_op jit(solution)/shard_map/ppermute | solution.py:393
  85.7 29.3 %collective-permute-start.6 = (bf16[2,2,144,1152]{3,2,1,0:T(8,128)(2,1)}, bf16[2,2,144,1152]{3,2,1,0:T(8,128)(2,1)}, u32[]{:S(2)}, u32[]{:S(2)}) collective-permute-start(bf16[2,2,144,1152]{3,2,1,0:T(8,128)(2,1)} %pad_maximum_fusion.2.refs_6_), channel_id=1, source_target_pairs={{0,8},{8,0},{16,24},{24,16},{1,9},{9,1},{17,25},{25,17},{2,10},{10... | collective-permute-start | bytes 3981320 | tf_op jit(solution)/shard_map/ppermute | solution.py:393
  85.9 1.4 copy-start.10
  87.1 29.0 %collective-permute-start.4 = (bf16[2,2,144,1152]{3,2,1,0:T(8,128)(2,1)}, bf16[2,2,144,1152]{3,2,1,0:T(8,128)(2,1)}, u32[]{:S(2)}, u32[]{:S(2)}) collective-permute-start(bf16[2,2,144,1152]{3,2,1,0:T(8,128)(2,1)} %pad_maximum_fusion.1.refs_4_), channel_id=1, source_target_pairs={{0,16},{8,24},{16,0},{24,8},{1,17},{9,25},{17,1},{25,9},{2,18},{10... | collective-permute-start | bytes 3981320 | tf_op jit(solution)/shard_map/ppermute | solution.py:393
  88.4 32.2 %collective-permute-start.16 = (bf16[2,2,144,1152]{3,2,1,0:T(8,128)(2,1)}, bf16[2,2,144,1152]{3,2,1,0:T(8,128)(2,1)}, u32[]{:S(2)}, u32[]{:S(2)}) collective-permute-start(bf16[2,2,144,1152]{3,2,1,0:T(8,128)(2,1)} %pad_maximum_fusion.2.refs_6_), channel_id=1, source_target_pairs={{0,4},{4,0},{1,5},{5,1},{2,6},{6,2},{3,7},{7,3},{8,12},{12,8},{9,1... | collective-permute-start | bytes 3981320 | tf_op jit(solution)/shard_map/ppermute | solution.py:393
  90.7 30.2 %collective-permute-start.14 = (bf16[2,2,144,1152]{3,2,1,0:T(8,128)(2,1)}, bf16[2,2,144,1152]{3,2,1,0:T(8,128)(2,1)}, u32[]{:S(2)}, u32[]{:S(2)}) collective-permute-start(bf16[2,2,144,1152]{3,2,1,0:T(8,128)(2,1)} %pad_maximum_fusion.1.refs_4_), channel_id=1, source_target_pairs={{0,4},{4,0},{1,5},{5,1},{2,6},{6,2},{3,7},{7,3},{8,12},{12,8},{9,1... | collective-permute-start | bytes 3981320 | tf_op jit(solution)/shard_map/ppermute | solution.py:393
  104.8 29.6 %copy-start.2 = (f32[1,4,1152]{1,2,0:T(8,128)S(1)}, f32[1,4,1152]{1,2,0:T(8,128)}, u32[]{:S(2)}) copy-start(f32[1,4,1152]{1,2,0:T(8,128)} %copy.9) | copy-start | bytes 55300
  116.1 18.3 %collective-permute-start.15 = (bf16[2,2,144,1152]{3,2,1,0:T(8,128)(2,1)}, bf16[2,2,144,1152]{3,2,1,0:T(8,128)(2,1)S(1)}, u32[]{:S(2)}, u32[]{:S(2)}) collective-permute-start(bf16[2,2,144,1152]{3,2,1,0:T(8,128)(2,1)} %collective-permute-done.4.refs_5_), channel_id=1, source_target_pairs={{0,4},{4,0},{1,5},{5,1},{2,6},{6,2},{3,7},{7,3},{8,12},{12,8},{9,1... | collective-permute-start | bytes 3981320 | tf_op jit(solution)/shard_map/ppermute | solution.py:393
  119.0 15.5 %collective-permute-start.17 = (bf16[2,2,144,1152]{3,2,1,0:T(8,128)(2,1)}, bf16[2,2,144,1152]{3,2,1,0:T(8,128)(2,1)S(1)}, u32[]{:S(2)}, u32[]{:S(2)}) collective-permute-start(bf16[2,2,144,1152]{3,2,1,0:T(8,128)(2,1)} %collective-permute-done.6.refs_7_), channel_id=1, source_target_pairs={{0,4},{4,0},{1,5},{5,1},{2,6},{6,2},{3,7},{7,3},{8,12},{12,8},{9,1... | collective-permute-start | bytes 3981320 | tf_op jit(solution)/shard_map/ppermute | solution.py:393
  119.0 7.9 %collective-permute-start.11 = (bf16[1152,128]{1,0:T(8,128)(2,1)S(1)}, bf16[1152,128]{1,0:T(8,128)(2,1)S(1)}, u32[]{:S(2)}, u32[]{:S(2)}) collective-permute-start(bf16[1152,128]{1,0:T(8,128)(2,1)S(1)} %get-tuple-element.40), channel_id=1, source_target_pairs={{0,4},{4,8},{8,12},{12,0},{1,5},{5,9},{9,13},{13,1},{2,6},{6,10},{... | collective-permute-start | bytes 884744 | tf_op jit(solution)/shard_map/ppermute | solution.py:387
  120.6 13.3 %collective-permute-start.12 = (bf16[1152,128]{1,0:T(8,128)(2,1)S(1)}, bf16[1152,128]{1,0:T(8,128)(2,1)S(1)}, u32[]{:S(2)}, u32[]{:S(2)}) collective-permute-start(bf16[1152,128]{1,0:T(8,128)(2,1)S(1)} %get-tuple-element.41), channel_id=1, source_target_pairs={{0,8},{4,12},{8,0},{12,4},{1,9},{5,13},{9,1},{13,5},{2,10},{6,14},... | collective-permute-start | bytes 884744 | tf_op jit(solution)/shard_map/ppermute | solution.py:387
  120.9 13.6 %collective-permute-start.13 = (bf16[1152,128]{1,0:T(8,128)(2,1)S(1)}, bf16[1152,128]{1,0:T(8,128)(2,1)S(1)}, u32[]{:S(2)}, u32[]{:S(2)}) collective-permute-start(bf16[1152,128]{1,0:T(8,128)(2,1)S(1)} %get-tuple-element.42), channel_id=1, source_target_pairs={{0,12},{4,0},{8,4},{12,8},{1,13},{5,1},{9,5},{13,9},{2,14},{6,2},{... | collective-permute-start | bytes 884744 | tf_op jit(solution)/shard_map/ppermute | solution.py:387
  152.1 21.6 %collective-permute-start.18 = (bf16[288,512]{1,0:T(8,128)(2,1)S(1)}, bf16[288,512]{1,0:T(8,128)(2,1)S(1)}, u32[]{:S(2)}, u32[]{:S(2)}) collective-permute-start(bf16[288,512]{1,0:T(8,128)(2,1)S(1)} %get-tuple-element.47), channel_id=1, source_target_pairs={{0,0},{1,1},{2,18},{3,19},{16,2},{17,3},{18,16},{19,17},{4,4},{5,5... | collective-permute-start | bytes 884744 | tf_op jit(solution)/shard_map/ppermute | solution.py:433
  154.3 25.5 %collective-permute-start.19 = (bf16[288,512]{1,0:T(8,128)(2,1)S(1)}, bf16[288,512]{1,0:T(8,128)(2,1)S(1)}, u32[]{:S(2)}, u32[]{:S(2)}) collective-permute-start(bf16[288,512]{1,0:T(8,128)(2,1)S(1)} %get-tuple-element.48), channel_id=1, source_target_pairs={{0,1},{1,2},{2,19},{3,16},{16,3},{17,0},{18,17},{19,18},{4,5},{5,6... | collective-permute-start | bytes 884744 | tf_op jit(solution)/shard_map/ppermute | solution.py:433
  154.3 25.4 %collective-permute-start.20 = (bf16[288,512]{1,0:T(8,128)(2,1)S(1)}, bf16[288,512]{1,0:T(8,128)(2,1)S(1)}, u32[]{:S(2)}, u32[]{:S(2)}) collective-permute-start(bf16[288,512]{1,0:T(8,128)(2,1)S(1)} %get-tuple-element.49), channel_id=1, source_target_pairs={{0,2},{1,3},{2,16},{3,17},{16,0},{17,1},{18,18},{19,19},{4,6},{5,7... | collective-permute-start | bytes 884744 | tf_op jit(solution)/shard_map/ppermute | solution.py:433
  156.9 27.3 %collective-permute-start.21 = (bf16[288,512]{1,0:T(8,128)(2,1)S(1)}, bf16[288,512]{1,0:T(8,128)(2,1)S(1)}, u32[]{:S(2)}, u32[]{:S(2)}) collective-permute-start(bf16[288,512]{1,0:T(8,128)(2,1)S(1)} %get-tuple-element.50), channel_id=1, source_target_pairs={{0,3},{1,0},{2,17},{3,18},{16,1},{17,2},{18,19},{19,16},{4,7},{5,4... | collective-permute-start | bytes 884744 | tf_op jit(solution)/shard_map/ppermute | solution.py:433
  (2 other events, 1.8 us)

commit v2 on v0

v2 whole, which is shorter than its diff:
```python
import functools
import math

import jax
import jax.numpy as jnp
from jax import lax
from jax.experimental import pallas as pl
from jax.experimental.pallas import tpu as pltpu
from jax.sharding import Mesh
from jax.sharding import PartitionSpec as P

HEAD_DIM = 72
FRAMES = 8
PAIR = 2 * HEAD_DIM
KINDS = 3
SLICES = 8
EPS = 1e-6
F32 = jnp.float32
BF16 = jnp.bfloat16
MIB = 1024 * 1024


def flip(array):
    return jnp.swapaxes(array, 0, 1)


def tn(lhs, rhs):
    return lax.dot_general(lhs, rhs, (((0,), (0,)), ((), ())), preferred_element_type=F32)


def runs_of(chunk, rank, sizes):
    groups, ranks, heads, block, span, run = sizes
    starts = []
    for piece in range(span // run):
        place = chunk * span + piece * run
        starts.append((place // block * ranks + rank) * block + place % block)
    return starts


def arrange_kernel(sizes, qkv_ref, stream_ref, query_ref, key_ref, value_ref, rows_ref):
    groups, ranks, heads, block, span, run = sizes
    _, frames, width, tokens = qkv_ref.shape
    for each in range(heads):
        for frame in range(frames):
            pieces = [
                qkv_ref[0, frame, :, start:start + run]
                for rank in range(ranks) for start in runs_of(each, rank, sizes)
            ]
            gathered = jnp.concatenate(pieces, axis=1)
            for pair in range(width // PAIR):
                query_ref[each, frame, pair] = gathered[pair * PAIR:(pair + 1) * PAIR]
        pieces = [
            stream_ref[frame, :, start:start + run]
            for rank in range(ranks) for frame in range(frames) for start in runs_of(each, rank, sizes)
        ]
        rows_ref[each] = jnp.concatenate(pieces, axis=1)
    for frame in range(frames):
        for pair in range(width // PAIR):
            keys = qkv_ref[1, frame, pair * PAIR:(pair + 1) * PAIR, :]
            key_ref[frame, pair] = flip(keys.astype(F32)).astype(BF16)
            value_ref[frame, pair, :PAIR, :] = qkv_ref[2, frame, pair * PAIR:(pair + 1) * PAIR, :]
            value_ref[frame, pair, PAIR:, :] = jnp.ones((value_ref.shape[2] - PAIR, tokens), BF16)


def arrange(qkv, stream, sizes):
    heads = sizes[2]
    _, frames, width, tokens = qkv.shape
    shapes = [
        (heads, frames, width // PAIR, PAIR, tokens // heads),
        (frames, width // PAIR, tokens, PAIR),
        (frames, width // PAIR, PAIR + 16, tokens),
        (heads, width, frames * tokens // heads),
    ]
    vmem = pl.BlockSpec(memory_space=pltpu.VMEM)
    return pl.pallas_call(
        functools.partial(arrange_kernel, sizes),
        in_specs=[vmem] * 2,
        out_specs=[vmem] * len(shapes),
        out_shape=[jax.ShapeDtypeStruct(shape, BF16) for shape in shapes],
        compiler_params=pltpu.CompilerParams(vmem_limit_bytes=16 * MIB),
        cost_estimate=pl.CostEstimate(flops=6 * 10**9, bytes_accessed=5 * 10**6, transcendentals=0),
        name="arrange",
    )(qkv, stream)


def spatial_kernel(ranks, first, info_ref, query_ref, key_ref, value_ref, *refs):
    held_refs, out_ref, part_ref = refs[:-2], refs[-2], refs[-1]
    turn = pl.program_id(0)
    chunk = turn + first
    to = chunk if held_refs else turn
    _, frames, pairs, _, per_frame = query_ref.shape
    tokens = key_ref.shape[2]
    width = pairs * PAIR
    span = per_frame // ranks
    scale = math.log2(math.e) / math.sqrt(HEAD_DIM)
    count = info_ref[0]

    def attend(keys, masked):
        def of_pair(at, carry):
            frame, pair = at // pairs, at % pairs
            row = lax.broadcasted_iota(jnp.int32, (PAIR, per_frame), 0)
            queries = query_ref[chunk, frame, pair]
            for head in range(2):
                mine = (row >= head * HEAD_DIM) & (row < (head + 1) * HEAD_DIM)
                query = jnp.where(mine, queries, jnp.zeros((), BF16))
                scores = jnp.dot(key_ref[frame, pair, :keys, :], query, preferred_element_type=F32)
                if masked:
                    token = lax.broadcasted_iota(jnp.int32, (keys, per_frame), 0)
                    scores = jnp.where(token < count, scores, -jnp.inf)
                highest = jnp.max(scores, axis=0, keepdims=True)
                raised = jnp.exp2(scores * scale - highest * scale).astype(BF16)
                summed = jnp.dot(value_ref[frame, pair, :, :keys], raised, preferred_element_type=F32)
                inside = slice(head * HEAD_DIM, (head + 1) * HEAD_DIM)
                part_ref[frame, pair, inside, :] = summed[inside] / summed[PAIR:PAIR + 1]
            return carry

        lax.fori_loop(0, frames * pairs, of_pair, 0)

    half = tokens // 2

    @pl.when(count >= tokens)
    def whole():
        attend(tokens, False)

    @pl.when((count < tokens) & (count > half))
    def some():
        attend(tokens, True)

    @pl.when(count <= half)
    def few():
        attend(half, True)

    for pair in range(pairs):
        pieces = [
            part_ref[frame, pair, :, rank * span:(rank + 1) * span] for rank in range(ranks) for frame in range(frames)
        ]
        out_ref[to, pair * PAIR:(pair + 1) * PAIR, :] = jnp.concatenate(pieces, axis=1).astype(BF16)
    if held_refs:
        @pl.when(turn == 0)
        def join():
            out_ref[:first, :width, :] = held_refs[0][...]
            out_ref[:, width:, :] = held_refs[1][...]


def spatial_attention(info, queries, keys, values, ranks, first, count, *held):
    heads, frames, pairs, _, per_frame = queries.shape
    shape = (heads, 2 * pairs * PAIR, frames * per_frame) if held else (count, pairs * PAIR, frames * per_frame)
    vmem = pl.BlockSpec(memory_space=pltpu.VMEM)
    return pl.pallas_call(
        functools.partial(spatial_kernel, ranks, first),
        grid_spec=pltpu.PrefetchScalarGridSpec(
            num_scalar_prefetch=1,
            grid=(count,),
            in_specs=[vmem] * (3 + len(held)),
            out_specs=vmem,
            scratch_shapes=[pltpu.VMEM((frames, pairs, PAIR, per_frame), F32)],
        ),
        out_shape=jax.ShapeDtypeStruct(shape, BF16),
        compiler_params=pltpu.CompilerParams(vmem_limit_bytes=16 * MIB),
        cost_estimate=pl.CostEstimate(flops=14 * 10**9, bytes_accessed=5 * 10**6, transcendentals=4 * 10**6),
        name="spatial_attention",
    )(info, queries, keys, values, *held)


def strips_kernel(heads, info_ref, plane_ref, core_ref, out_ref):
    me, core, member = info_ref[4], info_ref[5], info_ref[6]
    members, _, strip, _ = plane_ref.shape
    width = out_ref.shape[0] // heads
    half = width // 2
    last = half // strip - 1
    for far, ref in enumerate((plane_ref, core_ref)):
        for other in range(members):
            whose = jnp.minimum(member ^ other, last)
            for step in range(heads):
                source = lax.rem(me - step + heads, heads)
                start = source * width + (core ^ far) * half + whose * strip
                out_ref[pl.ds(pl.multiple_of(start, 16), strip), :] = ref[other, step]


def strips_in_place(info, by_plane, by_core, width):
    heads, features = by_plane.shape[1], by_plane.shape[3]
    vmem = pl.BlockSpec(memory_space=pltpu.VMEM)
    return pl.pallas_call(
        functools.partial(strips_kernel, heads),
        in_specs=[pl.BlockSpec(memory_space=pltpu.SMEM)] + [vmem] * 2,
        out_specs=vmem,
        out_shape=jax.ShapeDtypeStruct((heads * width, features), BF16),
        compiler_params=pltpu.CompilerParams(vmem_limit_bytes=12 * MIB),
        cost_estimate=pl.CostEstimate(flops=2 * 10**9, bytes_accessed=5 * 10**6, transcendentals=0),
        name="strips_in_place",
    )(info, by_plane, by_core)


def mix_kernel(heads, ranks, info_ref, weight_ref, gate_ref, rows_ref, *refs):
    out_refs, mixed_ref = refs[:-1], refs[-1]
    rank = info_ref[3]
    width = rows_ref.shape[1] // 2
    summed = None
    for source in range(heads):
        term = tn(weight_ref[source * width:(source + 1) * width, :], rows_ref[source, :width, :])
        summed = term if summed is None else summed + term
    for source in range(heads):
        here = slice(source * width, (source + 1) * width)
        mixed = rows_ref[source, width:, :].astype(F32) + gate_ref[here, 0:1] * summed[here]
        mixed_ref[here, :] = mixed.astype(BF16)
    lanes = mixed_ref.shape[1] // ranks
    for step in range(ranks):
        to = lax.rem(rank + step, ranks)
        out_refs[step][...] = mixed_ref[:, pl.ds(pl.multiple_of(to * lanes, lanes), lanes)]


def mix(info, weight, arrived, columns, ranks):
    heads, width, rows = arrived.shape
    features = weight.shape[1]
    vmem = pl.BlockSpec(memory_space=pltpu.VMEM)
    return pl.pallas_call(
        functools.partial(mix_kernel, heads, ranks),
        in_specs=[pl.BlockSpec(memory_space=pltpu.SMEM)] + [vmem] * 3,
        out_specs=[vmem] * ranks,
        out_shape=[jax.ShapeDtypeStruct((features, rows // ranks), BF16)] * ranks,
        scratch_shapes=[pltpu.VMEM((features, rows), BF16)],
        compiler_params=pltpu.CompilerParams(vmem_limit_bytes=20 * MIB),
        cost_estimate=pl.CostEstimate(flops=4 * 10**9, bytes_accessed=4 * 10**6, transcendentals=0),
        name="mix",
    )(info, weight, columns, arrived)


def frame_at(place, rank, sizes):
    ranks = sizes[1]
    frames = FRAMES // ranks
    return lax.rem(rank - place // frames + ranks, ranks) * frames + place % frames


def pieces_kernel(info_ref, *refs):
    piece_refs, qkv_ref, out_ref = refs[:-2], refs[-2], refs[-1]
    member = info_ref[6]
    for group in range(len(piece_refs) // 2):
        for other in range(KINDS + 1):
            kind = member ^ other
            at = (other // 2, other % 2) if group % 2 == 0 else (other % 2, other // 2)
            ref = piece_refs[2 * group + at[0]]

            @pl.when(kind < KINDS)
            def projection():
                for head in range(2):
                    qkv_ref[2 * group + head, pl.ds(pl.multiple_of(kind * PAIR, 16), PAIR), :] = ref[at[1], head]

            @pl.when(kind == KINDS)
            def output():
                for head in range(2):
                    start = (2 * group + head) * PAIR
                    out_ref[start:start + PAIR, :] = ref[at[1], head]


def pieces_in_place(info, pieces):
    features = pieces[0].shape[3]
    count = features // PAIR
    vmem = pl.BlockSpec(memory_space=pltpu.VMEM)
    return pl.pallas_call(
        pieces_kernel,
        in_specs=[pl.BlockSpec(memory_space=pltpu.SMEM)] + [vmem] * len(pieces),
        out_specs=[vmem] * 2,
        out_shape=[
            jax.ShapeDtypeStruct((count, KINDS * PAIR, features), BF16),
            jax.ShapeDtypeStruct((features, features), BF16),
        ],
        compiler_params=pltpu.CompilerParams(vmem_limit_bytes=28 * MIB),
        cost_estimate=pl.CostEstimate(flops=3 * 10**9, bytes_accessed=20 * 10**6, transcendentals=0),
        name="pieces_in_place",
    )(info, *pieces)


def turned(array, span):
    lanes = array.shape[1]
    if 2 * span % 128 or span % 128 == 0:
        return [array if d == 0 else pltpu.roll(array, d * span, 1) for d in range(FRAMES)]
    odd = pltpu.roll(array, span, 1)
    found = []
    for d in range(FRAMES):
        base, shift = (odd, (d - 1) * span) if d % 2 else (array, d * span)
        whole = jnp.concatenate([base[:, lanes - shift:], base[:, :lanes - shift]], axis=1) if shift else base
        found.append(whole)
    return found


def temporal_kernel(sizes, info_ref, cols_ref, qkv_ref, last_ref, *refs):
    groups, ranks, heads, block, span, run = sizes
    mixed_refs, out_refs = refs[:ranks], refs[ranks:-3]
    normed_ref, attended_ref, result_ref = refs[-3:]
    step = pl.program_id(0)
    features, lanes = mixed_refs[0].shape
    rows = ranks * lanes
    scale = 1.0 / math.sqrt(HEAD_DIM)
    frame_count = info_ref[1]
    rank_here = info_ref[3]
    each_step = qkv_ref.shape[0] // pl.num_programs(0)

    @pl.when(step == 0)
    def norm():
        for rank in range(ranks):
            full = mixed_refs[rank][...].astype(F32)
            center = full - jnp.mean(full, axis=0, keepdims=True)
            variance = jnp.mean(center * center, axis=0, keepdims=True)
            normed = center * lax.rsqrt(variance + EPS)
            normed = normed * (1.0 + cols_ref[:, 2:3]) + cols_ref[:, 1:2]
            normed_ref[:, rank * lanes:(rank + 1) * lanes] = normed.astype(BF16)

    frame = lax.broadcasted_iota(jnp.int32, (FRAMES, rows), 1) // span
    delta = lax.broadcasted_iota(jnp.int32, (FRAMES, rows), 0)
    key_frame = frame_at(lax.rem(frame - delta + FRAMES, FRAMES), rank_here, sizes)
    live = key_frame < frame_count
    all_projected = [
        jnp.dot(qkv_ref[step * each_step + which], normed_ref[...], preferred_element_type=F32)
        for which in range(each_step)
    ]
    for which, projected in enumerate(all_projected):
        attended = []
        for head in range(2):
            query = projected[head * HEAD_DIM:(head + 1) * HEAD_DIM]
            key = projected[PAIR + head * HEAD_DIM:PAIR + (head + 1) * HEAD_DIM]
            value = projected[2 * PAIR + head * HEAD_DIM:2 * PAIR + (head + 1) * HEAD_DIM]
            scores = [jnp.sum(query * each, axis=0, keepdims=True) for each in turned(key, span)]
            scores = jnp.concatenate(scores, axis=0) * scale
            scores = jnp.where(live, scores, -jnp.inf)
            raised = jnp.exp(scores - jnp.max(scores, axis=0, keepdims=True))
            shares = raised / jnp.sum(raised, axis=0, keepdims=True)
            summed = None
            for d, each in enumerate(turned(value, span)):
                term = shares[d:d + 1] * each
                summed = term if summed is None else summed + term
            attended.append(summed)
        here = pl.ds(pl.multiple_of((step * each_step + which) * PAIR, PAIR), PAIR)
        attended_ref[here, :] = jnp.concatenate(attended, axis=0).astype(BF16)

    @pl.when(step == pl.num_programs(0) - 1)
    def finish():
        width = features // heads
        clip, me, count = info_ref[2], info_ref[4], info_ref[0]
        total = tn(last_ref[...], attended_ref[...])
        for rank in range(ranks):
            lane = slice(rank * lanes, (rank + 1) * lanes)
            full = mixed_refs[rank][...].astype(F32) + cols_ref[:, 3:4] * total[:, lane]
            place = lax.broadcasted_iota(jnp.int32, (1, lanes), 1) + rank * lanes
            among = me * span + place % span
            token = (among // block * ranks + rank_here) * block + among % block
            valid = (frame_at(place // span, rank_here, sizes) < frame_count) & (token < count)
            result_ref[:, lane] = jnp.where(valid, full, 0.0).astype(BF16)
        parts = span // run
        share = max(heads // groups, 1)
        for part in range(parts):
            slot = lax.rem(part + parts - lax.rem(clip, parts), parts)
            turn = clip * share if parts == 1 else clip // parts
            for step_to in range(heads):
                to = lax.rem(me * (parts == 1) + step_to + turn, heads)
                rows_to = pl.ds(pl.multiple_of(to * width, width), width)

                def pick():
                    if parts == 1:
                        return result_ref[rows_to, :]
                    found = result_ref[rows_to, :]
                    return jnp.concatenate(
                        [found[:, f * span + part * run:f * span + (part + 1) * run] for f in range(FRAMES)], axis=1
                    )

                for each in range(parts):
                    @pl.when(slot == each)
                    def store():
                        out_refs[each * heads + step_to][...] = pick()


def temporal(info, mixed, columns, weights, sizes):
    groups, ranks, heads, block, span, run = sizes
    features, lanes = mixed[0].shape
    rows = ranks * lanes
    count = heads * (span // run)
    shape = (features // heads, FRAMES * run)
    vmem = pl.BlockSpec(memory_space=pltpu.VMEM)
    return pl.pallas_call(
        functools.partial(temporal_kernel, sizes),
        grid_spec=pltpu.PrefetchScalarGridSpec(
            num_scalar_prefetch=1,
            grid=(heads,),
            in_specs=[vmem] * (3 + ranks),
            out_specs=[vmem] * count,
            scratch_shapes=[pltpu.VMEM((features, rows), BF16)] * 3,
        ),
        out_shape=[jax.ShapeDtypeStruct(shape, BF16)] * count,
        compiler_params=pltpu.CompilerParams(vmem_limit_bytes=20 * MIB),
        cost_estimate=pl.CostEstimate(flops=18 * 10**9, bytes_accessed=12 * 10**6, transcendentals=0),
        name="temporal",
    )(info, columns, *weights, *mixed)


def place_kernel(sizes, info_ref, *refs):
    groups, ranks, heads, block, span, run = sizes
    parts = span // run
    share = block // run
    piece_refs, out_ref, held_ref = refs[:-2], refs[-2], refs[-1]
    clip, rank, me = info_ref[2], info_ref[3], info_ref[4]
    for part in range(parts):
        for step in range(heads):
            if parts == 1:
                source = lax.rem(me - step + heads + groups * heads - clip * share, heads)
            else:
                source = lax.rem(me - step + heads, heads) * parts + lax.rem(clip - part + parts, parts)
            held_ref[source] = piece_refs[part * heads + step][...]
    for group in range(groups):
        for at in range(FRAMES):
            pieces = [held_ref[group * share + e, :, at * run:(at + 1) * run] for e in range(share)]
            out_ref[group * FRAMES + frame_at(at, rank, sizes)] = jnp.concatenate(pieces, axis=1) if share > 1 else pieces[0]


def place(info, pieces, sizes):
    groups, ranks, heads, block, span, run = sizes
    width, lanes = pieces[0].shape
    vmem = pl.BlockSpec(memory_space=pltpu.VMEM)
    return pl.pallas_call(
        functools.partial(place_kernel, sizes),
        in_specs=[pl.BlockSpec(memory_space=pltpu.SMEM)] + [vmem] * len(pieces),
        out_specs=vmem,
        out_shape=jax.ShapeDtypeStruct((groups * FRAMES, width, block), BF16),
        scratch_shapes=[pltpu.VMEM((len(pieces), width, lanes), BF16)],
        compiler_params=pltpu.CompilerParams(vmem_limit_bytes=12 * MIB),
        name="place",
    )(info, *pieces)


def routes(step, part, sizes):
    groups, ranks, heads, block, span, run = sizes
    parts = span // run
    share = block // run
    pairs = []
    for clip in range(groups):
        for head in range(heads):
            if parts == 1:
                to = (head // share, (head + step + clip * share) % heads)
            else:
                to = (head * parts + (part + clip) % parts, (step + clip // parts) % heads)
            pairs.append((clip * heads + head, to[0] * heads + to[1]))
    return pairs


def on_device(
    shape, spatial_qkv, stream, out_spatial, qkv_temporal, out_temporal, modulation, tok_count, frame_count
):
    outer, clips_inner, rank_hi, cores, heads = shape
    groups = outer * clips_inner
    ranks = rank_hi * cores
    assert cores == 2 and clips_inner * rank_hi == KINDS + 1
    clip = lax.axis_index(("outer", "clip"))
    rank = lax.axis_index(("rank", "core"))
    core = lax.axis_index("core")
    head = lax.axis_index("head")
    member = lax.axis_index(("clip", "rank"))
    width = spatial_qkv.shape[3]
    features = out_spatial.shape[1]
    frames, tokens = stream.shape[:2]
    block = tokens // (groups * ranks)
    span = tokens // (ranks * heads)
    run = min(block, span)
    sizes = (groups, ranks, heads, block, span, run)

    def send(array, axis, size, step):
        return lax.ppermute(array, axis, [(i, (i + step) % size) for i in range(size)])

    def around(arrays, axis, size):
        return [arrays[0]] + [send(arrays[k], axis, size, k) for k in range(1, size)]

    def swap(array, axis, size, bit):
        return lax.ppermute(array, axis, [(i, i ^ bit) for i in range(size)])

    info = jnp.stack([tok_count[clip], frame_count[clip], clip, rank, head, core, member]).astype(jnp.int32)
    here = lax.dynamic_index_in_dim(modulation, clip, 0, keepdims=False)
    columns = here.T

    plane = clips_inner * rank_hi
    turned = jnp.swapaxes(qkv_temporal, 1, 2)
    weight = lax.dynamic_slice(turned, (jnp.minimum(member, KINDS - 1), core * PAIR, 0), (1, PAIR, features))[0]
    other = lax.dynamic_slice(out_temporal, (core * PAIR, 0), (PAIR, features))
    weight = jnp.where(member < KINDS, weight, other)
    half = width // cores
    strip = half // KINDS
    spatial = lax.dynamic_slice(
        out_spatial, (core * half + jnp.minimum(member, KINDS - 1) * strip, 0), (strip, features)
    )
    spatial, info, weight = lax.optimization_barrier((spatial, info, weight))

    mine = around([weight] * heads, "head", heads)
    *arranged, rows = arrange(jnp.swapaxes(spatial_qkv, 2, 3), jnp.swapaxes(stream, 1, 2), sizes)
    early = spatial_attention(info, *arranged, ranks, 0, heads - 1)
    mine, early, spatial = lax.optimization_barrier((mine, early, spatial))

    first = [jnp.stack(pair) for pair in (mine[:2], mine[2:])]
    second = [swap(part, ("clip", "rank"), plane, bit) for part, bit in zip(first, (1, 2))]
    strips = around([spatial] * heads, "head", heads)
    first, info = lax.optimization_barrier((first, info))
    attended = spatial_attention(info, *arranged, ranks, heads - 1, 1, early, rows)
    first, second, strips, attended = lax.optimization_barrier((first, second, strips, attended))

    arrived = lax.all_to_all(attended, "head", 0, 0)
    pieces = []
    for near, far, bit in zip(first, second, (2, 1)):
        part = jnp.stack([near, far])
        pieces += [part, swap(part, ("clip", "rank"), plane, bit)]
    same = jnp.stack(strips)
    by_plane = jnp.stack([same] + [swap(same, ("clip", "rank"), plane, bit) for bit in range(1, plane)])
    strips = strips_in_place(info, by_plane, swap(by_plane, "core", cores, 1), width)
    pieces += [swap(each, "core", cores, 1) for each in pieces]
    arrived, strips = lax.optimization_barrier((arrived, strips))
    mixed = mix(info, strips, arrived, columns, ranks)
    mixed = around(mixed, ("rank", "core"), ranks)
    result = temporal(info, mixed, columns, pieces_in_place(info, pieces), sizes)
    arrived = [
        lax.ppermute(result[part * heads + step], ("outer", "clip", "head"), routes(step, part, sizes))
        for part in range(span // run) for step in range(heads)
    ]
    return jnp.swapaxes(place(info, arrived, sizes), 1, 2)


def solution(mesh):
    seq, heads = mesh.shape["seq"], mesh.shape["head"]

    def whole(spatial_qkv, stream, *rest):
        frames = spatial_qkv.shape[1] // seq
        ranks = FRAMES // frames
        clips_inner = SLICES // ranks
        shape = (seq // SLICES, clips_inner, ranks // 2, 2, heads)
        fine = Mesh(mesh.devices.reshape(shape), ("outer", "clip", "rank", "core", "head"))
        split = ("outer", "clip", "rank", "core")
        in_specs = (
            P(None, split, None, "head"),
            P(split, None, "head"),
            P("head", None),
            P(None, None, "head"),
            P("head", None),
            P(),
            P(),
            P(),
        )
        return jax.shard_map(
            functools.partial(on_device, shape), mesh=fine, in_specs=in_specs, out_specs=P(None, split, "head"),
            check_vma=False,
        )(spatial_qkv, stream, *rest)

    return whole
```

time: 209 us -> 183 us (0.88)
  waiting for transfers between devices: 99.2 us -> 71.3 us
  between operations: 13.5 us -> 0.22 us
  starting transfers between devices: 25.5 us -> 35.4 us
  other arithmetic: 4.03 us -> 6.41 us
  Pallas kernels: 54 us -> 56.1 us
    ppermute x6 -> x9, waiting for transfers between devices: 32.6 us -> 12.4 us  [send(): lax.ppermute(array, axis, [(i, (i + step) % size) for i in range(size)])]
    ppermute x4 -> x12, starting transfers between devices: 4.78 us -> 15.4 us  [swap(): return lax.ppermute(array, axis, [(i, i ^ bit) for i in range(size)])]
    pallas_call x1 -> x5, Pallas kernels: 29.3 us -> 38.5 us  [the longest x2 29.9 us: spatial_attention(): pl.pallas_call(functools.partial(spatial_kernel, ranks, first), grid_spec...]
    all_to_all x1, waiting for transfers between devices: 6.42 us -> 0.01 us  [on_device(): arrived = lax.all_to_all(attended, 'head', 0, 0)]
    pallas_call x1, Pallas kernels: 17.1 us -> 11.8 us  [temporal(): pl.pallas_call(functools.partial(temporal_kernel, sizes), grid_spec=pltpu...]
    unnamed x26 -> x28, local copies, waits for them, and re-layouts: 3.81 us -> 8.44 us
    another operation x4 -> x0, local copies, waits for them, and re-layouts: 3 us -> none  [the longest x2 1.9 us: on_device(): same = jnp.stack([each[PAIR:] for each in mine])]
    another operation x3 -> x6, other arithmetic: 2.83 us -> 5.24 us  [the longest x2 3.54 us: on_device(): part = jnp.stack([near, far])]
  transfers between devices with their start and end apart: 16 -> 26, of which waited for: 14 -> 13; matrix products, arithmetic and copies ran while one was open for 2% -> 3% of each run, Pallas kernels for 17% -> 23%
where the time goes in v2:
time: 183 us
  waiting for transfers between devices  71.3 us (39%)
  Pallas kernels  56.1 us (31%)
  starting transfers between devices  35.4 us (19%)
  local copies, waits for them, and re-layouts  13.4 us (7%)
  other arithmetic  6.41 us (4%)
    ppermute x12, waiting for transfers between devices, swap(): return lax.ppermute(array, axis, [(i, i ^ bit) for i in range(size)])  35.6 us
    pallas_call x2, Pallas kernels, spatial_attention(): pl.pallas_call(functools.partial(spatial_kernel, ranks, first), grid_spec...  29.9 us
    ppermute x4, waiting for transfers between devices, on_device(): lax.ppermute(result[part * heads + step], ('outer', 'clip', 'head'), rout...  23.4 us
    ppermute x12, starting transfers between devices, swap(): return lax.ppermute(array, axis, [(i, i ^ bit) for i in range(size)])  15.4 us
    ppermute x9, waiting for transfers between devices, send(): lax.ppermute(array, axis, [(i, (i + step) % size) for i in range(size)])  12.4 us
    pallas_call x1, Pallas kernels, temporal(): pl.pallas_call(functools.partial(temporal_kernel, sizes), grid_spec=pltpu...  11.8 us
    ppermute x4, starting transfers between devices, on_device(): lax.ppermute(result[part * heads + step], ('outer', 'clip', 'head'), rout...  9.33 us
    unnamed x28, local copies, waits for them, and re-layouts  8.44 us
  transfers between devices with their start and end apart: 26, of which 13 were waited for; matrix products, arithmetic and copies ran while one was open for 3% of the time, Pallas kernels for 23%

profile of v2, /device:TPU:13, one launch (start us, length us, event | category | flops | bytes accessed | tf_op | source)
XLA Modules:
  0.0 182.9 jit_solution(5671637735951561026)
XLA Ops:
  0.0 1.4 dynamic_slice.20
  3.8 1.3 stack.89.info_ref
  7.4 1.4 collective-permute-start.2
  8.8 2.0 %copy-done.3 = bf16[3,2,1024,288]{2,3,1,0:T(8,128)(2,1)S(1)} copy-done((bf16[3,2,1024,288]{2,3,1,0:T(8,128)(2,1)S(1)}, bf16[3,2,1024,288]{2,3,1,0:T(8,128)(2,1)}, u32[]{:S(2)}) %copy-start.3) | copy-done | bytes 3538968
  12.1 1.3 arrange.1
  13.4 21.0 %spatial_attention.2.refs_0_ = bf16[3,288,512]{2,1,0:T(8,128)(2,1)S(1)} custom-call(s32[7]{0:T(128)S(1)} %stack.89.info_ref, bf16[4,2,2,144,256]{4,3,2,1,0:T(8,128)(2,1)S(1)} %get-tuple-element.44.query_ref, bf16[2,2,1024,144]{3,2,1,0:T(8,128)(2,1)S(1)} %get-tuple-element.45.key_ref, bf16[2,2,160,1024]{3,2,1,0:T(8,128)(2,1)S(1)} %get-tuple-element.46.value_ref), custom_call_target="tpu_custom_call" | custom-call | flops 14000000000 | bytes 5000000 | tf_op jit(solution)/shard_map/spatial_attention/pallas_call | solution.py:149
  34.5 2.5 %collective-permute-done.2 = bf16[144,1152]{1,0:T(8,128)(2,1)S(1)} collective-permute-done((bf16[144,1152]{1,0:T(8,128)(2,1)S(1)}, bf16[144,1152]{1,0:T(8,128)(2,1)S(1)}, u32[]{:S(2)}, u32[]{:S(2)}) %collective-permute-start.2) | collective-permute-done | bytes 331808 | tf_op jit(solution)/shard_map/ppermute | solution.py:464
  40.5 8.9 %spatial_attention.3 = bf16[4,576,512]{2,1,0:T(8,128)(2,1)} custom-call(s32[7]{0:T(128)S(1)} %stack.89.info_ref, bf16[4,2,2,144,256]{4,3,2,1,0:T(8,128)(2,1)S(1)} %get-tuple-element.44.query_ref, bf16[2,2,1024,144]{3,2,1,0:T(8,128)(2,1)S(1)} %get-tuple-element.45.key_ref, bf16[2,2,160,1024]{3,2,1,0:T(8,128)(2,1)S(1)} %get-tuple-element.46.value_ref, ...), custom_call_target="tpu_custom_call" | custom-call | flops 14000000000 | bytes 5000000 | tf_op jit(solution)/shard_map/spatial_attention/pallas_call | solution.py:149
  50.7 2.6 %collective-permute-done.4 = bf16[2,144,1152]{2,1,0:T(8,128)(2,1)S(1)} collective-permute-done((bf16[2,144,1152]{2,1,0:T(8,128)(2,1)S(1)}, bf16[2,144,1152]{2,1,0:T(8,128)(2,1)S(1)}, u32[]{:S(2)}, u32[]{:S(2)}) %collective-permute-start.4) | collective-permute-done | bytes 663584 | tf_op jit(solution)/shard_map/ppermute | solution.py:470
  54.1 3.8 %all-to-all-start = ((bf16[4,576,512]{2,1,0:T(8,128)(2,1)}), bf16[4,576,512]{2,1,0:T(8,128)(2,1)S(1)}, u32[]{:S(2)}, u32[]{:S(2)}) async-start(bf16[4,576,512]{2,1,0:T(8,128)(2,1)} %spatial_attention.3), calls=%async_computation | async-start | bytes 4718592 | tf_op jit(solution)/shard_map/all_to_all | solution.py:500
  63.2 2.3 %pad_maximum_fusion.1.refs_0_ = bf16[2,2,144,1152]{3,2,1,0:T(8,128)(2,1)} fusion(bf16[1,2,144,1152]{3,2,1,0:T(8,128)(2,1)} %bitcast.16, bf16[1,2,144,1152]{3,2,1,0:T(8,128)(2,1)S(1)} %bitcast.37), kind=kLoop, calls=%fused_computation.1 | loop fusion | flops 663552 | bytes 2654208 | tf_op jit(solution)/shard_map/stack | solution.py:503
  65.9 2.6 %collective-permute-done.14 = bf16[4,48,1152]{2,1,0:T(8,128)(2,1)S(1)} collective-permute-done((bf16[4,48,1152]{2,1,0:T(8,128)(2,1)S(1)}, bf16[4,48,1152]{2,1,0:T(8,128)(2,1)S(1)}, u32[]{:S(2)}, u32[]{:S(2)}) %collective-permute-start.14) | collective-permute-done | bytes 442400 | tf_op jit(solution)/shard_map/ppermute | solution.py:470
  68.5 2.1 %collective-permute-done.15 = bf16[4,48,1152]{2,1,0:T(8,128)(2,1)S(1)} collective-permute-done((bf16[4,48,1152]{2,1,0:T(8,128)(2,1)S(1)}, bf16[4,48,1152]{2,1,0:T(8,128)(2,1)S(1)}, u32[]{:S(2)}, u32[]{:S(2)}) %collective-permute-start.15) | collective-permute-done | bytes 442400 | tf_op jit(solution)/shard_map/ppermute | solution.py:470
  70.6 7.1 %collective-permute-done.16 = bf16[4,48,1152]{2,1,0:T(8,128)(2,1)S(1)} collective-permute-done((bf16[4,48,1152]{2,1,0:T(8,128)(2,1)S(1)}, bf16[4,48,1152]{2,1,0:T(8,128)(2,1)S(1)}, u32[]{:S(2)}, u32[]{:S(2)}) %collective-permute-start.16) | collective-permute-done | bytes 442400 | tf_op jit(solution)/shard_map/ppermute | solution.py:470
  77.8 1.5 pad_maximum_fusion.plane_ref
  79.2 5.6 %collective-permute-start.17 = (bf16[4,4,48,1152]{3,2,1,0:T(8,128)(2,1)}, bf16[4,4,48,1152]{3,2,1,0:T(8,128)(2,1)}, u32[]{:S(2)}, u32[]{:S(2)}) collective-permute-start(bf16[4,4,48,1152]{3,2,1,0:T(8,128)(2,1)} %pad_maximum_fusion.plane_ref), channel_id=1, source_target_pairs={{0,4},{4,0},{1,5},{5,1},{2,6},{6,2},{3,7},{7,3},{8,12},{12,8},{9,1... | collective-permute-start | bytes 5308424 | tf_op jit(solution)/shard_map/ppermute | solution.py:470
  85.4 21.2 %collective-permute-done.9.refs_3_ = bf16[2,2,144,1152]{3,2,1,0:T(8,128)(2,1)} collective-permute-done((bf16[2,2,144,1152]{3,2,1,0:T(8,128)(2,1)}, bf16[2,2,144,1152]{3,2,1,0:T(8,128)(2,1)}, u32[]{:S(2)}, u32[]{:S(2)}) %collective-permute-start.9) | collective-permute-done | bytes 1327136 | tf_op jit(solution)/shard_map/ppermute | solution.py:470
  106.6 2.2 %collective-permute-start.13 = (bf16[2,2,144,1152]{3,2,1,0:T(8,128)(2,1)}, bf16[2,2,144,1152]{3,2,1,0:T(8,128)(2,1)}, u32[]{:S(2)}, u32[]{:S(2)}) collective-permute-start(bf16[2,2,144,1152]{3,2,1,0:T(8,128)(2,1)} %collective-permute-done.9.refs_3_), channel_id=1, source_target_pairs={{0,4},{4,0},{1,5},{5,1},{2,6},{6,2},{3,7},{7,3},{8,12},{12,8},{9,1... | collective-permute-start | bytes 3981320 | tf_op jit(solution)/shard_map/ppermute | solution.py:470
  111.0 2.3 %strips_in_place.1.weight_ref = bf16[1152,1152]{1,0:T(8,128)(2,1)S(1)} custom-call(s32[7]{0:T(128)S(1)} %stack.89.info_ref, bf16[4,4,48,1152]{3,2,1,0:T(8,128)(2,1)} %pad_maximum_fusion.plane_ref, bf16[4,4,48,1152]{3,2,1,0:T(8,128)(2,1)} %collective-permute-done.17.core_ref), custom_call_target="tpu_custom_call" | custom-call | flops 2000000000 | bytes 5000000 | tf_op jit(solution)/shard_map/strips_in_place/pallas_call | solution.py:183
  113.3 1.5 copy-done.5
  115.8 1.7 copy-done.6
  117.6 3.8 %mix.1 = (bf16[1152,128]{1,0:T(8,128)(2,1)S(1)}, bf16[1152,128]{1,0:T(8,128)(2,1)S(1)}, bf16[1152,128]{1,0:T(8,128)(2,1)S(1)}, bf16[1152,128]{1,0:T(8,128)(2,1)S(1)}) custom-call(s32[7]{0:T(128)S(1)} %stack.89.info_ref, bf16[1152,1152]{1,0:T(8,128)(2,1)S(1)} %copy-done.6, f32[1152,4]{1,0:T(8,128)S(1)} %bitcast.32, bf16[4,576,512]{2,1,0:T(8,128)(2,1)S(1)} %all-to-all-done.rows_ref), custom_call_target="tpu_custom_call" | custom-call | flops 4000000000 | bytes 4000000 | tf_op jit(solution)/shard_map/mix/pallas_call | solution.py:216
  122.8 5.0 %pieces_in_place.1 = (bf16[8,432,1152]{2,1,0:T(8,128)(2,1)S(1)}, bf16[1152,1152]{1,0:T(8,128)(2,1)S(1)}) custom-call(s32[7]{0:T(128)S(1)} %stack.89.info_ref, bf16[2,2,144,1152]{3,2,1,0:T(8,128)(2,1)} %pad_maximum_fusion.1.refs_0_, bf16[2,2,144,1152]{3,2,1,0:T(8,128)(2,1)} %collective-permute-done.8.refs_1_, ...), custom_call_target="tpu_custom_call" | custom-call | flops 3000000000 | bytes 20000000 | tf_op jit(solution)/shard_map/pieces_in_place/pallas_call | solution.py:259
  127.9 7.3 %collective-permute-done.19.refs_2_ = bf16[1152,128]{1,0:T(8,128)(2,1)S(1)} collective-permute-done((bf16[1152,128]{1,0:T(8,128)(2,1)S(1)}, bf16[1152,128]{1,0:T(8,128)(2,1)S(1)}, u32[]{:S(2)}, u32[]{:S(2)}) %collective-permute-start.19) | collective-permute-done | bytes 294944 | tf_op jit(solution)/shard_map/ppermute | solution.py:464
  136.4 11.8 %temporal.1 = (bf16[288,512]{1,0:T(8,128)(2,1)S(1)}, bf16[288,512]{1,0:T(8,128)(2,1)S(1)}, bf16[288,512]{1,0:T(8,128)(2,1)S(1)}, bf16[288,512]{1,0:T(8,128)(2,1)S(1)}) custom-call(s32[7]{0:T(128)S(1)} %stack.89.info_ref, f32[1152,4]{1,0:T(8,128)S(1)} %bitcast.33, bf16[8,432,1152]{2,1,0:T(8,128)(2,1)S(1)} %get-tuple-element.62.qkv_ref, ...), custom_call_target="tpu_custom_call" | custom-call | flops 17999998976 | bytes 12000000 | tf_op jit(solution)/shard_map/temporal/pallas_call | solution.py:378
  148.2 3.1 %collective-permute-start.21 = (bf16[288,512]{1,0:T(8,128)(2,1)S(1)}, bf16[288,512]{1,0:T(8,128)(2,1)S(1)}, u32[]{:S(2)}, u32[]{:S(2)}) collective-permute-start(bf16[288,512]{1,0:T(8,128)(2,1)S(1)} %get-tuple-element.75), channel_id=1, source_target_pairs={{0,0},{1,1},{2,18},{3,19},{16,2},{17,3},{18,16},{19,17},{4,4},{5,5... | collective-permute-start | bytes 884744 | tf_op jit(solution)/shard_map/ppermute | solution.py:514
  151.3 2.3 %collective-permute-start.23 = (bf16[288,512]{1,0:T(8,128)(2,1)S(1)}, bf16[288,512]{1,0:T(8,128)(2,1)S(1)}, u32[]{:S(2)}, u32[]{:S(2)}) collective-permute-start(bf16[288,512]{1,0:T(8,128)(2,1)S(1)} %get-tuple-element.77), channel_id=1, source_target_pairs={{0,2},{1,3},{2,16},{3,17},{16,0},{17,1},{18,18},{19,19},{4,6},{5,7... | collective-permute-start | bytes 884744 | tf_op jit(solution)/shard_map/ppermute | solution.py:514
  153.6 3.9 %collective-permute-start.24 = (bf16[288,512]{1,0:T(8,128)(2,1)S(1)}, bf16[288,512]{1,0:T(8,128)(2,1)S(1)}, u32[]{:S(2)}, u32[]{:S(2)}) collective-permute-start(bf16[288,512]{1,0:T(8,128)(2,1)S(1)} %get-tuple-element.78), channel_id=1, source_target_pairs={{0,3},{1,0},{2,17},{3,18},{16,1},{17,2},{18,19},{19,16},{4,7},{5,4... | collective-permute-start | bytes 884744 | tf_op jit(solution)/shard_map/ppermute | solution.py:514
  157.5 12.8 %collective-permute-done.21.refs_0_ = bf16[288,512]{1,0:T(8,128)(2,1)S(1)} collective-permute-done((bf16[288,512]{1,0:T(8,128)(2,1)S(1)}, bf16[288,512]{1,0:T(8,128)(2,1)S(1)}, u32[]{:S(2)}, u32[]{:S(2)}) %collective-permute-start.21) | collective-permute-done | bytes 294944 | tf_op jit(solution)/shard_map/ppermute | solution.py:514
  170.3 5.8 %collective-permute-done.22.refs_1_ = bf16[288,512]{1,0:T(8,128)(2,1)S(1)} collective-permute-done((bf16[288,512]{1,0:T(8,128)(2,1)S(1)}, bf16[288,512]{1,0:T(8,128)(2,1)S(1)}, u32[]{:S(2)}, u32[]{:S(2)}) %collective-permute-start.22) | collective-permute-done | bytes 294944 | tf_op jit(solution)/shard_map/ppermute | solution.py:514
  176.2 4.7 %collective-permute-done.24.refs_3_ = bf16[288,512]{1,0:T(8,128)(2,1)S(1)} collective-permute-done((bf16[288,512]{1,0:T(8,128)(2,1)S(1)}, bf16[288,512]{1,0:T(8,128)(2,1)S(1)}, u32[]{:S(2)}, u32[]{:S(2)}) %collective-permute-start.24) | collective-permute-done | bytes 294944 | tf_op jit(solution)/shard_map/ppermute | solution.py:514
  180.9 2.0 %place.1 = bf16[16,288,128]{2,1,0:T(8,128)(2,1)} custom-call(s32[7]{0:T(128)S(1)} %stack.89.info_ref, bf16[288,512]{1,0:T(8,128)(2,1)S(1)} %collective-permute-done.21.refs_0_, bf16[288,512]{1,0:T(8,128)(2,1)S(1)} %collective-permute-done.22.refs_1_, bf16[288,512]{1,0:T(8,128)(2,1)S(1)} %collective-permute-done.23.refs_2_, ...), custom_call_target="tpu_custom_call" | custom-call | tf_op jit(solution)/shard_map/place/pallas_call | solution.py:417
  (69 shorter events, 23.8 us)
Async XLA Ops:
  5.1 29.4 %collective-permute-start = (bf16[144,1152]{1,0:T(8,128)(2,1)S(1)}, bf16[144,1152]{1,0:T(8,128)(2,1)S(1)}, u32[]{:S(2)}, u32[]{:S(2)}) collective-permute-start(bf16[144,1152]{1,0:T(8,128)(2,1)S(1)} %bitcast_select_fusion), channel_id=1, source_target_pairs={{0,1},{1,2},{2,3},{3,0},{4,5},{5,6},{6,7},{7,4},{8,9},{9,10},{10,1... | collective-permute-start | bytes 995336 | tf_op jit(solution)/shard_map/ppermute | solution.py:464
  6.4 28.1 %collective-permute-start.1 = (bf16[144,1152]{1,0:T(8,128)(2,1)S(1)}, bf16[144,1152]{1,0:T(8,128)(2,1)S(1)}, u32[]{:S(2)}, u32[]{:S(2)}) collective-permute-start(bf16[144,1152]{1,0:T(8,128)(2,1)S(1)} %bitcast_select_fusion), channel_id=1, source_target_pairs={{0,2},{1,3},{2,0},{3,1},{4,6},{5,7},{6,4},{7,5},{8,10},{9,11},{10,... | collective-permute-start | bytes 995336 | tf_op jit(solution)/shard_map/ppermute | solution.py:464
  7.4 29.6 %collective-permute-start.2 = (bf16[144,1152]{1,0:T(8,128)(2,1)S(1)}, bf16[144,1152]{1,0:T(8,128)(2,1)S(1)}, u32[]{:S(2)}, u32[]{:S(2)}) collective-permute-start(bf16[144,1152]{1,0:T(8,128)(2,1)S(1)} %bitcast_select_fusion), channel_id=1, source_target_pairs={{0,3},{1,0},{2,1},{3,2},{4,7},{5,4},{6,5},{7,6},{8,11},{9,8},{10,9... | collective-permute-start | bytes 995336 | tf_op jit(solution)/shard_map/ppermute | solution.py:464
  37.1 12.3 %copy-start.7 = (bf16[2,144,1152]{2,1,0:T(8,128)(2,1)}, bf16[2,144,1152]{2,1,0:T(8,128)(2,1)S(1)}, u32[]{:S(2)}) copy-start(bf16[2,144,1152]{2,1,0:T(8,128)(2,1)S(1)} %pad_maximum_fusion.4) | copy-start | bytes 1990660
  37.1 16.2 %collective-permute-start.4 = (bf16[2,144,1152]{2,1,0:T(8,128)(2,1)S(1)}, bf16[2,144,1152]{2,1,0:T(8,128)(2,1)S(1)}, u32[]{:S(2)}, u32[]{:S(2)}) collective-permute-start(bf16[2,144,1152]{2,1,0:T(8,128)(2,1)S(1)} %pad_maximum_fusion.4), channel_id=1, source_target_pairs={{0,16},{8,24},{16,0},{24,8},{1,17},{9,25},{17,1},{25,9},{2,18},{10... | collective-permute-start | bytes 1990664 | tf_op jit(solution)/shard_map/ppermute | solution.py:470
  37.4 11.9 %copy-start.9 = (bf16[2,144,1152]{2,1,0:T(8,128)(2,1)}, bf16[2,144,1152]{2,1,0:T(8,128)(2,1)S(1)}, u32[]{:S(2)}) copy-start(bf16[2,144,1152]{2,1,0:T(8,128)(2,1)S(1)} %pad_maximum_fusion.3) | copy-start | bytes 1990660
  37.5 16.6 %collective-permute-start.3 = (bf16[2,144,1152]{2,1,0:T(8,128)(2,1)S(1)}, bf16[2,144,1152]{2,1,0:T(8,128)(2,1)}, u32[]{:S(2)}, u32[]{:S(2)}) collective-permute-start(bf16[2,144,1152]{2,1,0:T(8,128)(2,1)S(1)} %pad_maximum_fusion.3), channel_id=1, source_target_pairs={{0,8},{8,0},{16,24},{24,16},{1,9},{9,1},{17,25},{25,17},{2,10},{10... | collective-permute-start | bytes 1990664 | tf_op jit(solution)/shard_map/ppermute | solution.py:470
  38.7 10.6 %collective-permute-start.5 = (bf16[48,1152]{1,0:T(8,128)(2,1)S(1)}, bf16[48,1152]{1,0:T(8,128)(2,1)S(1)}, u32[]{:S(2)}, u32[]{:S(2)}) collective-permute-start(bf16[48,1152]{1,0:T(8,128)(2,1)S(1)} %constant_dynamic-slice_fusion.1), channel_id=1, source_target_pairs={{0,1},{1,2},{2,3},{3,0},{4,5},{5,6},{6,7},{7,4},{8,9},{9,10},{10,1... | collective-permute-start | bytes 331784 | tf_op jit(solution)/shard_map/ppermute | solution.py:464
  38.7 10.6 %collective-permute-start.6 = (bf16[48,1152]{1,0:T(8,128)(2,1)S(1)}, bf16[48,1152]{1,0:T(8,128)(2,1)S(1)}, u32[]{:S(2)}, u32[]{:S(2)}) collective-permute-start(bf16[48,1152]{1,0:T(8,128)(2,1)S(1)} %constant_dynamic-slice_fusion.1), channel_id=1, source_target_pairs={{0,2},{1,3},{2,0},{3,1},{4,6},{5,7},{6,4},{7,5},{8,10},{9,11},{10,... | collective-permute-start | bytes 331784 | tf_op jit(solution)/shard_map/ppermute | solution.py:464
  39.2 11.5 %collective-permute-start.7 = (bf16[48,1152]{1,0:T(8,128)(2,1)S(1)}, bf16[48,1152]{1,0:T(8,128)(2,1)S(1)}, u32[]{:S(2)}, u32[]{:S(2)}) collective-permute-start(bf16[48,1152]{1,0:T(8,128)(2,1)S(1)} %constant_dynamic-slice_fusion.1), channel_id=1, source_target_pairs={{0,3},{1,0},{2,1},{3,2},{4,7},{5,4},{6,5},{7,6},{8,11},{9,8},{10,9... | collective-permute-start | bytes 331784 | tf_op jit(solution)/shard_map/ppermute | solution.py:464
  54.1 60.7 %all-to-all-start = ((bf16[4,576,512]{2,1,0:T(8,128)(2,1)}), bf16[4,576,512]{2,1,0:T(8,128)(2,1)S(1)}, u32[]{:S(2)}, u32[]{:S(2)}) async-start(bf16[4,576,512]{2,1,0:T(8,128)(2,1)} %spatial_attention.3), calls=%async_computation | async-start | bytes 4718592 | tf_op jit(solution)/shard_map/all_to_all | solution.py:500
  57.9 2.8 %copy-start.8 = (bf16[2,144,1152]{2,1,0:T(8,128)(2,1)S(1)}, bf16[2,144,1152]{2,1,0:T(8,128)(2,1)}, u32[]{:S(2)}) copy-start(bf16[2,144,1152]{2,1,0:T(8,128)(2,1)} %copy-done.7) | copy-start | bytes 1990660
  57.9 2.8 %copy-start.12 = (bf16[2,144,1152]{2,1,0:T(8,128)(2,1)S(1)}, bf16[2,144,1152]{2,1,0:T(8,128)(2,1)}, u32[]{:S(2)}) copy-start(bf16[2,144,1152]{2,1,0:T(8,128)(2,1)} %copy-done.11) | copy-start | bytes 1990660
  58.0 10.5 %collective-permute-start.14 = (bf16[4,48,1152]{2,1,0:T(8,128)(2,1)S(1)}, bf16[4,48,1152]{2,1,0:T(8,128)(2,1)S(1)}, u32[]{:S(2)}, u32[]{:S(2)}) collective-permute-start(bf16[4,48,1152]{2,1,0:T(8,128)(2,1)S(1)} %get-tuple-element.80), channel_id=1, source_target_pairs={{0,8},{8,0},{16,24},{24,16},{1,9},{9,1},{17,25},{25,17},{2,10},{10... | collective-permute-start | bytes 1327112 | tf_op jit(solution)/shard_map/ppermute | solution.py:470
  59.3 11.3 %collective-permute-start.15 = (bf16[4,48,1152]{2,1,0:T(8,128)(2,1)S(1)}, bf16[4,48,1152]{2,1,0:T(8,128)(2,1)S(1)}, u32[]{:S(2)}, u32[]{:S(2)}) collective-permute-start(bf16[4,48,1152]{2,1,0:T(8,128)(2,1)S(1)} %get-tuple-element.80), channel_id=1, source_target_pairs={{0,16},{8,24},{16,0},{24,8},{1,17},{9,25},{17,1},{25,9},{2,18},{10... | collective-permute-start | bytes 1327112 | tf_op jit(solution)/shard_map/ppermute | solution.py:470
  59.7 18.0 %collective-permute-start.16 = (bf16[4,48,1152]{2,1,0:T(8,128)(2,1)S(1)}, bf16[4,48,1152]{2,1,0:T(8,128)(2,1)S(1)}, u32[]{:S(2)}, u32[]{:S(2)}) collective-permute-start(bf16[4,48,1152]{2,1,0:T(8,128)(2,1)S(1)} %get-tuple-element.80), channel_id=1, source_target_pairs={{0,24},{8,16},{16,8},{24,0},{1,25},{9,17},{17,9},{25,1},{2,26},{10... | collective-permute-start | bytes 1327112 | tf_op jit(solution)/shard_map/ppermute | solution.py:470
  62.0 44.6 %collective-permute-start.9 = (bf16[2,2,144,1152]{3,2,1,0:T(8,128)(2,1)}, bf16[2,2,144,1152]{3,2,1,0:T(8,128)(2,1)}, u32[]{:S(2)}, u32[]{:S(2)}) collective-permute-start(bf16[2,2,144,1152]{3,2,1,0:T(8,128)(2,1)} %pad_maximum_fusion.2.refs_2_), channel_id=1, source_target_pairs={{0,8},{8,0},{16,24},{24,16},{1,9},{9,1},{17,25},{25,17},{2,10},{10... | collective-permute-start | bytes 3981320 | tf_op jit(solution)/shard_map/ppermute | solution.py:470
  65.5 43.2 %collective-permute-start.8 = (bf16[2,2,144,1152]{3,2,1,0:T(8,128)(2,1)}, bf16[2,2,144,1152]{3,2,1,0:T(8,128)(2,1)}, u32[]{:S(2)}, u32[]{:S(2)}) collective-permute-start(bf16[2,2,144,1152]{3,2,1,0:T(8,128)(2,1)} %pad_maximum_fusion.1.refs_0_), channel_id=1, source_target_pairs={{0,16},{8,24},{16,0},{24,8},{1,17},{9,25},{17,1},{25,9},{2,18},{10... | collective-permute-start | bytes 3981320 | tf_op jit(solution)/shard_map/ppermute | solution.py:470
  77.8 32.1 %copy-start.13 = (f32[2,4,1152]{2,1,0:T(4,128)S(1)}, f32[2,4,1152]{2,1,0:T(4,128)}, u32[]{:S(2)}) copy-start(f32[2,4,1152]{2,1,0:T(4,128)} %param.13) | copy-start | bytes 110596
  79.2 31.7 %collective-permute-start.17 = (bf16[4,4,48,1152]{3,2,1,0:T(8,128)(2,1)}, bf16[4,4,48,1152]{3,2,1,0:T(8,128)(2,1)}, u32[]{:S(2)}, u32[]{:S(2)}) collective-permute-start(bf16[4,4,48,1152]{3,2,1,0:T(8,128)(2,1)} %pad_maximum_fusion.plane_ref), channel_id=1, source_target_pairs={{0,4},{4,0},{1,5},{5,1},{2,6},{6,2},{3,7},{7,3},{8,12},{12,8},{9,1... | collective-permute-start | bytes 5308424 | tf_op jit(solution)/shard_map/ppermute | solution.py:470
  84.9 37.0 %collective-permute-start.12 = (bf16[2,2,144,1152]{3,2,1,0:T(8,128)(2,1)}, bf16[2,2,144,1152]{3,2,1,0:T(8,128)(2,1)}, u32[]{:S(2)}, u32[]{:S(2)}) collective-permute-start(bf16[2,2,144,1152]{3,2,1,0:T(8,128)(2,1)} %pad_maximum_fusion.2.refs_2_), channel_id=1, source_target_pairs={{0,4},{4,0},{1,5},{5,1},{2,6},{6,2},{3,7},{7,3},{8,12},{12,8},{9,1... | collective-permute-start | bytes 3981320 | tf_op jit(solution)/shard_map/ppermute | solution.py:470
  84.9 37.9 %collective-permute-start.10 = (bf16[2,2,144,1152]{3,2,1,0:T(8,128)(2,1)}, bf16[2,2,144,1152]{3,2,1,0:T(8,128)(2,1)}, u32[]{:S(2)}, u32[]{:S(2)}) collective-permute-start(bf16[2,2,144,1152]{3,2,1,0:T(8,128)(2,1)} %pad_maximum_fusion.1.refs_0_), channel_id=1, source_target_pairs={{0,4},{4,0},{1,5},{5,1},{2,6},{6,2},{3,7},{7,3},{8,12},{12,8},{9,1... | collective-permute-start | bytes 3981320 | tf_op jit(solution)/shard_map/ppermute | solution.py:470
  106.6 16.2 %collective-permute-start.13 = (bf16[2,2,144,1152]{3,2,1,0:T(8,128)(2,1)}, bf16[2,2,144,1152]{3,2,1,0:T(8,128)(2,1)}, u32[]{:S(2)}, u32[]{:S(2)}) collective-permute-start(bf16[2,2,144,1152]{3,2,1,0:T(8,128)(2,1)} %collective-permute-done.9.refs_3_), channel_id=1, source_target_pairs={{0,4},{4,0},{1,5},{5,1},{2,6},{6,2},{3,7},{7,3},{8,12},{12,8},{9,1... | collective-permute-start | bytes 3981320 | tf_op jit(solution)/shard_map/ppermute | solution.py:470
  108.7 14.1 %collective-permute-start.11 = (bf16[2,2,144,1152]{3,2,1,0:T(8,128)(2,1)}, bf16[2,2,144,1152]{3,2,1,0:T(8,128)(2,1)}, u32[]{:S(2)}, u32[]{:S(2)}) collective-permute-start(bf16[2,2,144,1152]{3,2,1,0:T(8,128)(2,1)} %collective-permute-done.8.refs_1_), channel_id=1, source_target_pairs={{0,4},{4,0},{1,5},{5,1},{2,6},{6,2},{3,7},{7,3},{8,12},{12,8},{9,1... | collective-permute-start | bytes 3981320 | tf_op jit(solution)/shard_map/ppermute | solution.py:470
  121.4 6.6 %collective-permute-start.18 = (bf16[1152,128]{1,0:T(8,128)(2,1)S(1)}, bf16[1152,128]{1,0:T(8,128)(2,1)S(1)}, u32[]{:S(2)}, u32[]{:S(2)}) collective-permute-start(bf16[1152,128]{1,0:T(8,128)(2,1)S(1)} %get-tuple-element.72), channel_id=1, source_target_pairs={{0,4},{4,8},{8,12},{12,0},{1,5},{5,9},{9,13},{13,1},{2,6},{6,10},{... | collective-permute-start | bytes 884744 | tf_op jit(solution)/shard_map/ppermute | solution.py:464
  121.9 13.4 %collective-permute-start.19 = (bf16[1152,128]{1,0:T(8,128)(2,1)S(1)}, bf16[1152,128]{1,0:T(8,128)(2,1)S(1)}, u32[]{:S(2)}, u32[]{:S(2)}) collective-permute-start(bf16[1152,128]{1,0:T(8,128)(2,1)S(1)} %get-tuple-element.73), channel_id=1, source_target_pairs={{0,8},{4,12},{8,0},{12,4},{1,9},{5,13},{9,1},{13,5},{2,10},{6,14},... | collective-permute-start | bytes 884744 | tf_op jit(solution)/shard_map/ppermute | solution.py:464
  122.8 13.6 %copy-start.2 = (f32[1,4,1152]{1,2,0:T(8,128)S(1)}, f32[1,4,1152]{1,2,0:T(8,128)}, u32[]{:S(2)}) copy-start(f32[1,4,1152]{1,2,0:T(8,128)} %copy.9) | copy-start | bytes 55300
  122.8 13.6 %collective-permute-start.20 = (bf16[1152,128]{1,0:T(8,128)(2,1)S(1)}, bf16[1152,128]{1,0:T(8,128)(2,1)S(1)}, u32[]{:S(2)}, u32[]{:S(2)}) collective-permute-start(bf16[1152,128]{1,0:T(8,128)(2,1)S(1)} %get-tuple-element.74), channel_id=1, source_target_pairs={{0,12},{4,0},{8,4},{12,8},{1,13},{5,1},{9,5},{13,9},{2,14},{6,2},{... | collective-permute-start | bytes 884744 | tf_op jit(solution)/shard_map/ppermute | solution.py:464
  148.2 22.2 %collective-permute-start.21 = (bf16[288,512]{1,0:T(8,128)(2,1)S(1)}, bf16[288,512]{1,0:T(8,128)(2,1)S(1)}, u32[]{:S(2)}, u32[]{:S(2)}) collective-permute-start(bf16[288,512]{1,0:T(8,128)(2,1)S(1)} %get-tuple-element.75), channel_id=1, source_target_pairs={{0,0},{1,1},{2,18},{3,19},{16,2},{17,3},{18,16},{19,17},{4,4},{5,5... | collective-permute-start | bytes 884744 | tf_op jit(solution)/shard_map/ppermute | solution.py:514
  151.2 24.9 %collective-permute-start.22 = (bf16[288,512]{1,0:T(8,128)(2,1)S(1)}, bf16[288,512]{1,0:T(8,128)(2,1)S(1)}, u32[]{:S(2)}, u32[]{:S(2)}) collective-permute-start(bf16[288,512]{1,0:T(8,128)(2,1)S(1)} %get-tuple-element.76), channel_id=1, source_target_pairs={{0,1},{1,2},{2,19},{3,16},{16,3},{17,0},{18,17},{19,18},{4,5},{5,6... | collective-permute-start | bytes 884744 | tf_op jit(solution)/shard_map/ppermute | solution.py:514
  151.3 24.9 %collective-permute-start.23 = (bf16[288,512]{1,0:T(8,128)(2,1)S(1)}, bf16[288,512]{1,0:T(8,128)(2,1)S(1)}, u32[]{:S(2)}, u32[]{:S(2)}) collective-permute-start(bf16[288,512]{1,0:T(8,128)(2,1)S(1)} %get-tuple-element.77), channel_id=1, source_target_pairs={{0,2},{1,3},{2,16},{3,17},{16,0},{17,1},{18,18},{19,19},{4,6},{5,7... | collective-permute-start | bytes 884744 | tf_op jit(solution)/shard_map/ppermute | solution.py:514
  153.6 27.3 %collective-permute-start.24 = (bf16[288,512]{1,0:T(8,128)(2,1)S(1)}, bf16[288,512]{1,0:T(8,128)(2,1)S(1)}, u32[]{:S(2)}, u32[]{:S(2)}) collective-permute-start(bf16[288,512]{1,0:T(8,128)(2,1)S(1)} %get-tuple-element.78), channel_id=1, source_target_pairs={{0,3},{1,0},{2,17},{3,18},{16,1},{17,2},{18,19},{19,16},{4,7},{5,4... | collective-permute-start | bytes 884744 | tf_op jit(solution)/shard_map/ppermute | solution.py:514
  (8 other events, 13.4 us)

commit v3 on v2

--- a/solution.py
+++ b/solution.py
@@ -162,46 +162,28 @@
     )(info, queries, keys, values, *held)
 
 
-def strips_kernel(heads, info_ref, plane_ref, core_ref, out_ref):
-    me, core, member = info_ref[4], info_ref[5], info_ref[6]
+def mix_kernel(heads, ranks, info_ref, plane_ref, core_ref, gates_ref, rows_ref, *refs):
+    out_refs, weight_ref, mixed_ref = refs[:-2], refs[-2], refs[-1]
+    rank, me, core, member = info_ref[3], info_ref[4], info_ref[5], info_ref[6]
     members, _, strip, _ = plane_ref.shape
-    width = out_ref.shape[0] // heads
+    width = rows_ref.shape[1] // 2
     half = width // 2
     last = half // strip - 1
+    gate = flip(gates_ref[...])[:, 0:1]
     for far, ref in enumerate((plane_ref, core_ref)):
         for other in range(members):
             whose = jnp.minimum(member ^ other, last)
             for step in range(heads):
                 source = lax.rem(me - step + heads, heads)
                 start = source * width + (core ^ far) * half + whose * strip
-                out_ref[pl.ds(pl.multiple_of(start, 16), strip), :] = ref[other, step]
-
-
-def strips_in_place(info, by_plane, by_core, width):
-    heads, features = by_plane.shape[1], by_plane.shape[3]
-    vmem = pl.BlockSpec(memory_space=pltpu.VMEM)
-    return pl.pallas_call(
-        functools.partial(strips_kernel, heads),
-        in_specs=[pl.BlockSpec(memory_space=pltpu.SMEM)] + [vmem] * 2,
-        out_specs=vmem,
-        out_shape=jax.ShapeDtypeStruct((heads * width, features), BF16),
-        compiler_params=pltpu.CompilerParams(vmem_limit_bytes=12 * MIB),
-        cost_estimate=pl.CostEstimate(flops=2 * 10**9, bytes_accessed=5 * 10**6, transcendentals=0),
-        name="strips_in_place",
-    )(info, by_plane, by_core)
-
-
-def mix_kernel(heads, ranks, info_ref, weight_ref, gate_ref, rows_ref, *refs):
-    out_refs, mixed_ref = refs[:-1], refs[-1]
-    rank = info_ref[3]
-    width = rows_ref.shape[1] // 2
+                weight_ref[pl.ds(pl.multiple_of(start, 16), strip), :] = ref[other, step]
     summed = None
     for source in range(heads):
         term = tn(weight_ref[source * width:(source + 1) * width, :], rows_ref[source, :width, :])
         summed = term if summed is None else summed + term
     for source in range(heads):
         here = slice(source * width, (source + 1) * width)
-        mixed = rows_ref[source, width:, :].astype(F32) + gate_ref[here, 0:1] * summed[here]
+        mixed = rows_ref[source, width:, :].astype(F32) + gate[here] * summed[here]
         mixed_ref[here, :] = mixed.astype(BF16)
     lanes = mixed_ref.shape[1] // ranks
     for step in range(ranks):
@@ -209,20 +191,20 @@
         out_refs[step][...] = mixed_ref[:, pl.ds(pl.multiple_of(to * lanes, lanes), lanes)]
 
 
-def mix(info, weight, arrived, columns, ranks):
+def mix(info, by_plane, by_core, arrived, gates, ranks):
     heads, width, rows = arrived.shape
-    features = weight.shape[1]
+    features = by_plane.shape[3]
     vmem = pl.BlockSpec(memory_space=pltpu.VMEM)
     return pl.pallas_call(
         functools.partial(mix_kernel, heads, ranks),
-        in_specs=[pl.BlockSpec(memory_space=pltpu.SMEM)] + [vmem] * 3,
+        in_specs=[pl.BlockSpec(memory_space=pltpu.SMEM)] + [vmem] * 4,
         out_specs=[vmem] * ranks,
         out_shape=[jax.ShapeDtypeStruct((features, rows // ranks), BF16)] * ranks,
-        scratch_shapes=[pltpu.VMEM((features, rows), BF16)],
+        scratch_shapes=[pltpu.VMEM((features, features), BF16), pltpu.VMEM((features, rows), BF16)],
         compiler_params=pltpu.CompilerParams(vmem_limit_bytes=20 * MIB),
         cost_estimate=pl.CostEstimate(flops=4 * 10**9, bytes_accessed=4 * 10**6, transcendentals=0),
         name="mix",
-    )(info, weight, columns, arrived)
+    )(info, by_plane, by_core, gates, arrived)
 
 
 def frame_at(place, rank, sizes):
@@ -283,7 +265,7 @@
     return found
 
 
-def temporal_kernel(sizes, info_ref, cols_ref, qkv_ref, last_ref, *refs):
+def temporal_kernel(sizes, info_ref, gates_ref, qkv_ref, last_ref, *refs):
     groups, ranks, heads, block, span, run = sizes
     mixed_refs, out_refs = refs[:ranks], refs[ranks:-3]
     normed_ref, attended_ref, result_ref = refs[-3:]
@@ -297,12 +279,13 @@
 
     @pl.when(step == 0)
     def norm():
+        columns = flip(gates_ref[...])
         for rank in range(ranks):
             full = mixed_refs[rank][...].astype(F32)
             center = full - jnp.mean(full, axis=0, keepdims=True)
             variance = jnp.mean(center * center, axis=0, keepdims=True)
             normed = center * lax.rsqrt(variance + EPS)
-            normed = normed * (1.0 + cols_ref[:, 2:3]) + cols_ref[:, 1:2]
+            normed = normed * (1.0 + columns[:, 2:3]) + columns[:, 1:2]
             normed_ref[:, rank * lanes:(rank + 1) * lanes] = normed.astype(BF16)
 
     frame = lax.broadcasted_iota(jnp.int32, (FRAMES, rows), 1) // span
@@ -336,10 +319,11 @@
     def finish():
         width = features // heads
         clip, me, count = info_ref[2], info_ref[4], info_ref[0]
+        gate = flip(gates_ref[...])[:, 3:4]
         total = tn(last_ref[...], attended_ref[...])
         for rank in range(ranks):
             lane = slice(rank * lanes, (rank + 1) * lanes)
-            full = mixed_refs[rank][...].astype(F32) + cols_ref[:, 3:4] * total[:, lane]
+            full = mixed_refs[rank][...].astype(F32) + gate * total[:, lane]
             place = lax.broadcasted_iota(jnp.int32, (1, lanes), 1) + rank * lanes
             among = me * span + place % span
             token = (among // block * ranks + rank_here) * block + among % block
@@ -368,7 +352,7 @@
                         out_refs[each * heads + step_to][...] = pick()
 
 
-def temporal(info, mixed, columns, weights, sizes):
+def temporal(info, mixed, gates, weights, sizes):
     groups, ranks, heads, block, span, run = sizes
     features, lanes = mixed[0].shape
     rows = ranks * lanes
@@ -388,7 +372,7 @@
         compiler_params=pltpu.CompilerParams(vmem_limit_bytes=20 * MIB),
         cost_estimate=pl.CostEstimate(flops=18 * 10**9, bytes_accessed=12 * 10**6, transcendentals=0),
         name="temporal",
-    )(info, columns, *weights, *mixed)
+    )(info, gates, *weights, *mixed)
 
 
 def place_kernel(sizes, info_ref, *refs):
@@ -471,7 +455,7 @@
 
     info = jnp.stack([tok_count[clip], frame_count[clip], clip, rank, head, core, member]).astype(jnp.int32)
     here = lax.dynamic_index_in_dim(modulation, clip, 0, keepdims=False)
-    columns = here.T
+    gates = jnp.concatenate([here, here], axis=0)
 
     plane = clips_inner * rank_hi
     turned = jnp.swapaxes(qkv_temporal, 1, 2)
@@ -504,12 +488,11 @@
         pieces += [part, swap(part, ("clip", "rank"), plane, bit)]
     same = jnp.stack(strips)
     by_plane = jnp.stack([same] + [swap(same, ("clip", "rank"), plane, bit) for bit in range(1, plane)])
-    strips = strips_in_place(info, by_plane, swap(by_plane, "core", cores, 1), width)
+    by_core = swap(by_plane, "core", cores, 1)
     pieces += [swap(each, "core", cores, 1) for each in pieces]
-    arrived, strips = lax.optimization_barrier((arrived, strips))
-    mixed = mix(info, strips, arrived, columns, ranks)
+    mixed = mix(info, by_plane, by_core, arrived, gates, ranks)
     mixed = around(mixed, ("rank", "core"), ranks)
-    result = temporal(info, mixed, columns, pieces_in_place(info, pieces), sizes)
+    result = temporal(info, mixed, gates, pieces_in_place(info, pieces), sizes)
     arrived = [
         lax.ppermute(result[part * heads + step], ("outer", "clip", "head"), routes(step, part, sizes))
         for part in range(span // run) for step in range(heads)

time: 183 us -> 179 us (0.978)
  Pallas kernels: 56.1 us -> 43.9 us
  waiting for transfers between devices: 71.3 us -> 80.2 us
    pallas_call x2, Pallas kernels: 29.9 us -> 20.4 us  [spatial_attention(): pl.pallas_call(functools.partial(spatial_kernel, ranks, first), grid_spec...]
    ppermute x9, waiting for transfers between devices: 12.4 us -> 21.8 us  [send(): lax.ppermute(array, axis, [(i, (i + step) % size) for i in range(size)])]
    pallas_call x1 -> x0, Pallas kernels: 2.28 us -> none  [strips_in_place(): pl.pallas_call(functools.partial(strips_kernel, heads), in_specs=[pl.Bloc...]
  transfers between devices with their start and end apart: 26 -> 26, of which waited for: 13 -> 14; matrix products, arithmetic and copies ran while one was open for 3% -> 2% of each run, Pallas kernels for 23% -> 17%
where the time goes in v3:
time: 179 us
  waiting for transfers between devices  80.2 us (45%)
  Pallas kernels  43.9 us (25%)
  starting transfers between devices  36 us (20%)
  local copies, waits for them, and re-layouts  13.5 us (8%)
  other arithmetic  5.22 us (3%)
    ppermute x12, waiting for transfers between devices, swap(): return lax.ppermute(array, axis, [(i, i ^ bit) for i in range(size)])  35.7 us
    ppermute x4, waiting for transfers between devices, on_device(): lax.ppermute(result[part * heads + step], ('outer', 'clip', 'head'), rout...  22.8 us
    ppermute x9, waiting for transfers between devices, send(): lax.ppermute(array, axis, [(i, (i + step) % size) for i in range(size)])  21.8 us
    pallas_call x2, Pallas kernels, spatial_attention(): pl.pallas_call(functools.partial(spatial_kernel, ranks, first), grid_spec...  20.4 us
    ppermute x12, starting transfers between devices, swap(): return lax.ppermute(array, axis, [(i, i ^ bit) for i in range(size)])  15.5 us
    pallas_call x1, Pallas kernels, temporal(): pl.pallas_call(functools.partial(temporal_kernel, sizes), grid_spec=pltpu...  11.1 us
    ppermute x4, starting transfers between devices, on_device(): lax.ppermute(result[part * heads + step], ('outer', 'clip', 'head'), rout...  9.8 us
    unnamed x28, local copies, waits for them, and re-layouts  9.57 us
  transfers between devices with their start and end apart: 26, of which 14 were waited for; matrix products, arithmetic and copies ran while one was open for 2% of the time, Pallas kernels for 17%

profile of v3, /device:TPU:13, one launch (start us, length us, event | category | flops | bytes accessed | tf_op | source)
XLA Modules:
  0.0 179.0 jit_solution(18246054419397611819)
XLA Ops:
  0.0 1.4 dynamic_slice.20
  3.8 1.3 stack.89.info_ref
  7.4 1.4 collective-permute-start.2
  8.8 2.0 %copy-done.3 = bf16[3,2,1024,288]{2,3,1,0:T(8,128)(2,1)S(1)} copy-done((bf16[3,2,1024,288]{2,3,1,0:T(8,128)(2,1)S(1)}, bf16[3,2,1024,288]{2,3,1,0:T(8,128)(2,1)}, u32[]{:S(2)}) %copy-start.3) | copy-done | bytes 3538968
  12.1 1.3 arrange.1
  13.4 13.9 %spatial_attention.2.refs_0_ = bf16[3,288,512]{2,1,0:T(8,128)(2,1)S(1)} custom-call(s32[7]{0:T(128)S(1)} %stack.89.info_ref, bf16[4,2,2,144,256]{4,3,2,1,0:T(8,128)(2,1)S(1)} %get-tuple-element.42.query_ref, bf16[2,2,1024,144]{3,2,1,0:T(8,128)(2,1)S(1)} %get-tuple-element.43.key_ref, bf16[2,2,160,1024]{3,2,1,0:T(8,128)(2,1)S(1)} %get-tuple-element.44.value_ref), custom_call_target="tpu_custom_call" | custom-call | flops 14000000000 | bytes 5000000 | tf_op jit(solution)/shard_map/spatial_attention/pallas_call | solution.py:149
  27.4 6.8 %collective-permute-done.1 = bf16[144,1152]{1,0:T(8,128)(2,1)S(1)} collective-permute-done((bf16[144,1152]{1,0:T(8,128)(2,1)S(1)}, bf16[144,1152]{1,0:T(8,128)(2,1)S(1)}, u32[]{:S(2)}, u32[]{:S(2)}) %collective-permute-start.1) | collective-permute-done | bytes 331808 | tf_op jit(solution)/shard_map/ppermute | solution.py:448
  34.2 2.8 %collective-permute-done.2 = bf16[144,1152]{1,0:T(8,128)(2,1)S(1)} collective-permute-done((bf16[144,1152]{1,0:T(8,128)(2,1)S(1)}, bf16[144,1152]{1,0:T(8,128)(2,1)S(1)}, u32[]{:S(2)}, u32[]{:S(2)}) %collective-permute-start.2) | collective-permute-done | bytes 331808 | tf_op jit(solution)/shard_map/ppermute | solution.py:448
  40.5 6.5 %spatial_attention.3 = bf16[4,576,512]{2,1,0:T(8,128)(2,1)} custom-call(s32[7]{0:T(128)S(1)} %stack.89.info_ref, bf16[4,2,2,144,256]{4,3,2,1,0:T(8,128)(2,1)S(1)} %get-tuple-element.42.query_ref, bf16[2,2,1024,144]{3,2,1,0:T(8,128)(2,1)S(1)} %get-tuple-element.43.key_ref, bf16[2,2,160,1024]{3,2,1,0:T(8,128)(2,1)S(1)} %get-tuple-element.44.value_ref, ...), custom_call_target="tpu_custom_call" | custom-call | flops 14000000000 | bytes 5000000 | tf_op jit(solution)/shard_map/spatial_attention/pallas_call | solution.py:149
  47.0 3.5 %collective-permute-done.7 = bf16[48,1152]{1,0:T(8,128)(2,1)S(1)} collective-permute-done((bf16[48,1152]{1,0:T(8,128)(2,1)S(1)}, bf16[48,1152]{1,0:T(8,128)(2,1)S(1)}, u32[]{:S(2)}, u32[]{:S(2)}) %collective-permute-start.7) | collective-permute-done | bytes 110624 | tf_op jit(solution)/shard_map/ppermute | solution.py:448
  50.5 2.7 %collective-permute-done.4 = bf16[2,144,1152]{2,1,0:T(8,128)(2,1)S(1)} collective-permute-done((bf16[2,144,1152]{2,1,0:T(8,128)(2,1)S(1)}, bf16[2,144,1152]{2,1,0:T(8,128)(2,1)S(1)}, u32[]{:S(2)}, u32[]{:S(2)}) %collective-permute-start.4) | collective-permute-done | bytes 663584 | tf_op jit(solution)/shard_map/ppermute | solution.py:454
  54.1 3.8 %all-to-all-start = ((bf16[4,576,512]{2,1,0:T(8,128)(2,1)}), bf16[4,576,512]{2,1,0:T(8,128)(2,1)S(1)}, u32[]{:S(2)}, u32[]{:S(2)}) async-start(bf16[4,576,512]{2,1,0:T(8,128)(2,1)} %spatial_attention.3), calls=%async_computation | async-start | bytes 4718592 | tf_op jit(solution)/shard_map/all_to_all | solution.py:484
  63.2 2.3 %pad_maximum_fusion.1.refs_0_ = bf16[2,2,144,1152]{3,2,1,0:T(8,128)(2,1)} fusion(bf16[1,2,144,1152]{3,2,1,0:T(8,128)(2,1)} %bitcast.15, bf16[1,2,144,1152]{3,2,1,0:T(8,128)(2,1)S(1)} %bitcast.34), kind=kLoop, calls=%fused_computation.1 | loop fusion | flops 663552 | bytes 2654208 | tf_op jit(solution)/shard_map/stack | solution.py:487
  65.9 2.6 %collective-permute-done.14 = bf16[4,48,1152]{2,1,0:T(8,128)(2,1)S(1)} collective-permute-done((bf16[4,48,1152]{2,1,0:T(8,128)(2,1)S(1)}, bf16[4,48,1152]{2,1,0:T(8,128)(2,1)S(1)}, u32[]{:S(2)}, u32[]{:S(2)}) %collective-permute-start.14) | collective-permute-done | bytes 442400 | tf_op jit(solution)/shard_map/ppermute | solution.py:454
  68.5 2.1 %collective-permute-done.15 = bf16[4,48,1152]{2,1,0:T(8,128)(2,1)S(1)} collective-permute-done((bf16[4,48,1152]{2,1,0:T(8,128)(2,1)S(1)}, bf16[4,48,1152]{2,1,0:T(8,128)(2,1)S(1)}, u32[]{:S(2)}, u32[]{:S(2)}) %collective-permute-start.15) | collective-permute-done | bytes 442400 | tf_op jit(solution)/shard_map/ppermute | solution.py:454
  70.6 7.1 %collective-permute-done.16 = bf16[4,48,1152]{2,1,0:T(8,128)(2,1)S(1)} collective-permute-done((bf16[4,48,1152]{2,1,0:T(8,128)(2,1)S(1)}, bf16[4,48,1152]{2,1,0:T(8,128)(2,1)S(1)}, u32[]{:S(2)}, u32[]{:S(2)}) %collective-permute-start.16) | collective-permute-done | bytes 442400 | tf_op jit(solution)/shard_map/ppermute | solution.py:454
  78.0 5.7 %collective-permute-start.17 = (bf16[4,4,48,1152]{3,2,1,0:T(8,128)(2,1)S(1)}, bf16[4,4,48,1152]{3,2,1,0:T(8,128)(2,1)S(1)}, u32[]{:S(2)}, u32[]{:S(2)}) collective-permute-start(bf16[4,4,48,1152]{3,2,1,0:T(8,128)(2,1)S(1)} %pad_maximum_fusion.plane_ref), channel_id=1, source_target_pairs={{0,4},{4,0},{1,5},{5,1},{2,6},{6,2},{3,7},{7,3},{8,12},{12,8},{9,1... | collective-permute-start | bytes 5308424 | tf_op jit(solution)/shard_map/ppermute | solution.py:454
  85.5 21.1 %collective-permute-done.9.refs_3_ = bf16[2,2,144,1152]{3,2,1,0:T(8,128)(2,1)} collective-permute-done((bf16[2,2,144,1152]{3,2,1,0:T(8,128)(2,1)}, bf16[2,2,144,1152]{3,2,1,0:T(8,128)(2,1)}, u32[]{:S(2)}, u32[]{:S(2)}) %collective-permute-start.9) | collective-permute-done | bytes 1327136 | tf_op jit(solution)/shard_map/ppermute | solution.py:454
  106.6 2.2 %collective-permute-start.13 = (bf16[2,2,144,1152]{3,2,1,0:T(8,128)(2,1)}, bf16[2,2,144,1152]{3,2,1,0:T(8,128)(2,1)}, u32[]{:S(2)}, u32[]{:S(2)}) collective-permute-start(bf16[2,2,144,1152]{3,2,1,0:T(8,128)(2,1)} %collective-permute-done.9.refs_3_), channel_id=1, source_target_pairs={{0,4},{4,0},{1,5},{5,1},{2,6},{6,2},{3,7},{7,3},{8,12},{12,8},{9,1... | collective-permute-start | bytes 3981320 | tf_op jit(solution)/shard_map/ppermute | solution.py:454
  111.2 1.5 copy-done.2
  112.7 1.5 copy-done.5
  114.1 4.1 %mix.1 = (bf16[1152,128]{1,0:T(8,128)(2,1)S(1)}, bf16[1152,128]{1,0:T(8,128)(2,1)S(1)}, bf16[1152,128]{1,0:T(8,128)(2,1)S(1)}, bf16[1152,128]{1,0:T(8,128)(2,1)S(1)}) custom-call(s32[7]{0:T(128)S(1)} %stack.89.info_ref, bf16[4,4,48,1152]{3,2,1,0:T(8,128)(2,1)S(1)} %copy-done.2, bf16[4,4,48,1152]{3,2,1,0:T(8,128)(2,1)S(1)} %copy-done.5, ...), custom_call_target="tpu_custom_call" | custom-call | flops 4000000000 | bytes 4000000 | tf_op jit(solution)/shard_map/mix/pallas_call | solution.py:198
  119.7 4.9 %pieces_in_place.1 = (bf16[8,432,1152]{2,1,0:T(8,128)(2,1)S(1)}, bf16[1152,1152]{1,0:T(8,128)(2,1)S(1)}) custom-call(s32[7]{0:T(128)S(1)} %stack.89.info_ref, bf16[2,2,144,1152]{3,2,1,0:T(8,128)(2,1)} %pad_maximum_fusion.1.refs_0_, bf16[2,2,144,1152]{3,2,1,0:T(8,128)(2,1)} %collective-permute-done.8.refs_1_, ...), custom_call_target="tpu_custom_call" | custom-call | flops 3000000000 | bytes 20000000 | tf_op jit(solution)/shard_map/pieces_in_place/pallas_call | solution.py:241
  124.8 7.4 %collective-permute-done.19.refs_2_ = bf16[1152,128]{1,0:T(8,128)(2,1)S(1)} collective-permute-done((bf16[1152,128]{1,0:T(8,128)(2,1)S(1)}, bf16[1152,128]{1,0:T(8,128)(2,1)S(1)}, u32[]{:S(2)}, u32[]{:S(2)}) %collective-permute-start.19) | collective-permute-done | bytes 294944 | tf_op jit(solution)/shard_map/ppermute | solution.py:448
  133.2 11.1 %temporal.1 = (bf16[288,512]{1,0:T(8,128)(2,1)S(1)}, bf16[288,512]{1,0:T(8,128)(2,1)S(1)}, bf16[288,512]{1,0:T(8,128)(2,1)S(1)}, bf16[288,512]{1,0:T(8,128)(2,1)S(1)}) custom-call(s32[7]{0:T(128)S(1)} %stack.89.info_ref, f32[8,1152]{1,0:T(8,128)S(1)} %pad_maximum_fusion.6.gates_ref, bf16[8,432,1152]{2,1,0:T(8,128)(2,1)S(1)} %get-tuple-element.60.qkv_ref, ...), custom_call_target="tpu_custom_call" | custom-call | flops 17999998976 | bytes 12000000 | tf_op jit(solution)/shard_map/temporal/pallas_call | solution.py:362
  144.3 3.5 %collective-permute-start.21 = (bf16[288,512]{1,0:T(8,128)(2,1)S(1)}, bf16[288,512]{1,0:T(8,128)(2,1)S(1)}, u32[]{:S(2)}, u32[]{:S(2)}) collective-permute-start(bf16[288,512]{1,0:T(8,128)(2,1)S(1)} %get-tuple-element.71), channel_id=1, source_target_pairs={{0,0},{1,1},{2,18},{3,19},{16,2},{17,3},{18,16},{19,17},{4,4},{5,5... | collective-permute-start | bytes 884744 | tf_op jit(solution)/shard_map/ppermute | solution.py:497
  147.9 1.9 %collective-permute-start.23 = (bf16[288,512]{1,0:T(8,128)(2,1)S(1)}, bf16[288,512]{1,0:T(8,128)(2,1)S(1)}, u32[]{:S(2)}, u32[]{:S(2)}) collective-permute-start(bf16[288,512]{1,0:T(8,128)(2,1)S(1)} %get-tuple-element.73), channel_id=1, source_target_pairs={{0,2},{1,3},{2,16},{3,17},{16,0},{17,1},{18,18},{19,19},{4,6},{5,7... | collective-permute-start | bytes 884744 | tf_op jit(solution)/shard_map/ppermute | solution.py:497
  149.9 4.3 %collective-permute-start.24 = (bf16[288,512]{1,0:T(8,128)(2,1)S(1)}, bf16[288,512]{1,0:T(8,128)(2,1)S(1)}, u32[]{:S(2)}, u32[]{:S(2)}) collective-permute-start(bf16[288,512]{1,0:T(8,128)(2,1)S(1)} %get-tuple-element.74), channel_id=1, source_target_pairs={{0,3},{1,0},{2,17},{3,18},{16,1},{17,2},{18,19},{19,16},{4,7},{5,4... | collective-permute-start | bytes 884744 | tf_op jit(solution)/shard_map/ppermute | solution.py:497
  154.2 12.2 %collective-permute-done.21.refs_0_ = bf16[288,512]{1,0:T(8,128)(2,1)S(1)} collective-permute-done((bf16[288,512]{1,0:T(8,128)(2,1)S(1)}, bf16[288,512]{1,0:T(8,128)(2,1)S(1)}, u32[]{:S(2)}, u32[]{:S(2)}) %collective-permute-start.21) | collective-permute-done | bytes 294944 | tf_op jit(solution)/shard_map/ppermute | solution.py:497
  166.4 7.8 %collective-permute-done.22.refs_1_ = bf16[288,512]{1,0:T(8,128)(2,1)S(1)} collective-permute-done((bf16[288,512]{1,0:T(8,128)(2,1)S(1)}, bf16[288,512]{1,0:T(8,128)(2,1)S(1)}, u32[]{:S(2)}, u32[]{:S(2)}) %collective-permute-start.22) | collective-permute-done | bytes 294944 | tf_op jit(solution)/shard_map/ppermute | solution.py:497
  174.2 2.8 %collective-permute-done.24.refs_3_ = bf16[288,512]{1,0:T(8,128)(2,1)S(1)} collective-permute-done((bf16[288,512]{1,0:T(8,128)(2,1)S(1)}, bf16[288,512]{1,0:T(8,128)(2,1)S(1)}, u32[]{:S(2)}, u32[]{:S(2)}) %collective-permute-start.24) | collective-permute-done | bytes 294944 | tf_op jit(solution)/shard_map/ppermute | solution.py:497
  177.0 2.0 %place.1 = bf16[16,288,128]{2,1,0:T(8,128)(2,1)} custom-call(s32[7]{0:T(128)S(1)} %stack.89.info_ref, bf16[288,512]{1,0:T(8,128)(2,1)S(1)} %collective-permute-done.21.refs_0_, bf16[288,512]{1,0:T(8,128)(2,1)S(1)} %collective-permute-done.22.refs_1_, bf16[288,512]{1,0:T(8,128)(2,1)S(1)} %collective-permute-done.23.refs_2_, ...), custom_call_target="tpu_custom_call" | custom-call | tf_op jit(solution)/shard_map/place/pallas_call | solution.py:401
  (68 shorter events, 23.2 us)
Async XLA Ops:
  0.0 2.6 %copy-start = (bf16[288,1152]{1,0:T(8,128)(2,1)S(1)}, bf16[288,1152]{1,0:T(8,128)(2,1)}, u32[]{:S(2)}) copy-start(bf16[288,1152]{1,0:T(8,128)(2,1)} %param.10) | copy-start | bytes 1990660
  5.1 22.3 %collective-permute-start = (bf16[144,1152]{1,0:T(8,128)(2,1)S(1)}, bf16[144,1152]{1,0:T(8,128)(2,1)S(1)}, u32[]{:S(2)}, u32[]{:S(2)}) collective-permute-start(bf16[144,1152]{1,0:T(8,128)(2,1)S(1)} %bitcast_select_fusion), channel_id=1, source_target_pairs={{0,1},{1,2},{2,3},{3,0},{4,5},{5,6},{6,7},{7,4},{8,9},{9,10},{10,1... | collective-permute-start | bytes 995336 | tf_op jit(solution)/shard_map/ppermute | solution.py:448
  6.4 27.8 %collective-permute-start.1 = (bf16[144,1152]{1,0:T(8,128)(2,1)S(1)}, bf16[144,1152]{1,0:T(8,128)(2,1)S(1)}, u32[]{:S(2)}, u32[]{:S(2)}) collective-permute-start(bf16[144,1152]{1,0:T(8,128)(2,1)S(1)} %bitcast_select_fusion), channel_id=1, source_target_pairs={{0,2},{1,3},{2,0},{3,1},{4,6},{5,7},{6,4},{7,5},{8,10},{9,11},{10,... | collective-permute-start | bytes 995336 | tf_op jit(solution)/shard_map/ppermute | solution.py:448
  7.4 29.6 %collective-permute-start.2 = (bf16[144,1152]{1,0:T(8,128)(2,1)S(1)}, bf16[144,1152]{1,0:T(8,128)(2,1)S(1)}, u32[]{:S(2)}, u32[]{:S(2)}) collective-permute-start(bf16[144,1152]{1,0:T(8,128)(2,1)S(1)} %bitcast_select_fusion), channel_id=1, source_target_pairs={{0,3},{1,0},{2,1},{3,2},{4,7},{5,4},{6,5},{7,6},{8,11},{9,8},{10,9... | collective-permute-start | bytes 995336 | tf_op jit(solution)/shard_map/ppermute | solution.py:448
  37.1 9.9 %copy-start.7 = (bf16[2,144,1152]{2,1,0:T(8,128)(2,1)}, bf16[2,144,1152]{2,1,0:T(8,128)(2,1)S(1)}, u32[]{:S(2)}) copy-start(bf16[2,144,1152]{2,1,0:T(8,128)(2,1)S(1)} %pad_maximum_fusion.4) | copy-start | bytes 1990660
  37.1 16.2 %collective-permute-start.4 = (bf16[2,144,1152]{2,1,0:T(8,128)(2,1)S(1)}, bf16[2,144,1152]{2,1,0:T(8,128)(2,1)S(1)}, u32[]{:S(2)}, u32[]{:S(2)}) collective-permute-start(bf16[2,144,1152]{2,1,0:T(8,128)(2,1)S(1)} %pad_maximum_fusion.4), channel_id=1, source_target_pairs={{0,16},{8,24},{16,0},{24,8},{1,17},{9,25},{17,1},{25,9},{2,18},{10... | collective-permute-start | bytes 1990664 | tf_op jit(solution)/shard_map/ppermute | solution.py:454
  37.4 9.5 %copy-start.9 = (bf16[2,144,1152]{2,1,0:T(8,128)(2,1)}, bf16[2,144,1152]{2,1,0:T(8,128)(2,1)S(1)}, u32[]{:S(2)}) copy-start(bf16[2,144,1152]{2,1,0:T(8,128)(2,1)S(1)} %pad_maximum_fusion.3) | copy-start | bytes 1990660
  37.5 16.6 %collective-permute-start.3 = (bf16[2,144,1152]{2,1,0:T(8,128)(2,1)S(1)}, bf16[2,144,1152]{2,1,0:T(8,128)(2,1)}, u32[]{:S(2)}, u32[]{:S(2)}) collective-permute-start(bf16[2,144,1152]{2,1,0:T(8,128)(2,1)S(1)} %pad_maximum_fusion.3), channel_id=1, source_target_pairs={{0,8},{8,0},{16,24},{24,16},{1,9},{9,1},{17,25},{25,17},{2,10},{10... | collective-permute-start | bytes 1990664 | tf_op jit(solution)/shard_map/ppermute | solution.py:454
  38.7 8.2 %collective-permute-start.5 = (bf16[48,1152]{1,0:T(8,128)(2,1)S(1)}, bf16[48,1152]{1,0:T(8,128)(2,1)S(1)}, u32[]{:S(2)}, u32[]{:S(2)}) collective-permute-start(bf16[48,1152]{1,0:T(8,128)(2,1)S(1)} %constant_dynamic-slice_fusion), channel_id=1, source_target_pairs={{0,1},{1,2},{2,3},{3,0},{4,5},{5,6},{6,7},{7,4},{8,9},{9,10},{10,1... | collective-permute-start | bytes 331784 | tf_op jit(solution)/shard_map/ppermute | solution.py:448
  38.7 8.2 %collective-permute-start.6 = (bf16[48,1152]{1,0:T(8,128)(2,1)S(1)}, bf16[48,1152]{1,0:T(8,128)(2,1)S(1)}, u32[]{:S(2)}, u32[]{:S(2)}) collective-permute-start(bf16[48,1152]{1,0:T(8,128)(2,1)S(1)} %constant_dynamic-slice_fusion), channel_id=1, source_target_pairs={{0,2},{1,3},{2,0},{3,1},{4,6},{5,7},{6,4},{7,5},{8,10},{9,11},{10,... | collective-permute-start | bytes 331784 | tf_op jit(solution)/shard_map/ppermute | solution.py:448
  39.4 11.1 %collective-permute-start.7 = (bf16[48,1152]{1,0:T(8,128)(2,1)S(1)}, bf16[48,1152]{1,0:T(8,128)(2,1)S(1)}, u32[]{:S(2)}, u32[]{:S(2)}) collective-permute-start(bf16[48,1152]{1,0:T(8,128)(2,1)S(1)} %constant_dynamic-slice_fusion), channel_id=1, source_target_pairs={{0,3},{1,0},{2,1},{3,2},{4,7},{5,4},{6,5},{7,6},{8,11},{9,8},{10,9... | collective-permute-start | bytes 331784 | tf_op jit(solution)/shard_map/ppermute | solution.py:448
  54.1 57.1 %all-to-all-start = ((bf16[4,576,512]{2,1,0:T(8,128)(2,1)}), bf16[4,576,512]{2,1,0:T(8,128)(2,1)S(1)}, u32[]{:S(2)}, u32[]{:S(2)}) async-start(bf16[4,576,512]{2,1,0:T(8,128)(2,1)} %spatial_attention.3), calls=%async_computation | async-start | bytes 4718592 | tf_op jit(solution)/shard_map/all_to_all | solution.py:484
  57.9 2.8 %copy-start.8 = (bf16[2,144,1152]{2,1,0:T(8,128)(2,1)S(1)}, bf16[2,144,1152]{2,1,0:T(8,128)(2,1)}, u32[]{:S(2)}) copy-start(bf16[2,144,1152]{2,1,0:T(8,128)(2,1)} %copy-done.7) | copy-start | bytes 1990660
  57.9 2.8 %copy-start.12 = (bf16[2,144,1152]{2,1,0:T(8,128)(2,1)S(1)}, bf16[2,144,1152]{2,1,0:T(8,128)(2,1)}, u32[]{:S(2)}) copy-start(bf16[2,144,1152]{2,1,0:T(8,128)(2,1)} %copy-done.11) | copy-start | bytes 1990660
  58.0 10.5 %collective-permute-start.14 = (bf16[4,48,1152]{2,1,0:T(8,128)(2,1)S(1)}, bf16[4,48,1152]{2,1,0:T(8,128)(2,1)S(1)}, u32[]{:S(2)}, u32[]{:S(2)}) collective-permute-start(bf16[4,48,1152]{2,1,0:T(8,128)(2,1)S(1)} %get-tuple-element.76), channel_id=1, source_target_pairs={{0,8},{8,0},{16,24},{24,16},{1,9},{9,1},{17,25},{25,17},{2,10},{10... | collective-permute-start | bytes 1327112 | tf_op jit(solution)/shard_map/ppermute | solution.py:454
  59.3 11.3 %collective-permute-start.15 = (bf16[4,48,1152]{2,1,0:T(8,128)(2,1)S(1)}, bf16[4,48,1152]{2,1,0:T(8,128)(2,1)S(1)}, u32[]{:S(2)}, u32[]{:S(2)}) collective-permute-start(bf16[4,48,1152]{2,1,0:T(8,128)(2,1)S(1)} %get-tuple-element.76), channel_id=1, source_target_pairs={{0,16},{8,24},{16,0},{24,8},{1,17},{9,25},{17,1},{25,9},{2,18},{10... | collective-permute-start | bytes 1327112 | tf_op jit(solution)/shard_map/ppermute | solution.py:454
  59.7 18.0 %collective-permute-start.16 = (bf16[4,48,1152]{2,1,0:T(8,128)(2,1)S(1)}, bf16[4,48,1152]{2,1,0:T(8,128)(2,1)S(1)}, u32[]{:S(2)}, u32[]{:S(2)}) collective-permute-start(bf16[4,48,1152]{2,1,0:T(8,128)(2,1)S(1)} %get-tuple-element.76), channel_id=1, source_target_pairs={{0,24},{8,16},{16,8},{24,0},{1,25},{9,17},{17,9},{25,1},{2,26},{10... | collective-permute-start | bytes 1327112 | tf_op jit(solution)/shard_map/ppermute | solution.py:454
  62.0 44.6 %collective-permute-start.9 = (bf16[2,2,144,1152]{3,2,1,0:T(8,128)(2,1)}, bf16[2,2,144,1152]{3,2,1,0:T(8,128)(2,1)}, u32[]{:S(2)}, u32[]{:S(2)}) collective-permute-start(bf16[2,2,144,1152]{3,2,1,0:T(8,128)(2,1)} %pad_maximum_fusion.2.refs_2_), channel_id=1, source_target_pairs={{0,8},{8,0},{16,24},{24,16},{1,9},{9,1},{17,25},{25,17},{2,10},{10... | collective-permute-start | bytes 3981320 | tf_op jit(solution)/shard_map/ppermute | solution.py:454
  65.5 43.2 %collective-permute-start.8 = (bf16[2,2,144,1152]{3,2,1,0:T(8,128)(2,1)}, bf16[2,2,144,1152]{3,2,1,0:T(8,128)(2,1)}, u32[]{:S(2)}, u32[]{:S(2)}) collective-permute-start(bf16[2,2,144,1152]{3,2,1,0:T(8,128)(2,1)} %pad_maximum_fusion.1.refs_0_), channel_id=1, source_target_pairs={{0,16},{8,24},{16,0},{24,8},{1,17},{9,25},{17,1},{25,9},{2,18},{10... | collective-permute-start | bytes 3981320 | tf_op jit(solution)/shard_map/ppermute | solution.py:454
  77.8 32.1 %copy-start.13 = (f32[2,4,1152]{2,1,0:T(4,128)S(1)}, f32[2,4,1152]{2,1,0:T(4,128)}, u32[]{:S(2)}) copy-start(f32[2,4,1152]{2,1,0:T(4,128)} %param.13) | copy-start | bytes 110596
  78.0 31.9 %collective-permute-start.17 = (bf16[4,4,48,1152]{3,2,1,0:T(8,128)(2,1)S(1)}, bf16[4,4,48,1152]{3,2,1,0:T(8,128)(2,1)S(1)}, u32[]{:S(2)}, u32[]{:S(2)}) collective-permute-start(bf16[4,4,48,1152]{3,2,1,0:T(8,128)(2,1)S(1)} %pad_maximum_fusion.plane_ref), channel_id=1, source_target_pairs={{0,4},{4,0},{1,5},{5,1},{2,6},{6,2},{3,7},{7,3},{8,12},{12,8},{9,1... | collective-permute-start | bytes 5308424 | tf_op jit(solution)/shard_map/ppermute | solution.py:454
  85.0 33.7 %collective-permute-start.12 = (bf16[2,2,144,1152]{3,2,1,0:T(8,128)(2,1)}, bf16[2,2,144,1152]{3,2,1,0:T(8,128)(2,1)}, u32[]{:S(2)}, u32[]{:S(2)}) collective-permute-start(bf16[2,2,144,1152]{3,2,1,0:T(8,128)(2,1)} %pad_maximum_fusion.2.refs_2_), channel_id=1, source_target_pairs={{0,4},{4,0},{1,5},{5,1},{2,6},{6,2},{3,7},{7,3},{8,12},{12,8},{9,1... | collective-permute-start | bytes 3981320 | tf_op jit(solution)/shard_map/ppermute | solution.py:454
  85.0 34.7 %collective-permute-start.10 = (bf16[2,2,144,1152]{3,2,1,0:T(8,128)(2,1)}, bf16[2,2,144,1152]{3,2,1,0:T(8,128)(2,1)}, u32[]{:S(2)}, u32[]{:S(2)}) collective-permute-start(bf16[2,2,144,1152]{3,2,1,0:T(8,128)(2,1)} %pad_maximum_fusion.1.refs_0_), channel_id=1, source_target_pairs={{0,4},{4,0},{1,5},{5,1},{2,6},{6,2},{3,7},{7,3},{8,12},{12,8},{9,1... | collective-permute-start | bytes 3981320 | tf_op jit(solution)/shard_map/ppermute | solution.py:454
  106.6 13.1 %collective-permute-start.13 = (bf16[2,2,144,1152]{3,2,1,0:T(8,128)(2,1)}, bf16[2,2,144,1152]{3,2,1,0:T(8,128)(2,1)}, u32[]{:S(2)}, u32[]{:S(2)}) collective-permute-start(bf16[2,2,144,1152]{3,2,1,0:T(8,128)(2,1)} %collective-permute-done.9.refs_3_), channel_id=1, source_target_pairs={{0,4},{4,0},{1,5},{5,1},{2,6},{6,2},{3,7},{7,3},{8,12},{12,8},{9,1... | collective-permute-start | bytes 3981320 | tf_op jit(solution)/shard_map/ppermute | solution.py:454
  108.7 10.9 %collective-permute-start.11 = (bf16[2,2,144,1152]{3,2,1,0:T(8,128)(2,1)}, bf16[2,2,144,1152]{3,2,1,0:T(8,128)(2,1)}, u32[]{:S(2)}, u32[]{:S(2)}) collective-permute-start(bf16[2,2,144,1152]{3,2,1,0:T(8,128)(2,1)} %collective-permute-done.8.refs_1_), channel_id=1, source_target_pairs={{0,4},{4,0},{1,5},{5,1},{2,6},{6,2},{3,7},{7,3},{8,12},{12,8},{9,1... | collective-permute-start | bytes 3981320 | tf_op jit(solution)/shard_map/ppermute | solution.py:454
  118.2 6.6 %collective-permute-start.18 = (bf16[1152,128]{1,0:T(8,128)(2,1)S(1)}, bf16[1152,128]{1,0:T(8,128)(2,1)S(1)}, u32[]{:S(2)}, u32[]{:S(2)}) collective-permute-start(bf16[1152,128]{1,0:T(8,128)(2,1)S(1)} %get-tuple-element.68), channel_id=1, source_target_pairs={{0,4},{4,8},{8,12},{12,0},{1,5},{5,9},{9,13},{13,1},{2,6},{6,10},{... | collective-permute-start | bytes 884744 | tf_op jit(solution)/shard_map/ppermute | solution.py:448
  118.7 13.4 %collective-permute-start.19 = (bf16[1152,128]{1,0:T(8,128)(2,1)S(1)}, bf16[1152,128]{1,0:T(8,128)(2,1)S(1)}, u32[]{:S(2)}, u32[]{:S(2)}) collective-permute-start(bf16[1152,128]{1,0:T(8,128)(2,1)S(1)} %get-tuple-element.69), channel_id=1, source_target_pairs={{0,8},{4,12},{8,0},{12,4},{1,9},{5,13},{9,1},{13,5},{2,10},{6,14},... | collective-permute-start | bytes 884744 | tf_op jit(solution)/shard_map/ppermute | solution.py:448
  119.6 13.6 %collective-permute-start.20 = (bf16[1152,128]{1,0:T(8,128)(2,1)S(1)}, bf16[1152,128]{1,0:T(8,128)(2,1)S(1)}, u32[]{:S(2)}, u32[]{:S(2)}) collective-permute-start(bf16[1152,128]{1,0:T(8,128)(2,1)S(1)} %get-tuple-element.70), channel_id=1, source_target_pairs={{0,12},{4,0},{8,4},{12,8},{1,13},{5,1},{9,5},{13,9},{2,14},{6,2},{... | collective-permute-start | bytes 884744 | tf_op jit(solution)/shard_map/ppermute | solution.py:448
  144.3 22.0 %collective-permute-start.21 = (bf16[288,512]{1,0:T(8,128)(2,1)S(1)}, bf16[288,512]{1,0:T(8,128)(2,1)S(1)}, u32[]{:S(2)}, u32[]{:S(2)}) collective-permute-start(bf16[288,512]{1,0:T(8,128)(2,1)S(1)} %get-tuple-element.71), channel_id=1, source_target_pairs={{0,0},{1,1},{2,18},{3,19},{16,2},{17,3},{18,16},{19,17},{4,4},{5,5... | collective-permute-start | bytes 884744 | tf_op jit(solution)/shard_map/ppermute | solution.py:497
  147.9 26.3 %collective-permute-start.22 = (bf16[288,512]{1,0:T(8,128)(2,1)S(1)}, bf16[288,512]{1,0:T(8,128)(2,1)S(1)}, u32[]{:S(2)}, u32[]{:S(2)}) collective-permute-start(bf16[288,512]{1,0:T(8,128)(2,1)S(1)} %get-tuple-element.72), channel_id=1, source_target_pairs={{0,1},{1,2},{2,19},{3,16},{16,3},{17,0},{18,17},{19,18},{4,5},{5,6... | collective-permute-start | bytes 884744 | tf_op jit(solution)/shard_map/ppermute | solution.py:497
  147.9 26.3 %collective-permute-start.23 = (bf16[288,512]{1,0:T(8,128)(2,1)S(1)}, bf16[288,512]{1,0:T(8,128)(2,1)S(1)}, u32[]{:S(2)}, u32[]{:S(2)}) collective-permute-start(bf16[288,512]{1,0:T(8,128)(2,1)S(1)} %get-tuple-element.73), channel_id=1, source_target_pairs={{0,2},{1,3},{2,16},{3,17},{16,0},{17,1},{18,18},{19,19},{4,6},{5,7... | collective-permute-start | bytes 884744 | tf_op jit(solution)/shard_map/ppermute | solution.py:497
  149.9 27.1 %collective-permute-start.24 = (bf16[288,512]{1,0:T(8,128)(2,1)S(1)}, bf16[288,512]{1,0:T(8,128)(2,1)S(1)}, u32[]{:S(2)}, u32[]{:S(2)}) collective-permute-start(bf16[288,512]{1,0:T(8,128)(2,1)S(1)} %get-tuple-element.74), channel_id=1, source_target_pairs={{0,3},{1,0},{2,17},{3,18},{16,1},{17,2},{18,19},{19,16},{4,7},{5,4... | collective-permute-start | bytes 884744 | tf_op jit(solution)/shard_map/ppermute | solution.py:497
  (8 other events, 12.0 us)

commit v4 on v3

--- a/solution.py
+++ b/solution.py
@@ -363,7 +363,7 @@
         functools.partial(temporal_kernel, sizes),
         grid_spec=pltpu.PrefetchScalarGridSpec(
             num_scalar_prefetch=1,
-            grid=(heads,),
+            grid=(heads // 2,),
             in_specs=[vmem] * (3 + ranks),
             out_specs=[vmem] * count,
             scratch_shapes=[pltpu.VMEM((features, rows), BF16)] * 3,

time: 179 us -> 179 us (level)
  no operation moved by 1% of the time
where the time goes in v4:
time: 179 us; the launch traced here: 178 us
  waiting for transfers between devices  80.3 us (45%)
  Pallas kernels  43.2 us (24%)
  starting transfers between devices  36 us (20%)
  local copies, waits for them, and re-layouts  13.5 us (8%)
  other arithmetic  5.22 us (3%)
    ppermute x12, waiting for transfers between devices, swap(): return lax.ppermute(array, axis, [(i, i ^ bit) for i in range(size)])  35.7 us
    ppermute x4, waiting for transfers between devices, on_device(): lax.ppermute(result[part * heads + step], ('outer', 'clip', 'head'), rout...  22.8 us
    ppermute x9, waiting for transfers between devices, send(): lax.ppermute(array, axis, [(i, (i + step) % size) for i in range(size)])  21.8 us
    pallas_call x2, Pallas kernels, spatial_attention(): pl.pallas_call(functools.partial(spatial_kernel, ranks, first), grid_spec...  20.4 us
    ppermute x12, starting transfers between devices, swap(): return lax.ppermute(array, axis, [(i, i ^ bit) for i in range(size)])  15.5 us
    pallas_call x1, Pallas kernels, temporal(): pl.pallas_call(functools.partial(temporal_kernel, sizes), grid_spec=pltpu...  10.5 us
    ppermute x4, starting transfers between devices, on_device(): lax.ppermute(result[part * heads + step], ('outer', 'clip', 'head'), rout...  9.8 us
    unnamed x28, local copies, waits for them, and re-layouts  9.57 us
  transfers between devices with their start and end apart: 26, of which 14 were waited for; matrix products, arithmetic and copies ran while one was open for 2% of the time, Pallas kernels for 17%

profile of v4, /device:TPU:13, one launch (start us, length us, event | category | flops | bytes accessed | tf_op | source)
XLA Modules:
  0.0 178.4 jit_solution(5324963535567525238)
XLA Ops:
  0.0 1.4 dynamic_slice.20
  3.8 1.3 stack.89.info_ref
  7.4 1.4 collective-permute-start.2
  8.8 2.0 %copy-done.3 = bf16[3,2,1024,288]{2,3,1,0:T(8,128)(2,1)S(1)} copy-done((bf16[3,2,1024,288]{2,3,1,0:T(8,128)(2,1)S(1)}, bf16[3,2,1024,288]{2,3,1,0:T(8,128)(2,1)}, u32[]{:S(2)}) %copy-start.3) | copy-done | bytes 3538968
  12.1 1.3 arrange.1
  13.4 13.9 %spatial_attention.2.refs_0_ = bf16[3,288,512]{2,1,0:T(8,128)(2,1)S(1)} custom-call(s32[7]{0:T(128)S(1)} %stack.89.info_ref, bf16[4,2,2,144,256]{4,3,2,1,0:T(8,128)(2,1)S(1)} %get-tuple-element.42.query_ref, bf16[2,2,1024,144]{3,2,1,0:T(8,128)(2,1)S(1)} %get-tuple-element.43.key_ref, bf16[2,2,160,1024]{3,2,1,0:T(8,128)(2,1)S(1)} %get-tuple-element.44.value_ref), custom_call_target="tpu_custom_call" | custom-call | flops 14000000000 | bytes 5000000 | tf_op jit(solution)/shard_map/spatial_attention/pallas_call | solution.py:149
  27.4 6.8 %collective-permute-done.1 = bf16[144,1152]{1,0:T(8,128)(2,1)S(1)} collective-permute-done((bf16[144,1152]{1,0:T(8,128)(2,1)S(1)}, bf16[144,1152]{1,0:T(8,128)(2,1)S(1)}, u32[]{:S(2)}, u32[]{:S(2)}) %collective-permute-start.1) | collective-permute-done | bytes 331808 | tf_op jit(solution)/shard_map/ppermute | solution.py:448
  34.2 2.8 %collective-permute-done.2 = bf16[144,1152]{1,0:T(8,128)(2,1)S(1)} collective-permute-done((bf16[144,1152]{1,0:T(8,128)(2,1)S(1)}, bf16[144,1152]{1,0:T(8,128)(2,1)S(1)}, u32[]{:S(2)}, u32[]{:S(2)}) %collective-permute-start.2) | collective-permute-done | bytes 331808 | tf_op jit(solution)/shard_map/ppermute | solution.py:448
  40.5 6.5 %spatial_attention.3 = bf16[4,576,512]{2,1,0:T(8,128)(2,1)} custom-call(s32[7]{0:T(128)S(1)} %stack.89.info_ref, bf16[4,2,2,144,256]{4,3,2,1,0:T(8,128)(2,1)S(1)} %get-tuple-element.42.query_ref, bf16[2,2,1024,144]{3,2,1,0:T(8,128)(2,1)S(1)} %get-tuple-element.43.key_ref, bf16[2,2,160,1024]{3,2,1,0:T(8,128)(2,1)S(1)} %get-tuple-element.44.value_ref, ...), custom_call_target="tpu_custom_call" | custom-call | flops 14000000000 | bytes 5000000 | tf_op jit(solution)/shard_map/spatial_attention/pallas_call | solution.py:149
  47.0 3.5 %collective-permute-done.7 = bf16[48,1152]{1,0:T(8,128)(2,1)S(1)} collective-permute-done((bf16[48,1152]{1,0:T(8,128)(2,1)S(1)}, bf16[48,1152]{1,0:T(8,128)(2,1)S(1)}, u32[]{:S(2)}, u32[]{:S(2)}) %collective-permute-start.7) | collective-permute-done | bytes 110624 | tf_op jit(solution)/shard_map/ppermute | solution.py:448
  50.5 2.7 %collective-permute-done.4 = bf16[2,144,1152]{2,1,0:T(8,128)(2,1)S(1)} collective-permute-done((bf16[2,144,1152]{2,1,0:T(8,128)(2,1)S(1)}, bf16[2,144,1152]{2,1,0:T(8,128)(2,1)S(1)}, u32[]{:S(2)}, u32[]{:S(2)}) %collective-permute-start.4) | collective-permute-done | bytes 663584 | tf_op jit(solution)/shard_map/ppermute | solution.py:454
  54.1 3.8 %all-to-all-start = ((bf16[4,576,512]{2,1,0:T(8,128)(2,1)}), bf16[4,576,512]{2,1,0:T(8,128)(2,1)S(1)}, u32[]{:S(2)}, u32[]{:S(2)}) async-start(bf16[4,576,512]{2,1,0:T(8,128)(2,1)} %spatial_attention.3), calls=%async_computation | async-start | bytes 4718592 | tf_op jit(solution)/shard_map/all_to_all | solution.py:484
  63.2 2.3 %pad_maximum_fusion.1.refs_0_ = bf16[2,2,144,1152]{3,2,1,0:T(8,128)(2,1)} fusion(bf16[1,2,144,1152]{3,2,1,0:T(8,128)(2,1)} %bitcast.15, bf16[1,2,144,1152]{3,2,1,0:T(8,128)(2,1)S(1)} %bitcast.34), kind=kLoop, calls=%fused_computation.1 | loop fusion | flops 663552 | bytes 2654208 | tf_op jit(solution)/shard_map/stack | solution.py:487
  65.9 2.6 %collective-permute-done.14 = bf16[4,48,1152]{2,1,0:T(8,128)(2,1)S(1)} collective-permute-done((bf16[4,48,1152]{2,1,0:T(8,128)(2,1)S(1)}, bf16[4,48,1152]{2,1,0:T(8,128)(2,1)S(1)}, u32[]{:S(2)}, u32[]{:S(2)}) %collective-permute-start.14) | collective-permute-done | bytes 442400 | tf_op jit(solution)/shard_map/ppermute | solution.py:454
  68.5 2.1 %collective-permute-done.15 = bf16[4,48,1152]{2,1,0:T(8,128)(2,1)S(1)} collective-permute-done((bf16[4,48,1152]{2,1,0:T(8,128)(2,1)S(1)}, bf16[4,48,1152]{2,1,0:T(8,128)(2,1)S(1)}, u32[]{:S(2)}, u32[]{:S(2)}) %collective-permute-start.15) | collective-permute-done | bytes 442400 | tf_op jit(solution)/shard_map/ppermute | solution.py:454
  70.6 7.1 %collective-permute-done.16 = bf16[4,48,1152]{2,1,0:T(8,128)(2,1)S(1)} collective-permute-done((bf16[4,48,1152]{2,1,0:T(8,128)(2,1)S(1)}, bf16[4,48,1152]{2,1,0:T(8,128)(2,1)S(1)}, u32[]{:S(2)}, u32[]{:S(2)}) %collective-permute-start.16) | collective-permute-done | bytes 442400 | tf_op jit(solution)/shard_map/ppermute | solution.py:454
  78.0 5.7 %collective-permute-start.17 = (bf16[4,4,48,1152]{3,2,1,0:T(8,128)(2,1)S(1)}, bf16[4,4,48,1152]{3,2,1,0:T(8,128)(2,1)S(1)}, u32[]{:S(2)}, u32[]{:S(2)}) collective-permute-start(bf16[4,4,48,1152]{3,2,1,0:T(8,128)(2,1)S(1)} %pad_maximum_fusion.plane_ref), channel_id=1, source_target_pairs={{0,4},{4,0},{1,5},{5,1},{2,6},{6,2},{3,7},{7,3},{8,12},{12,8},{9,1... | collective-permute-start | bytes 5308424 | tf_op jit(solution)/shard_map/ppermute | solution.py:454
  85.5 21.1 %collective-permute-done.9.refs_3_ = bf16[2,2,144,1152]{3,2,1,0:T(8,128)(2,1)} collective-permute-done((bf16[2,2,144,1152]{3,2,1,0:T(8,128)(2,1)}, bf16[2,2,144,1152]{3,2,1,0:T(8,128)(2,1)}, u32[]{:S(2)}, u32[]{:S(2)}) %collective-permute-start.9) | collective-permute-done | bytes 1327136 | tf_op jit(solution)/shard_map/ppermute | solution.py:454
  106.6 2.2 %collective-permute-start.13 = (bf16[2,2,144,1152]{3,2,1,0:T(8,128)(2,1)}, bf16[2,2,144,1152]{3,2,1,0:T(8,128)(2,1)}, u32[]{:S(2)}, u32[]{:S(2)}) collective-permute-start(bf16[2,2,144,1152]{3,2,1,0:T(8,128)(2,1)} %collective-permute-done.9.refs_3_), channel_id=1, source_target_pairs={{0,4},{4,0},{1,5},{5,1},{2,6},{6,2},{3,7},{7,3},{8,12},{12,8},{9,1... | collective-permute-start | bytes 3981320 | tf_op jit(solution)/shard_map/ppermute | solution.py:454
  111.2 1.5 copy-done.2
  112.7 1.5 copy-done.5
  114.1 4.1 %mix.1 = (bf16[1152,128]{1,0:T(8,128)(2,1)S(1)}, bf16[1152,128]{1,0:T(8,128)(2,1)S(1)}, bf16[1152,128]{1,0:T(8,128)(2,1)S(1)}, bf16[1152,128]{1,0:T(8,128)(2,1)S(1)}) custom-call(s32[7]{0:T(128)S(1)} %stack.89.info_ref, bf16[4,4,48,1152]{3,2,1,0:T(8,128)(2,1)S(1)} %copy-done.2, bf16[4,4,48,1152]{3,2,1,0:T(8,128)(2,1)S(1)} %copy-done.5, ...), custom_call_target="tpu_custom_call" | custom-call | flops 4000000000 | bytes 4000000 | tf_op jit(solution)/shard_map/mix/pallas_call | solution.py:198
  119.7 4.9 %pieces_in_place.1 = (bf16[8,432,1152]{2,1,0:T(8,128)(2,1)S(1)}, bf16[1152,1152]{1,0:T(8,128)(2,1)S(1)}) custom-call(s32[7]{0:T(128)S(1)} %stack.89.info_ref, bf16[2,2,144,1152]{3,2,1,0:T(8,128)(2,1)} %pad_maximum_fusion.1.refs_0_, bf16[2,2,144,1152]{3,2,1,0:T(8,128)(2,1)} %collective-permute-done.8.refs_1_, ...), custom_call_target="tpu_custom_call" | custom-call | flops 3000000000 | bytes 20000000 | tf_op jit(solution)/shard_map/pieces_in_place/pallas_call | solution.py:241
  124.8 7.4 %collective-permute-done.19.refs_2_ = bf16[1152,128]{1,0:T(8,128)(2,1)S(1)} collective-permute-done((bf16[1152,128]{1,0:T(8,128)(2,1)S(1)}, bf16[1152,128]{1,0:T(8,128)(2,1)S(1)}, u32[]{:S(2)}, u32[]{:S(2)}) %collective-permute-start.19) | collective-permute-done | bytes 294944 | tf_op jit(solution)/shard_map/ppermute | solution.py:448
  133.2 10.5 %temporal.1 = (bf16[288,512]{1,0:T(8,128)(2,1)S(1)}, bf16[288,512]{1,0:T(8,128)(2,1)S(1)}, bf16[288,512]{1,0:T(8,128)(2,1)S(1)}, bf16[288,512]{1,0:T(8,128)(2,1)S(1)}) custom-call(s32[7]{0:T(128)S(1)} %stack.89.info_ref, f32[8,1152]{1,0:T(8,128)S(1)} %pad_maximum_fusion.6.gates_ref, bf16[8,432,1152]{2,1,0:T(8,128)(2,1)S(1)} %get-tuple-element.60.qkv_ref, ...), custom_call_target="tpu_custom_call" | custom-call | flops 17999998976 | bytes 12000000 | tf_op jit(solution)/shard_map/temporal/pallas_call | solution.py:362
  143.7 3.5 %collective-permute-start.21 = (bf16[288,512]{1,0:T(8,128)(2,1)S(1)}, bf16[288,512]{1,0:T(8,128)(2,1)S(1)}, u32[]{:S(2)}, u32[]{:S(2)}) collective-permute-start(bf16[288,512]{1,0:T(8,128)(2,1)S(1)} %get-tuple-element.71), channel_id=1, source_target_pairs={{0,0},{1,1},{2,18},{3,19},{16,2},{17,3},{18,16},{19,17},{4,4},{5,5... | collective-permute-start | bytes 884744 | tf_op jit(solution)/shard_map/ppermute | solution.py:497
  147.3 1.9 %collective-permute-start.23 = (bf16[288,512]{1,0:T(8,128)(2,1)S(1)}, bf16[288,512]{1,0:T(8,128)(2,1)S(1)}, u32[]{:S(2)}, u32[]{:S(2)}) collective-permute-start(bf16[288,512]{1,0:T(8,128)(2,1)S(1)} %get-tuple-element.73), channel_id=1, source_target_pairs={{0,2},{1,3},{2,16},{3,17},{16,0},{17,1},{18,18},{19,19},{4,6},{5,7... | collective-permute-start | bytes 884744 | tf_op jit(solution)/shard_map/ppermute | solution.py:497
  149.2 4.3 %collective-permute-start.24 = (bf16[288,512]{1,0:T(8,128)(2,1)S(1)}, bf16[288,512]{1,0:T(8,128)(2,1)S(1)}, u32[]{:S(2)}, u32[]{:S(2)}) collective-permute-start(bf16[288,512]{1,0:T(8,128)(2,1)S(1)} %get-tuple-element.74), channel_id=1, source_target_pairs={{0,3},{1,0},{2,17},{3,18},{16,1},{17,2},{18,19},{19,16},{4,7},{5,4... | collective-permute-start | bytes 884744 | tf_op jit(solution)/shard_map/ppermute | solution.py:497
  153.5 12.2 %collective-permute-done.21.refs_0_ = bf16[288,512]{1,0:T(8,128)(2,1)S(1)} collective-permute-done((bf16[288,512]{1,0:T(8,128)(2,1)S(1)}, bf16[288,512]{1,0:T(8,128)(2,1)S(1)}, u32[]{:S(2)}, u32[]{:S(2)}) %collective-permute-start.21) | collective-permute-done | bytes 294944 | tf_op jit(solution)/shard_map/ppermute | solution.py:497
  165.7 7.8 %collective-permute-done.22.refs_1_ = bf16[288,512]{1,0:T(8,128)(2,1)S(1)} collective-permute-done((bf16[288,512]{1,0:T(8,128)(2,1)S(1)}, bf16[288,512]{1,0:T(8,128)(2,1)S(1)}, u32[]{:S(2)}, u32[]{:S(2)}) %collective-permute-start.22) | collective-permute-done | bytes 294944 | tf_op jit(solution)/shard_map/ppermute | solution.py:497
  173.6 2.8 %collective-permute-done.24.refs_3_ = bf16[288,512]{1,0:T(8,128)(2,1)S(1)} collective-permute-done((bf16[288,512]{1,0:T(8,128)(2,1)S(1)}, bf16[288,512]{1,0:T(8,128)(2,1)S(1)}, u32[]{:S(2)}, u32[]{:S(2)}) %collective-permute-start.24) | collective-permute-done | bytes 294944 | tf_op jit(solution)/shard_map/ppermute | solution.py:497
  176.3 2.0 %place.1 = bf16[16,288,128]{2,1,0:T(8,128)(2,1)} custom-call(s32[7]{0:T(128)S(1)} %stack.89.info_ref, bf16[288,512]{1,0:T(8,128)(2,1)S(1)} %collective-permute-done.21.refs_0_, bf16[288,512]{1,0:T(8,128)(2,1)S(1)} %collective-permute-done.22.refs_1_, bf16[288,512]{1,0:T(8,128)(2,1)S(1)} %collective-permute-done.23.refs_2_, ...), custom_call_target="tpu_custom_call" | custom-call | tf_op jit(solution)/shard_map/place/pallas_call | solution.py:401
  (68 shorter events, 23.2 us)
Async XLA Ops:
  0.0 2.6 %copy-start = (bf16[288,1152]{1,0:T(8,128)(2,1)S(1)}, bf16[288,1152]{1,0:T(8,128)(2,1)}, u32[]{:S(2)}) copy-start(bf16[288,1152]{1,0:T(8,128)(2,1)} %param.10) | copy-start | bytes 1990660
  5.1 22.3 %collective-permute-start = (bf16[144,1152]{1,0:T(8,128)(2,1)S(1)}, bf16[144,1152]{1,0:T(8,128)(2,1)S(1)}, u32[]{:S(2)}, u32[]{:S(2)}) collective-permute-start(bf16[144,1152]{1,0:T(8,128)(2,1)S(1)} %bitcast_select_fusion), channel_id=1, source_target_pairs={{0,1},{1,2},{2,3},{3,0},{4,5},{5,6},{6,7},{7,4},{8,9},{9,10},{10,1... | collective-permute-start | bytes 995336 | tf_op jit(solution)/shard_map/ppermute | solution.py:448
  6.4 27.8 %collective-permute-start.1 = (bf16[144,1152]{1,0:T(8,128)(2,1)S(1)}, bf16[144,1152]{1,0:T(8,128)(2,1)S(1)}, u32[]{:S(2)}, u32[]{:S(2)}) collective-permute-start(bf16[144,1152]{1,0:T(8,128)(2,1)S(1)} %bitcast_select_fusion), channel_id=1, source_target_pairs={{0,2},{1,3},{2,0},{3,1},{4,6},{5,7},{6,4},{7,5},{8,10},{9,11},{10,... | collective-permute-start | bytes 995336 | tf_op jit(solution)/shard_map/ppermute | solution.py:448
  7.4 29.6 %collective-permute-start.2 = (bf16[144,1152]{1,0:T(8,128)(2,1)S(1)}, bf16[144,1152]{1,0:T(8,128)(2,1)S(1)}, u32[]{:S(2)}, u32[]{:S(2)}) collective-permute-start(bf16[144,1152]{1,0:T(8,128)(2,1)S(1)} %bitcast_select_fusion), channel_id=1, source_target_pairs={{0,3},{1,0},{2,1},{3,2},{4,7},{5,4},{6,5},{7,6},{8,11},{9,8},{10,9... | collective-permute-start | bytes 995336 | tf_op jit(solution)/shard_map/ppermute | solution.py:448
  37.1 9.9 %copy-start.7 = (bf16[2,144,1152]{2,1,0:T(8,128)(2,1)}, bf16[2,144,1152]{2,1,0:T(8,128)(2,1)S(1)}, u32[]{:S(2)}) copy-start(bf16[2,144,1152]{2,1,0:T(8,128)(2,1)S(1)} %pad_maximum_fusion.4) | copy-start | bytes 1990660
  37.1 16.2 %collective-permute-start.4 = (bf16[2,144,1152]{2,1,0:T(8,128)(2,1)S(1)}, bf16[2,144,1152]{2,1,0:T(8,128)(2,1)S(1)}, u32[]{:S(2)}, u32[]{:S(2)}) collective-permute-start(bf16[2,144,1152]{2,1,0:T(8,128)(2,1)S(1)} %pad_maximum_fusion.4), channel_id=1, source_target_pairs={{0,16},{8,24},{16,0},{24,8},{1,17},{9,25},{17,1},{25,9},{2,18},{10... | collective-permute-start | bytes 1990664 | tf_op jit(solution)/shard_map/ppermute | solution.py:454
  37.4 9.5 %copy-start.9 = (bf16[2,144,1152]{2,1,0:T(8,128)(2,1)}, bf16[2,144,1152]{2,1,0:T(8,128)(2,1)S(1)}, u32[]{:S(2)}) copy-start(bf16[2,144,1152]{2,1,0:T(8,128)(2,1)S(1)} %pad_maximum_fusion.3) | copy-start | bytes 1990660
  37.5 16.6 %collective-permute-start.3 = (bf16[2,144,1152]{2,1,0:T(8,128)(2,1)S(1)}, bf16[2,144,1152]{2,1,0:T(8,128)(2,1)}, u32[]{:S(2)}, u32[]{:S(2)}) collective-permute-start(bf16[2,144,1152]{2,1,0:T(8,128)(2,1)S(1)} %pad_maximum_fusion.3), channel_id=1, source_target_pairs={{0,8},{8,0},{16,24},{24,16},{1,9},{9,1},{17,25},{25,17},{2,10},{10... | collective-permute-start | bytes 1990664 | tf_op jit(solution)/shard_map/ppermute | solution.py:454
  38.7 8.2 %collective-permute-start.5 = (bf16[48,1152]{1,0:T(8,128)(2,1)S(1)}, bf16[48,1152]{1,0:T(8,128)(2,1)S(1)}, u32[]{:S(2)}, u32[]{:S(2)}) collective-permute-start(bf16[48,1152]{1,0:T(8,128)(2,1)S(1)} %constant_dynamic-slice_fusion), channel_id=1, source_target_pairs={{0,1},{1,2},{2,3},{3,0},{4,5},{5,6},{6,7},{7,4},{8,9},{9,10},{10,1... | collective-permute-start | bytes 331784 | tf_op jit(solution)/shard_map/ppermute | solution.py:448
  38.7 8.2 %collective-permute-start.6 = (bf16[48,1152]{1,0:T(8,128)(2,1)S(1)}, bf16[48,1152]{1,0:T(8,128)(2,1)S(1)}, u32[]{:S(2)}, u32[]{:S(2)}) collective-permute-start(bf16[48,1152]{1,0:T(8,128)(2,1)S(1)} %constant_dynamic-slice_fusion), channel_id=1, source_target_pairs={{0,2},{1,3},{2,0},{3,1},{4,6},{5,7},{6,4},{7,5},{8,10},{9,11},{10,... | collective-permute-start | bytes 331784 | tf_op jit(solution)/shard_map/ppermute | solution.py:448
  39.4 11.1 %collective-permute-start.7 = (bf16[48,1152]{1,0:T(8,128)(2,1)S(1)}, bf16[48,1152]{1,0:T(8,128)(2,1)S(1)}, u32[]{:S(2)}, u32[]{:S(2)}) collective-permute-start(bf16[48,1152]{1,0:T(8,128)(2,1)S(1)} %constant_dynamic-slice_fusion), channel_id=1, source_target_pairs={{0,3},{1,0},{2,1},{3,2},{4,7},{5,4},{6,5},{7,6},{8,11},{9,8},{10,9... | collective-permute-start | bytes 331784 | tf_op jit(solution)/shard_map/ppermute | solution.py:448
  54.1 57.1 %all-to-all-start = ((bf16[4,576,512]{2,1,0:T(8,128)(2,1)}), bf16[4,576,512]{2,1,0:T(8,128)(2,1)S(1)}, u32[]{:S(2)}, u32[]{:S(2)}) async-start(bf16[4,576,512]{2,1,0:T(8,128)(2,1)} %spatial_attention.3), calls=%async_computation | async-start | bytes 4718592 | tf_op jit(solution)/shard_map/all_to_all | solution.py:484
  57.9 2.8 %copy-start.8 = (bf16[2,144,1152]{2,1,0:T(8,128)(2,1)S(1)}, bf16[2,144,1152]{2,1,0:T(8,128)(2,1)}, u32[]{:S(2)}) copy-start(bf16[2,144,1152]{2,1,0:T(8,128)(2,1)} %copy-done.7) | copy-start | bytes 1990660
  57.9 2.8 %copy-start.12 = (bf16[2,144,1152]{2,1,0:T(8,128)(2,1)S(1)}, bf16[2,144,1152]{2,1,0:T(8,128)(2,1)}, u32[]{:S(2)}) copy-start(bf16[2,144,1152]{2,1,0:T(8,128)(2,1)} %copy-done.11) | copy-start | bytes 1990660
  58.0 10.5 %collective-permute-start.14 = (bf16[4,48,1152]{2,1,0:T(8,128)(2,1)S(1)}, bf16[4,48,1152]{2,1,0:T(8,128)(2,1)S(1)}, u32[]{:S(2)}, u32[]{:S(2)}) collective-permute-start(bf16[4,48,1152]{2,1,0:T(8,128)(2,1)S(1)} %get-tuple-element.76), channel_id=1, source_target_pairs={{0,8},{8,0},{16,24},{24,16},{1,9},{9,1},{17,25},{25,17},{2,10},{10... | collective-permute-start | bytes 1327112 | tf_op jit(solution)/shard_map/ppermute | solution.py:454
  59.3 11.3 %collective-permute-start.15 = (bf16[4,48,1152]{2,1,0:T(8,128)(2,1)S(1)}, bf16[4,48,1152]{2,1,0:T(8,128)(2,1)S(1)}, u32[]{:S(2)}, u32[]{:S(2)}) collective-permute-start(bf16[4,48,1152]{2,1,0:T(8,128)(2,1)S(1)} %get-tuple-element.76), channel_id=1, source_target_pairs={{0,16},{8,24},{16,0},{24,8},{1,17},{9,25},{17,1},{25,9},{2,18},{10... | collective-permute-start | bytes 1327112 | tf_op jit(solution)/shard_map/ppermute | solution.py:454
  59.7 18.0 %collective-permute-start.16 = (bf16[4,48,1152]{2,1,0:T(8,128)(2,1)S(1)}, bf16[4,48,1152]{2,1,0:T(8,128)(2,1)S(1)}, u32[]{:S(2)}, u32[]{:S(2)}) collective-permute-start(bf16[4,48,1152]{2,1,0:T(8,128)(2,1)S(1)} %get-tuple-element.76), channel_id=1, source_target_pairs={{0,24},{8,16},{16,8},{24,0},{1,25},{9,17},{17,9},{25,1},{2,26},{10... | collective-permute-start | bytes 1327112 | tf_op jit(solution)/shard_map/ppermute | solution.py:454
  62.0 44.6 %collective-permute-start.9 = (bf16[2,2,144,1152]{3,2,1,0:T(8,128)(2,1)}, bf16[2,2,144,1152]{3,2,1,0:T(8,128)(2,1)}, u32[]{:S(2)}, u32[]{:S(2)}) collective-permute-start(bf16[2,2,144,1152]{3,2,1,0:T(8,128)(2,1)} %pad_maximum_fusion.2.refs_2_), channel_id=1, source_target_pairs={{0,8},{8,0},{16,24},{24,16},{1,9},{9,1},{17,25},{25,17},{2,10},{10... | collective-permute-start | bytes 3981320 | tf_op jit(solution)/shard_map/ppermute | solution.py:454
  65.5 43.2 %collective-permute-start.8 = (bf16[2,2,144,1152]{3,2,1,0:T(8,128)(2,1)}, bf16[2,2,144,1152]{3,2,1,0:T(8,128)(2,1)}, u32[]{:S(2)}, u32[]{:S(2)}) collective-permute-start(bf16[2,2,144,1152]{3,2,1,0:T(8,128)(2,1)} %pad_maximum_fusion.1.refs_0_), channel_id=1, source_target_pairs={{0,16},{8,24},{16,0},{24,8},{1,17},{9,25},{17,1},{25,9},{2,18},{10... | collective-permute-start | bytes 3981320 | tf_op jit(solution)/shard_map/ppermute | solution.py:454
  77.8 32.1 %copy-start.13 = (f32[2,4,1152]{2,1,0:T(4,128)S(1)}, f32[2,4,1152]{2,1,0:T(4,128)}, u32[]{:S(2)}) copy-start(f32[2,4,1152]{2,1,0:T(4,128)} %param.13) | copy-start | bytes 110596
  78.0 31.9 %collective-permute-start.17 = (bf16[4,4,48,1152]{3,2,1,0:T(8,128)(2,1)S(1)}, bf16[4,4,48,1152]{3,2,1,0:T(8,128)(2,1)S(1)}, u32[]{:S(2)}, u32[]{:S(2)}) collective-permute-start(bf16[4,4,48,1152]{3,2,1,0:T(8,128)(2,1)S(1)} %pad_maximum_fusion.plane_ref), channel_id=1, source_target_pairs={{0,4},{4,0},{1,5},{5,1},{2,6},{6,2},{3,7},{7,3},{8,12},{12,8},{9,1... | collective-permute-start | bytes 5308424 | tf_op jit(solution)/shard_map/ppermute | solution.py:454
  85.0 33.7 %collective-permute-start.12 = (bf16[2,2,144,1152]{3,2,1,0:T(8,128)(2,1)}, bf16[2,2,144,1152]{3,2,1,0:T(8,128)(2,1)}, u32[]{:S(2)}, u32[]{:S(2)}) collective-permute-start(bf16[2,2,144,1152]{3,2,1,0:T(8,128)(2,1)} %pad_maximum_fusion.2.refs_2_), channel_id=1, source_target_pairs={{0,4},{4,0},{1,5},{5,1},{2,6},{6,2},{3,7},{7,3},{8,12},{12,8},{9,1... | collective-permute-start | bytes 3981320 | tf_op jit(solution)/shard_map/ppermute | solution.py:454
  85.0 34.7 %collective-permute-start.10 = (bf16[2,2,144,1152]{3,2,1,0:T(8,128)(2,1)}, bf16[2,2,144,1152]{3,2,1,0:T(8,128)(2,1)}, u32[]{:S(2)}, u32[]{:S(2)}) collective-permute-start(bf16[2,2,144,1152]{3,2,1,0:T(8,128)(2,1)} %pad_maximum_fusion.1.refs_0_), channel_id=1, source_target_pairs={{0,4},{4,0},{1,5},{5,1},{2,6},{6,2},{3,7},{7,3},{8,12},{12,8},{9,1... | collective-permute-start | bytes 3981320 | tf_op jit(solution)/shard_map/ppermute | solution.py:454
  106.6 13.1 %collective-permute-start.13 = (bf16[2,2,144,1152]{3,2,1,0:T(8,128)(2,1)}, bf16[2,2,144,1152]{3,2,1,0:T(8,128)(2,1)}, u32[]{:S(2)}, u32[]{:S(2)}) collective-permute-start(bf16[2,2,144,1152]{3,2,1,0:T(8,128)(2,1)} %collective-permute-done.9.refs_3_), channel_id=1, source_target_pairs={{0,4},{4,0},{1,5},{5,1},{2,6},{6,2},{3,7},{7,3},{8,12},{12,8},{9,1... | collective-permute-start | bytes 3981320 | tf_op jit(solution)/shard_map/ppermute | solution.py:454
  108.7 10.9 %collective-permute-start.11 = (bf16[2,2,144,1152]{3,2,1,0:T(8,128)(2,1)}, bf16[2,2,144,1152]{3,2,1,0:T(8,128)(2,1)}, u32[]{:S(2)}, u32[]{:S(2)}) collective-permute-start(bf16[2,2,144,1152]{3,2,1,0:T(8,128)(2,1)} %collective-permute-done.8.refs_1_), channel_id=1, source_target_pairs={{0,4},{4,0},{1,5},{5,1},{2,6},{6,2},{3,7},{7,3},{8,12},{12,8},{9,1... | collective-permute-start | bytes 3981320 | tf_op jit(solution)/shard_map/ppermute | solution.py:454
  118.2 6.6 %collective-permute-start.18 = (bf16[1152,128]{1,0:T(8,128)(2,1)S(1)}, bf16[1152,128]{1,0:T(8,128)(2,1)S(1)}, u32[]{:S(2)}, u32[]{:S(2)}) collective-permute-start(bf16[1152,128]{1,0:T(8,128)(2,1)S(1)} %get-tuple-element.68), channel_id=1, source_target_pairs={{0,4},{4,8},{8,12},{12,0},{1,5},{5,9},{9,13},{13,1},{2,6},{6,10},{... | collective-permute-start | bytes 884744 | tf_op jit(solution)/shard_map/ppermute | solution.py:448
  118.7 13.4 %collective-permute-start.19 = (bf16[1152,128]{1,0:T(8,128)(2,1)S(1)}, bf16[1152,128]{1,0:T(8,128)(2,1)S(1)}, u32[]{:S(2)}, u32[]{:S(2)}) collective-permute-start(bf16[1152,128]{1,0:T(8,128)(2,1)S(1)} %get-tuple-element.69), channel_id=1, source_target_pairs={{0,8},{4,12},{8,0},{12,4},{1,9},{5,13},{9,1},{13,5},{2,10},{6,14},... | collective-permute-start | bytes 884744 | tf_op jit(solution)/shard_map/ppermute | solution.py:448
  119.6 13.6 %collective-permute-start.20 = (bf16[1152,128]{1,0:T(8,128)(2,1)S(1)}, bf16[1152,128]{1,0:T(8,128)(2,1)S(1)}, u32[]{:S(2)}, u32[]{:S(2)}) collective-permute-start(bf16[1152,128]{1,0:T(8,128)(2,1)S(1)} %get-tuple-element.70), channel_id=1, source_target_pairs={{0,12},{4,0},{8,4},{12,8},{1,13},{5,1},{9,5},{13,9},{2,14},{6,2},{... | collective-permute-start | bytes 884744 | tf_op jit(solution)/shard_map/ppermute | solution.py:448
  143.7 22.0 %collective-permute-start.21 = (bf16[288,512]{1,0:T(8,128)(2,1)S(1)}, bf16[288,512]{1,0:T(8,128)(2,1)S(1)}, u32[]{:S(2)}, u32[]{:S(2)}) collective-permute-start(bf16[288,512]{1,0:T(8,128)(2,1)S(1)} %get-tuple-element.71), channel_id=1, source_target_pairs={{0,0},{1,1},{2,18},{3,19},{16,2},{17,3},{18,16},{19,17},{4,4},{5,5... | collective-permute-start | bytes 884744 | tf_op jit(solution)/shard_map/ppermute | solution.py:497
  147.2 26.4 %collective-permute-start.22 = (bf16[288,512]{1,0:T(8,128)(2,1)S(1)}, bf16[288,512]{1,0:T(8,128)(2,1)S(1)}, u32[]{:S(2)}, u32[]{:S(2)}) collective-permute-start(bf16[288,512]{1,0:T(8,128)(2,1)S(1)} %get-tuple-element.72), channel_id=1, source_target_pairs={{0,1},{1,2},{2,19},{3,16},{16,3},{17,0},{18,17},{19,18},{4,5},{5,6... | collective-permute-start | bytes 884744 | tf_op jit(solution)/shard_map/ppermute | solution.py:497
  147.3 26.3 %collective-permute-start.23 = (bf16[288,512]{1,0:T(8,128)(2,1)S(1)}, bf16[288,512]{1,0:T(8,128)(2,1)S(1)}, u32[]{:S(2)}, u32[]{:S(2)}) collective-permute-start(bf16[288,512]{1,0:T(8,128)(2,1)S(1)} %get-tuple-element.73), channel_id=1, source_target_pairs={{0,2},{1,3},{2,16},{3,17},{16,0},{17,1},{18,18},{19,19},{4,6},{5,7... | collective-permute-start | bytes 884744 | tf_op jit(solution)/shard_map/ppermute | solution.py:497
  149.2 27.1 %collective-permute-start.24 = (bf16[288,512]{1,0:T(8,128)(2,1)S(1)}, bf16[288,512]{1,0:T(8,128)(2,1)S(1)}, u32[]{:S(2)}, u32[]{:S(2)}) collective-permute-start(bf16[288,512]{1,0:T(8,128)(2,1)S(1)} %get-tuple-element.74), channel_id=1, source_target_pairs={{0,3},{1,0},{2,17},{3,18},{16,1},{17,2},{18,19},{19,16},{4,7},{5,4... | collective-permute-start | bytes 884744 | tf_op jit(solution)/shard_map/ppermute | solution.py:497
  (8 other events, 12.0 us)

commit v5 on v4

--- a/solution.py
+++ b/solution.py
@@ -381,17 +381,21 @@
     share = block // run
     piece_refs, out_ref, held_ref = refs[:-2], refs[-2], refs[-1]
     clip, rank, me = info_ref[2], info_ref[3], info_ref[4]
-    for part in range(parts):
-        for step in range(heads):
-            if parts == 1:
-                source = lax.rem(me - step + heads + groups * heads - clip * share, heads)
-            else:
-                source = lax.rem(me - step + heads, heads) * parts + lax.rem(clip - part + parts, parts)
-            held_ref[source] = piece_refs[part * heads + step][...]
-    for group in range(groups):
-        for at in range(FRAMES):
-            pieces = [held_ref[group * share + e, :, at * run:(at + 1) * run] for e in range(share)]
-            out_ref[group * FRAMES + frame_at(at, rank, sizes)] = jnp.concatenate(pieces, axis=1) if share > 1 else pieces[0]
+    group = pl.program_id(0)
+
+    @pl.when(group == 0)
+    def hold():
+        for part in range(parts):
+            for step in range(heads):
+                if parts == 1:
+                    source = lax.rem(me - step + heads + groups * heads - clip * share, heads)
+                else:
+                    source = lax.rem(me - step + heads, heads) * parts + lax.rem(clip - part + parts, parts)
+                held_ref[source] = piece_refs[part * heads + step][...]
+
+    for at in range(FRAMES):
+        pieces = [held_ref[group * share + e, :, at * run:(at + 1) * run] for e in range(share)]
+        out_ref[frame_at(at, rank, sizes)] = jnp.concatenate(pieces, axis=1) if share > 1 else pieces[0]
 
 
 def place(info, pieces, sizes):
@@ -401,7 +405,8 @@
     return pl.pallas_call(
         functools.partial(place_kernel, sizes),
         in_specs=[pl.BlockSpec(memory_space=pltpu.SMEM)] + [vmem] * len(pieces),
-        out_specs=vmem,
+        out_specs=pl.BlockSpec((FRAMES, width, block), lambda g: (g, 0, 0)),
+        grid=(groups,),
         out_shape=jax.ShapeDtypeStruct((groups * FRAMES, width, block), BF16),
         scratch_shapes=[pltpu.VMEM((len(pieces), width, lanes), BF16)],
         compiler_params=pltpu.CompilerParams(vmem_limit_bytes=12 * MIB),

time: 179 us -> 179 us (level)
  waiting for transfers between devices: 80.3 us -> 70.8 us
  Pallas kernels: 43.2 us -> 52.6 us
    pallas_call x2, Pallas kernels: 20.4 us -> 29.9 us  [spatial_attention(): pl.pallas_call(functools.partial(spatial_kernel, ranks, first), grid_spec...]
    ppermute x9, waiting for transfers between devices: 21.8 us -> 12.4 us  [send(): lax.ppermute(array, axis, [(i, (i + step) % size) for i in range(size)])]
  transfers between devices with their start and end apart: 26 -> 26, of which waited for: 14 -> 13; matrix products, arithmetic and copies ran while one was open for 2% -> 2% of each run, Pallas kernels for 17% -> 23%
where the time goes in v5:
time: 179 us; the launch traced here: 178 us
  waiting for transfers between devices  70.8 us (40%)
  Pallas kernels  52.6 us (29%)
  starting transfers between devices  36 us (20%)
  local copies, waits for them, and re-layouts  13.5 us (8%)
  other arithmetic  5.22 us (3%)
    ppermute x12, waiting for transfers between devices, swap(): return lax.ppermute(array, axis, [(i, i ^ bit) for i in range(size)])  35.5 us
    pallas_call x2, Pallas kernels, spatial_attention(): pl.pallas_call(functools.partial(spatial_kernel, ranks, first), grid_spec...  29.9 us
    ppermute x4, waiting for transfers between devices, on_device(): lax.ppermute(result[part * heads + step], ('outer', 'clip', 'head'), rout...  22.8 us
    ppermute x12, starting transfers between devices, swap(): return lax.ppermute(array, axis, [(i, i ^ bit) for i in range(size)])  15.5 us
    ppermute x9, waiting for transfers between devices, send(): lax.ppermute(array, axis, [(i, (i + step) % size) for i in range(size)])  12.4 us
    pallas_call x1, Pallas kernels, temporal(): pl.pallas_call(functools.partial(temporal_kernel, sizes), grid_spec=pltpu...  10.5 us
    ppermute x4, starting transfers between devices, on_device(): lax.ppermute(result[part * heads + step], ('outer', 'clip', 'head'), rout...  9.8 us
    unnamed x28, local copies, waits for them, and re-layouts  9.57 us
  transfers between devices with their start and end apart: 26, of which 13 were waited for; matrix products, arithmetic and copies ran while one was open for 2% of the time, Pallas kernels for 23%

profile of v5, /device:TPU:13, one launch (start us, length us, event | category | flops | bytes accessed | tf_op | source)
XLA Modules:
  0.0 178.3 jit_solution(17641027363573409355)
XLA Ops:
  0.0 1.4 dynamic_slice.20
  3.8 1.3 stack.89.info_ref
  5.1 1.3 collective-permute-start
  7.4 1.4 collective-permute-start.2
  8.8 2.0 %copy-done.3 = bf16[3,2,1024,288]{2,3,1,0:T(8,128)(2,1)S(1)} copy-done((bf16[3,2,1024,288]{2,3,1,0:T(8,128)(2,1)S(1)}, bf16[3,2,1024,288]{2,3,1,0:T(8,128)(2,1)}, u32[]{:S(2)}) %copy-start.3) | copy-done | bytes 3538968
  12.1 1.3 arrange.1
  13.4 21.0 %spatial_attention.2.refs_0_ = bf16[3,288,512]{2,1,0:T(8,128)(2,1)S(1)} custom-call(s32[7]{0:T(128)S(1)} %stack.89.info_ref, bf16[4,2,2,144,256]{4,3,2,1,0:T(8,128)(2,1)S(1)} %get-tuple-element.42.query_ref, bf16[2,2,1024,144]{3,2,1,0:T(8,128)(2,1)S(1)} %get-tuple-element.43.key_ref, bf16[2,2,160,1024]{3,2,1,0:T(8,128)(2,1)S(1)} %get-tuple-element.44.value_ref), custom_call_target="tpu_custom_call" | custom-call | flops 14000000000 | bytes 5000000 | tf_op jit(solution)/shard_map/spatial_attention/pallas_call | solution.py:149
  34.5 2.5 %collective-permute-done.2 = bf16[144,1152]{1,0:T(8,128)(2,1)S(1)} collective-permute-done((bf16[144,1152]{1,0:T(8,128)(2,1)S(1)}, bf16[144,1152]{1,0:T(8,128)(2,1)S(1)}, u32[]{:S(2)}, u32[]{:S(2)}) %collective-permute-start.2) | collective-permute-done | bytes 331808 | tf_op jit(solution)/shard_map/ppermute | solution.py:453
  39.2 1.3 collective-permute-start.7
  40.5 8.9 %spatial_attention.3 = bf16[4,576,512]{2,1,0:T(8,128)(2,1)} custom-call(s32[7]{0:T(128)S(1)} %stack.89.info_ref, bf16[4,2,2,144,256]{4,3,2,1,0:T(8,128)(2,1)S(1)} %get-tuple-element.42.query_ref, bf16[2,2,1024,144]{3,2,1,0:T(8,128)(2,1)S(1)} %get-tuple-element.43.key_ref, bf16[2,2,160,1024]{3,2,1,0:T(8,128)(2,1)S(1)} %get-tuple-element.44.value_ref, ...), custom_call_target="tpu_custom_call" | custom-call | flops 14000000000 | bytes 5000000 | tf_op jit(solution)/shard_map/spatial_attention/pallas_call | solution.py:149
  50.7 2.6 %collective-permute-done.4 = bf16[2,144,1152]{2,1,0:T(8,128)(2,1)S(1)} collective-permute-done((bf16[2,144,1152]{2,1,0:T(8,128)(2,1)S(1)}, bf16[2,144,1152]{2,1,0:T(8,128)(2,1)S(1)}, u32[]{:S(2)}, u32[]{:S(2)}) %collective-permute-start.4) | collective-permute-done | bytes 663584 | tf_op jit(solution)/shard_map/ppermute | solution.py:459
  54.1 3.8 %all-to-all-start = ((bf16[4,576,512]{2,1,0:T(8,128)(2,1)}), bf16[4,576,512]{2,1,0:T(8,128)(2,1)S(1)}, u32[]{:S(2)}, u32[]{:S(2)}) async-start(bf16[4,576,512]{2,1,0:T(8,128)(2,1)} %spatial_attention.3), calls=%async_computation | async-start | bytes 4718592 | tf_op jit(solution)/shard_map/all_to_all | solution.py:489
  63.2 2.3 %pad_maximum_fusion.1.refs_0_ = bf16[2,2,144,1152]{3,2,1,0:T(8,128)(2,1)} fusion(bf16[1,2,144,1152]{3,2,1,0:T(8,128)(2,1)} %bitcast.15, bf16[1,2,144,1152]{3,2,1,0:T(8,128)(2,1)S(1)} %bitcast.34), kind=kLoop, calls=%fused_computation.1 | loop fusion | flops 663552 | bytes 2654208 | tf_op jit(solution)/shard_map/stack | solution.py:492
  65.9 2.6 %collective-permute-done.14 = bf16[4,48,1152]{2,1,0:T(8,128)(2,1)S(1)} collective-permute-done((bf16[4,48,1152]{2,1,0:T(8,128)(2,1)S(1)}, bf16[4,48,1152]{2,1,0:T(8,128)(2,1)S(1)}, u32[]{:S(2)}, u32[]{:S(2)}) %collective-permute-start.14) | collective-permute-done | bytes 442400 | tf_op jit(solution)/shard_map/ppermute | solution.py:459
  68.5 2.1 %collective-permute-done.15 = bf16[4,48,1152]{2,1,0:T(8,128)(2,1)S(1)} collective-permute-done((bf16[4,48,1152]{2,1,0:T(8,128)(2,1)S(1)}, bf16[4,48,1152]{2,1,0:T(8,128)(2,1)S(1)}, u32[]{:S(2)}, u32[]{:S(2)}) %collective-permute-start.15) | collective-permute-done | bytes 442400 | tf_op jit(solution)/shard_map/ppermute | solution.py:459
  70.6 7.1 %collective-permute-done.16 = bf16[4,48,1152]{2,1,0:T(8,128)(2,1)S(1)} collective-permute-done((bf16[4,48,1152]{2,1,0:T(8,128)(2,1)S(1)}, bf16[4,48,1152]{2,1,0:T(8,128)(2,1)S(1)}, u32[]{:S(2)}, u32[]{:S(2)}) %collective-permute-start.16) | collective-permute-done | bytes 442400 | tf_op jit(solution)/shard_map/ppermute | solution.py:459
  78.0 5.7 %collective-permute-start.17 = (bf16[4,4,48,1152]{3,2,1,0:T(8,128)(2,1)S(1)}, bf16[4,4,48,1152]{3,2,1,0:T(8,128)(2,1)S(1)}, u32[]{:S(2)}, u32[]{:S(2)}) collective-permute-start(bf16[4,4,48,1152]{3,2,1,0:T(8,128)(2,1)S(1)} %pad_maximum_fusion.plane_ref), channel_id=1, source_target_pairs={{0,4},{4,0},{1,5},{5,1},{2,6},{6,2},{3,7},{7,3},{8,12},{12,8},{9,1... | collective-permute-start | bytes 5308424 | tf_op jit(solution)/shard_map/ppermute | solution.py:459
  85.5 21.1 %collective-permute-done.9.refs_3_ = bf16[2,2,144,1152]{3,2,1,0:T(8,128)(2,1)} collective-permute-done((bf16[2,2,144,1152]{3,2,1,0:T(8,128)(2,1)}, bf16[2,2,144,1152]{3,2,1,0:T(8,128)(2,1)}, u32[]{:S(2)}, u32[]{:S(2)}) %collective-permute-start.9) | collective-permute-done | bytes 1327136 | tf_op jit(solution)/shard_map/ppermute | solution.py:459
  106.6 2.2 %collective-permute-start.13 = (bf16[2,2,144,1152]{3,2,1,0:T(8,128)(2,1)}, bf16[2,2,144,1152]{3,2,1,0:T(8,128)(2,1)}, u32[]{:S(2)}, u32[]{:S(2)}) collective-permute-start(bf16[2,2,144,1152]{3,2,1,0:T(8,128)(2,1)} %collective-permute-done.9.refs_3_), channel_id=1, source_target_pairs={{0,4},{4,0},{1,5},{5,1},{2,6},{6,2},{3,7},{7,3},{8,12},{12,8},{9,1... | collective-permute-start | bytes 3981320 | tf_op jit(solution)/shard_map/ppermute | solution.py:459
  111.2 1.5 copy-done.2
  112.7 1.5 copy-done.5
  114.1 4.1 %mix.1 = (bf16[1152,128]{1,0:T(8,128)(2,1)S(1)}, bf16[1152,128]{1,0:T(8,128)(2,1)S(1)}, bf16[1152,128]{1,0:T(8,128)(2,1)S(1)}, bf16[1152,128]{1,0:T(8,128)(2,1)S(1)}) custom-call(s32[7]{0:T(128)S(1)} %stack.89.info_ref, bf16[4,4,48,1152]{3,2,1,0:T(8,128)(2,1)S(1)} %copy-done.2, bf16[4,4,48,1152]{3,2,1,0:T(8,128)(2,1)S(1)} %copy-done.5, ...), custom_call_target="tpu_custom_call" | custom-call | flops 4000000000 | bytes 4000000 | tf_op jit(solution)/shard_map/mix/pallas_call | solution.py:198
  119.7 4.9 %pieces_in_place.1 = (bf16[8,432,1152]{2,1,0:T(8,128)(2,1)S(1)}, bf16[1152,1152]{1,0:T(8,128)(2,1)S(1)}) custom-call(s32[7]{0:T(128)S(1)} %stack.89.info_ref, bf16[2,2,144,1152]{3,2,1,0:T(8,128)(2,1)} %pad_maximum_fusion.1.refs_0_, bf16[2,2,144,1152]{3,2,1,0:T(8,128)(2,1)} %collective-permute-done.8.refs_1_, ...), custom_call_target="tpu_custom_call" | custom-call | flops 3000000000 | bytes 20000000 | tf_op jit(solution)/shard_map/pieces_in_place/pallas_call | solution.py:241
  124.8 7.4 %collective-permute-done.19.refs_2_ = bf16[1152,128]{1,0:T(8,128)(2,1)S(1)} collective-permute-done((bf16[1152,128]{1,0:T(8,128)(2,1)S(1)}, bf16[1152,128]{1,0:T(8,128)(2,1)S(1)}, u32[]{:S(2)}, u32[]{:S(2)}) %collective-permute-start.19) | collective-permute-done | bytes 294944 | tf_op jit(solution)/shard_map/ppermute | solution.py:453
  133.2 10.5 %temporal.1 = (bf16[288,512]{1,0:T(8,128)(2,1)S(1)}, bf16[288,512]{1,0:T(8,128)(2,1)S(1)}, bf16[288,512]{1,0:T(8,128)(2,1)S(1)}, bf16[288,512]{1,0:T(8,128)(2,1)S(1)}) custom-call(s32[7]{0:T(128)S(1)} %stack.89.info_ref, f32[8,1152]{1,0:T(8,128)S(1)} %pad_maximum_fusion.6.gates_ref, bf16[8,432,1152]{2,1,0:T(8,128)(2,1)S(1)} %get-tuple-element.60.qkv_ref, ...), custom_call_target="tpu_custom_call" | custom-call | flops 17999998976 | bytes 12000000 | tf_op jit(solution)/shard_map/temporal/pallas_call | solution.py:362
  143.7 3.5 %collective-permute-start.21 = (bf16[288,512]{1,0:T(8,128)(2,1)S(1)}, bf16[288,512]{1,0:T(8,128)(2,1)S(1)}, u32[]{:S(2)}, u32[]{:S(2)}) collective-permute-start(bf16[288,512]{1,0:T(8,128)(2,1)S(1)} %get-tuple-element.71), channel_id=1, source_target_pairs={{0,0},{1,1},{2,18},{3,19},{16,2},{17,3},{18,16},{19,17},{4,4},{5,5... | collective-permute-start | bytes 884744 | tf_op jit(solution)/shard_map/ppermute | solution.py:502
  147.3 1.9 %collective-permute-start.23 = (bf16[288,512]{1,0:T(8,128)(2,1)S(1)}, bf16[288,512]{1,0:T(8,128)(2,1)S(1)}, u32[]{:S(2)}, u32[]{:S(2)}) collective-permute-start(bf16[288,512]{1,0:T(8,128)(2,1)S(1)} %get-tuple-element.73), channel_id=1, source_target_pairs={{0,2},{1,3},{2,16},{3,17},{16,0},{17,1},{18,18},{19,19},{4,6},{5,7... | collective-permute-start | bytes 884744 | tf_op jit(solution)/shard_map/ppermute | solution.py:502
  149.2 4.3 %collective-permute-start.24 = (bf16[288,512]{1,0:T(8,128)(2,1)S(1)}, bf16[288,512]{1,0:T(8,128)(2,1)S(1)}, u32[]{:S(2)}, u32[]{:S(2)}) collective-permute-start(bf16[288,512]{1,0:T(8,128)(2,1)S(1)} %get-tuple-element.74), channel_id=1, source_target_pairs={{0,3},{1,0},{2,17},{3,18},{16,1},{17,2},{18,19},{19,16},{4,7},{5,4... | collective-permute-start | bytes 884744 | tf_op jit(solution)/shard_map/ppermute | solution.py:502
  153.5 12.2 %collective-permute-done.21.refs_0_ = bf16[288,512]{1,0:T(8,128)(2,1)S(1)} collective-permute-done((bf16[288,512]{1,0:T(8,128)(2,1)S(1)}, bf16[288,512]{1,0:T(8,128)(2,1)S(1)}, u32[]{:S(2)}, u32[]{:S(2)}) %collective-permute-start.21) | collective-permute-done | bytes 294944 | tf_op jit(solution)/shard_map/ppermute | solution.py:502
  165.7 7.8 %collective-permute-done.22.refs_1_ = bf16[288,512]{1,0:T(8,128)(2,1)S(1)} collective-permute-done((bf16[288,512]{1,0:T(8,128)(2,1)S(1)}, bf16[288,512]{1,0:T(8,128)(2,1)S(1)}, u32[]{:S(2)}, u32[]{:S(2)}) %collective-permute-start.22) | collective-permute-done | bytes 294944 | tf_op jit(solution)/shard_map/ppermute | solution.py:502
  173.6 2.8 %collective-permute-done.24.refs_3_ = bf16[288,512]{1,0:T(8,128)(2,1)S(1)} collective-permute-done((bf16[288,512]{1,0:T(8,128)(2,1)S(1)}, bf16[288,512]{1,0:T(8,128)(2,1)S(1)}, u32[]{:S(2)}, u32[]{:S(2)}) %collective-permute-start.24) | collective-permute-done | bytes 294944 | tf_op jit(solution)/shard_map/ppermute | solution.py:502
  176.3 1.9 %place.1 = bf16[16,288,128]{2,1,0:T(8,128)(2,1)} custom-call(s32[7]{0:T(128)S(1)} %stack.89.info_ref, bf16[288,512]{1,0:T(8,128)(2,1)S(1)} %collective-permute-done.21.refs_0_, bf16[288,512]{1,0:T(8,128)(2,1)S(1)} %collective-permute-done.22.refs_1_, bf16[288,512]{1,0:T(8,128)(2,1)S(1)} %collective-permute-done.23.refs_2_, ...), custom_call_target="tpu_custom_call" | custom-call | tf_op jit(solution)/shard_map/place/pallas_call | solution.py:405
  (68 shorter events, 21.9 us)
Async XLA Ops:
  0.0 2.6 %copy-start = (bf16[288,1152]{1,0:T(8,128)(2,1)S(1)}, bf16[288,1152]{1,0:T(8,128)(2,1)}, u32[]{:S(2)}) copy-start(bf16[288,1152]{1,0:T(8,128)(2,1)} %param.10) | copy-start | bytes 1990660
  5.1 29.4 %collective-permute-start = (bf16[144,1152]{1,0:T(8,128)(2,1)S(1)}, bf16[144,1152]{1,0:T(8,128)(2,1)S(1)}, u32[]{:S(2)}, u32[]{:S(2)}) collective-permute-start(bf16[144,1152]{1,0:T(8,128)(2,1)S(1)} %bitcast_select_fusion), channel_id=1, source_target_pairs={{0,1},{1,2},{2,3},{3,0},{4,5},{5,6},{6,7},{7,4},{8,9},{9,10},{10,1... | collective-permute-start | bytes 995336 | tf_op jit(solution)/shard_map/ppermute | solution.py:453
  6.4 28.1 %collective-permute-start.1 = (bf16[144,1152]{1,0:T(8,128)(2,1)S(1)}, bf16[144,1152]{1,0:T(8,128)(2,1)S(1)}, u32[]{:S(2)}, u32[]{:S(2)}) collective-permute-start(bf16[144,1152]{1,0:T(8,128)(2,1)S(1)} %bitcast_select_fusion), channel_id=1, source_target_pairs={{0,2},{1,3},{2,0},{3,1},{4,6},{5,7},{6,4},{7,5},{8,10},{9,11},{10,... | collective-permute-start | bytes 995336 | tf_op jit(solution)/shard_map/ppermute | solution.py:453
  7.4 29.6 %collective-permute-start.2 = (bf16[144,1152]{1,0:T(8,128)(2,1)S(1)}, bf16[144,1152]{1,0:T(8,128)(2,1)S(1)}, u32[]{:S(2)}, u32[]{:S(2)}) collective-permute-start(bf16[144,1152]{1,0:T(8,128)(2,1)S(1)} %bitcast_select_fusion), channel_id=1, source_target_pairs={{0,3},{1,0},{2,1},{3,2},{4,7},{5,4},{6,5},{7,6},{8,11},{9,8},{10,9... | collective-permute-start | bytes 995336 | tf_op jit(solution)/shard_map/ppermute | solution.py:453
  37.1 12.3 %copy-start.7 = (bf16[2,144,1152]{2,1,0:T(8,128)(2,1)}, bf16[2,144,1152]{2,1,0:T(8,128)(2,1)S(1)}, u32[]{:S(2)}) copy-start(bf16[2,144,1152]{2,1,0:T(8,128)(2,1)S(1)} %pad_maximum_fusion.4) | copy-start | bytes 1990660
  37.1 16.2 %collective-permute-start.4 = (bf16[2,144,1152]{2,1,0:T(8,128)(2,1)S(1)}, bf16[2,144,1152]{2,1,0:T(8,128)(2,1)S(1)}, u32[]{:S(2)}, u32[]{:S(2)}) collective-permute-start(bf16[2,144,1152]{2,1,0:T(8,128)(2,1)S(1)} %pad_maximum_fusion.4), channel_id=1, source_target_pairs={{0,16},{8,24},{16,0},{24,8},{1,17},{9,25},{17,1},{25,9},{2,18},{10... | collective-permute-start | bytes 1990664 | tf_op jit(solution)/shard_map/ppermute | solution.py:459
  37.4 11.9 %copy-start.9 = (bf16[2,144,1152]{2,1,0:T(8,128)(2,1)}, bf16[2,144,1152]{2,1,0:T(8,128)(2,1)S(1)}, u32[]{:S(2)}) copy-start(bf16[2,144,1152]{2,1,0:T(8,128)(2,1)S(1)} %pad_maximum_fusion.3) | copy-start | bytes 1990660
  37.5 16.6 %collective-permute-start.3 = (bf16[2,144,1152]{2,1,0:T(8,128)(2,1)S(1)}, bf16[2,144,1152]{2,1,0:T(8,128)(2,1)}, u32[]{:S(2)}, u32[]{:S(2)}) collective-permute-start(bf16[2,144,1152]{2,1,0:T(8,128)(2,1)S(1)} %pad_maximum_fusion.3), channel_id=1, source_target_pairs={{0,8},{8,0},{16,24},{24,16},{1,9},{9,1},{17,25},{25,17},{2,10},{10... | collective-permute-start | bytes 1990664 | tf_op jit(solution)/shard_map/ppermute | solution.py:459
  38.7 10.6 %collective-permute-start.5 = (bf16[48,1152]{1,0:T(8,128)(2,1)S(1)}, bf16[48,1152]{1,0:T(8,128)(2,1)S(1)}, u32[]{:S(2)}, u32[]{:S(2)}) collective-permute-start(bf16[48,1152]{1,0:T(8,128)(2,1)S(1)} %constant_dynamic-slice_fusion), channel_id=1, source_target_pairs={{0,1},{1,2},{2,3},{3,0},{4,5},{5,6},{6,7},{7,4},{8,9},{9,10},{10,1... | collective-permute-start | bytes 331784 | tf_op jit(solution)/shard_map/ppermute | solution.py:453
  38.7 10.6 %collective-permute-start.6 = (bf16[48,1152]{1,0:T(8,128)(2,1)S(1)}, bf16[48,1152]{1,0:T(8,128)(2,1)S(1)}, u32[]{:S(2)}, u32[]{:S(2)}) collective-permute-start(bf16[48,1152]{1,0:T(8,128)(2,1)S(1)} %constant_dynamic-slice_fusion), channel_id=1, source_target_pairs={{0,2},{1,3},{2,0},{3,1},{4,6},{5,7},{6,4},{7,5},{8,10},{9,11},{10,... | collective-permute-start | bytes 331784 | tf_op jit(solution)/shard_map/ppermute | solution.py:453
  39.2 11.5 %collective-permute-start.7 = (bf16[48,1152]{1,0:T(8,128)(2,1)S(1)}, bf16[48,1152]{1,0:T(8,128)(2,1)S(1)}, u32[]{:S(2)}, u32[]{:S(2)}) collective-permute-start(bf16[48,1152]{1,0:T(8,128)(2,1)S(1)} %constant_dynamic-slice_fusion), channel_id=1, source_target_pairs={{0,3},{1,0},{2,1},{3,2},{4,7},{5,4},{6,5},{7,6},{8,11},{9,8},{10,9... | collective-permute-start | bytes 331784 | tf_op jit(solution)/shard_map/ppermute | solution.py:453
  54.1 57.1 %all-to-all-start = ((bf16[4,576,512]{2,1,0:T(8,128)(2,1)}), bf16[4,576,512]{2,1,0:T(8,128)(2,1)S(1)}, u32[]{:S(2)}, u32[]{:S(2)}) async-start(bf16[4,576,512]{2,1,0:T(8,128)(2,1)} %spatial_attention.3), calls=%async_computation | async-start | bytes 4718592 | tf_op jit(solution)/shard_map/all_to_all | solution.py:489
  57.9 2.8 %copy-start.8 = (bf16[2,144,1152]{2,1,0:T(8,128)(2,1)S(1)}, bf16[2,144,1152]{2,1,0:T(8,128)(2,1)}, u32[]{:S(2)}) copy-start(bf16[2,144,1152]{2,1,0:T(8,128)(2,1)} %copy-done.7) | copy-start | bytes 1990660
  57.9 2.8 %copy-start.12 = (bf16[2,144,1152]{2,1,0:T(8,128)(2,1)S(1)}, bf16[2,144,1152]{2,1,0:T(8,128)(2,1)}, u32[]{:S(2)}) copy-start(bf16[2,144,1152]{2,1,0:T(8,128)(2,1)} %copy-done.11) | copy-start | bytes 1990660
  58.0 10.5 %collective-permute-start.14 = (bf16[4,48,1152]{2,1,0:T(8,128)(2,1)S(1)}, bf16[4,48,1152]{2,1,0:T(8,128)(2,1)S(1)}, u32[]{:S(2)}, u32[]{:S(2)}) collective-permute-start(bf16[4,48,1152]{2,1,0:T(8,128)(2,1)S(1)} %get-tuple-element.76), channel_id=1, source_target_pairs={{0,8},{8,0},{16,24},{24,16},{1,9},{9,1},{17,25},{25,17},{2,10},{10... | collective-permute-start | bytes 1327112 | tf_op jit(solution)/shard_map/ppermute | solution.py:459
  59.3 11.3 %collective-permute-start.15 = (bf16[4,48,1152]{2,1,0:T(8,128)(2,1)S(1)}, bf16[4,48,1152]{2,1,0:T(8,128)(2,1)S(1)}, u32[]{:S(2)}, u32[]{:S(2)}) collective-permute-start(bf16[4,48,1152]{2,1,0:T(8,128)(2,1)S(1)} %get-tuple-element.76), channel_id=1, source_target_pairs={{0,16},{8,24},{16,0},{24,8},{1,17},{9,25},{17,1},{25,9},{2,18},{10... | collective-permute-start | bytes 1327112 | tf_op jit(solution)/shard_map/ppermute | solution.py:459
  59.7 18.0 %collective-permute-start.16 = (bf16[4,48,1152]{2,1,0:T(8,128)(2,1)S(1)}, bf16[4,48,1152]{2,1,0:T(8,128)(2,1)S(1)}, u32[]{:S(2)}, u32[]{:S(2)}) collective-permute-start(bf16[4,48,1152]{2,1,0:T(8,128)(2,1)S(1)} %get-tuple-element.76), channel_id=1, source_target_pairs={{0,24},{8,16},{16,8},{24,0},{1,25},{9,17},{17,9},{25,1},{2,26},{10... | collective-permute-start | bytes 1327112 | tf_op jit(solution)/shard_map/ppermute | solution.py:459
  62.0 44.6 %collective-permute-start.9 = (bf16[2,2,144,1152]{3,2,1,0:T(8,128)(2,1)}, bf16[2,2,144,1152]{3,2,1,0:T(8,128)(2,1)}, u32[]{:S(2)}, u32[]{:S(2)}) collective-permute-start(bf16[2,2,144,1152]{3,2,1,0:T(8,128)(2,1)} %pad_maximum_fusion.2.refs_2_), channel_id=1, source_target_pairs={{0,8},{8,0},{16,24},{24,16},{1,9},{9,1},{17,25},{25,17},{2,10},{10... | collective-permute-start | bytes 3981320 | tf_op jit(solution)/shard_map/ppermute | solution.py:459
  65.5 43.2 %collective-permute-start.8 = (bf16[2,2,144,1152]{3,2,1,0:T(8,128)(2,1)}, bf16[2,2,144,1152]{3,2,1,0:T(8,128)(2,1)}, u32[]{:S(2)}, u32[]{:S(2)}) collective-permute-start(bf16[2,2,144,1152]{3,2,1,0:T(8,128)(2,1)} %pad_maximum_fusion.1.refs_0_), channel_id=1, source_target_pairs={{0,16},{8,24},{16,0},{24,8},{1,17},{9,25},{17,1},{25,9},{2,18},{10... | collective-permute-start | bytes 3981320 | tf_op jit(solution)/shard_map/ppermute | solution.py:459
  77.8 32.1 %copy-start.13 = (f32[2,4,1152]{2,1,0:T(4,128)S(1)}, f32[2,4,1152]{2,1,0:T(4,128)}, u32[]{:S(2)}) copy-start(f32[2,4,1152]{2,1,0:T(4,128)} %param.13) | copy-start | bytes 110596
  78.0 31.9 %collective-permute-start.17 = (bf16[4,4,48,1152]{3,2,1,0:T(8,128)(2,1)S(1)}, bf16[4,4,48,1152]{3,2,1,0:T(8,128)(2,1)S(1)}, u32[]{:S(2)}, u32[]{:S(2)}) collective-permute-start(bf16[4,4,48,1152]{3,2,1,0:T(8,128)(2,1)S(1)} %pad_maximum_fusion.plane_ref), channel_id=1, source_target_pairs={{0,4},{4,0},{1,5},{5,1},{2,6},{6,2},{3,7},{7,3},{8,12},{12,8},{9,1... | collective-permute-start | bytes 5308424 | tf_op jit(solution)/shard_map/ppermute | solution.py:459
  85.0 33.7 %collective-permute-start.12 = (bf16[2,2,144,1152]{3,2,1,0:T(8,128)(2,1)}, bf16[2,2,144,1152]{3,2,1,0:T(8,128)(2,1)}, u32[]{:S(2)}, u32[]{:S(2)}) collective-permute-start(bf16[2,2,144,1152]{3,2,1,0:T(8,128)(2,1)} %pad_maximum_fusion.2.refs_2_), channel_id=1, source_target_pairs={{0,4},{4,0},{1,5},{5,1},{2,6},{6,2},{3,7},{7,3},{8,12},{12,8},{9,1... | collective-permute-start | bytes 3981320 | tf_op jit(solution)/shard_map/ppermute | solution.py:459
  85.0 34.7 %collective-permute-start.10 = (bf16[2,2,144,1152]{3,2,1,0:T(8,128)(2,1)}, bf16[2,2,144,1152]{3,2,1,0:T(8,128)(2,1)}, u32[]{:S(2)}, u32[]{:S(2)}) collective-permute-start(bf16[2,2,144,1152]{3,2,1,0:T(8,128)(2,1)} %pad_maximum_fusion.1.refs_0_), channel_id=1, source_target_pairs={{0,4},{4,0},{1,5},{5,1},{2,6},{6,2},{3,7},{7,3},{8,12},{12,8},{9,1... | collective-permute-start | bytes 3981320 | tf_op jit(solution)/shard_map/ppermute | solution.py:459
  106.6 13.1 %collective-permute-start.13 = (bf16[2,2,144,1152]{3,2,1,0:T(8,128)(2,1)}, bf16[2,2,144,1152]{3,2,1,0:T(8,128)(2,1)}, u32[]{:S(2)}, u32[]{:S(2)}) collective-permute-start(bf16[2,2,144,1152]{3,2,1,0:T(8,128)(2,1)} %collective-permute-done.9.refs_3_), channel_id=1, source_target_pairs={{0,4},{4,0},{1,5},{5,1},{2,6},{6,2},{3,7},{7,3},{8,12},{12,8},{9,1... | collective-permute-start | bytes 3981320 | tf_op jit(solution)/shard_map/ppermute | solution.py:459
  108.7 10.9 %collective-permute-start.11 = (bf16[2,2,144,1152]{3,2,1,0:T(8,128)(2,1)}, bf16[2,2,144,1152]{3,2,1,0:T(8,128)(2,1)}, u32[]{:S(2)}, u32[]{:S(2)}) collective-permute-start(bf16[2,2,144,1152]{3,2,1,0:T(8,128)(2,1)} %collective-permute-done.8.refs_1_), channel_id=1, source_target_pairs={{0,4},{4,0},{1,5},{5,1},{2,6},{6,2},{3,7},{7,3},{8,12},{12,8},{9,1... | collective-permute-start | bytes 3981320 | tf_op jit(solution)/shard_map/ppermute | solution.py:459
  118.2 6.6 %collective-permute-start.18 = (bf16[1152,128]{1,0:T(8,128)(2,1)S(1)}, bf16[1152,128]{1,0:T(8,128)(2,1)S(1)}, u32[]{:S(2)}, u32[]{:S(2)}) collective-permute-start(bf16[1152,128]{1,0:T(8,128)(2,1)S(1)} %get-tuple-element.68), channel_id=1, source_target_pairs={{0,4},{4,8},{8,12},{12,0},{1,5},{5,9},{9,13},{13,1},{2,6},{6,10},{... | collective-permute-start | bytes 884744 | tf_op jit(solution)/shard_map/ppermute | solution.py:453
  118.7 13.4 %collective-permute-start.19 = (bf16[1152,128]{1,0:T(8,128)(2,1)S(1)}, bf16[1152,128]{1,0:T(8,128)(2,1)S(1)}, u32[]{:S(2)}, u32[]{:S(2)}) collective-permute-start(bf16[1152,128]{1,0:T(8,128)(2,1)S(1)} %get-tuple-element.69), channel_id=1, source_target_pairs={{0,8},{4,12},{8,0},{12,4},{1,9},{5,13},{9,1},{13,5},{2,10},{6,14},... | collective-permute-start | bytes 884744 | tf_op jit(solution)/shard_map/ppermute | solution.py:453
  119.6 13.6 %collective-permute-start.20 = (bf16[1152,128]{1,0:T(8,128)(2,1)S(1)}, bf16[1152,128]{1,0:T(8,128)(2,1)S(1)}, u32[]{:S(2)}, u32[]{:S(2)}) collective-permute-start(bf16[1152,128]{1,0:T(8,128)(2,1)S(1)} %get-tuple-element.70), channel_id=1, source_target_pairs={{0,12},{4,0},{8,4},{12,8},{1,13},{5,1},{9,5},{13,9},{2,14},{6,2},{... | collective-permute-start | bytes 884744 | tf_op jit(solution)/shard_map/ppermute | solution.py:453
  143.7 22.0 %collective-permute-start.21 = (bf16[288,512]{1,0:T(8,128)(2,1)S(1)}, bf16[288,512]{1,0:T(8,128)(2,1)S(1)}, u32[]{:S(2)}, u32[]{:S(2)}) collective-permute-start(bf16[288,512]{1,0:T(8,128)(2,1)S(1)} %get-tuple-element.71), channel_id=1, source_target_pairs={{0,0},{1,1},{2,18},{3,19},{16,2},{17,3},{18,16},{19,17},{4,4},{5,5... | collective-permute-start | bytes 884744 | tf_op jit(solution)/shard_map/ppermute | solution.py:502
  147.2 26.4 %collective-permute-start.22 = (bf16[288,512]{1,0:T(8,128)(2,1)S(1)}, bf16[288,512]{1,0:T(8,128)(2,1)S(1)}, u32[]{:S(2)}, u32[]{:S(2)}) collective-permute-start(bf16[288,512]{1,0:T(8,128)(2,1)S(1)} %get-tuple-element.72), channel_id=1, source_target_pairs={{0,1},{1,2},{2,19},{3,16},{16,3},{17,0},{18,17},{19,18},{4,5},{5,6... | collective-permute-start | bytes 884744 | tf_op jit(solution)/shard_map/ppermute | solution.py:502
  147.3 26.3 %collective-permute-start.23 = (bf16[288,512]{1,0:T(8,128)(2,1)S(1)}, bf16[288,512]{1,0:T(8,128)(2,1)S(1)}, u32[]{:S(2)}, u32[]{:S(2)}) collective-permute-start(bf16[288,512]{1,0:T(8,128)(2,1)S(1)} %get-tuple-element.73), channel_id=1, source_target_pairs={{0,2},{1,3},{2,16},{3,17},{16,0},{17,1},{18,18},{19,19},{4,6},{5,7... | collective-permute-start | bytes 884744 | tf_op jit(solution)/shard_map/ppermute | solution.py:502
  149.2 27.1 %collective-permute-start.24 = (bf16[288,512]{1,0:T(8,128)(2,1)S(1)}, bf16[288,512]{1,0:T(8,128)(2,1)S(1)}, u32[]{:S(2)}, u32[]{:S(2)}) collective-permute-start(bf16[288,512]{1,0:T(8,128)(2,1)S(1)} %get-tuple-element.74), channel_id=1, source_target_pairs={{0,3},{1,0},{2,17},{3,18},{16,1},{17,2},{18,19},{19,16},{4,7},{5,4... | collective-permute-start | bytes 884744 | tf_op jit(solution)/shard_map/ppermute | solution.py:502
  (8 other events, 12.0 us)
